TPU v7x, 32 devices: a whole 2x2x4 slice. The times are simulated.
32 devices in a mesh: section: 2 (over core), replica: 4 (over y, x), shard: 4 (over z).
Axes of the slice: x: 2, y: 2, z: 4, core: 2. Of those that a mesh axis runs over, the one named last changes fastest.
Arguments:
- boundary: bfloat16 [2, 2, 4, 1024, 1600], P('section', None, 'replica', 'shard'), may hold values from -6 to 6
- segments: int32 [2, 4, 1024], P(None, 'replica'), may hold values from 0 to 2, never falling along the last dimension, each value on 1 to 768 neighbouring positions
- attn_weight: bfloat16 [2, 1600, 4800], P('section', 'shard'), may hold values from -0.15625 to 0.15625
- proj_weight: bfloat16 [2, 1600, 1600], P('section', 'shard'), may hold values from -0.625 to 0.625
- fc_in_weight: bfloat16 [2, 1600, 6400], P('section', 'shard'), may hold values from -0.15625 to 0.15625
- fc_out_weight: bfloat16 [2, 6400, 1600], P('section', 'shard'), may hold values from -0.078125 to 0.078125
- norm_gains: float32 [2, 2, 1600], P('section'), may hold values from 0.5 to 1.5
- vector_bias: float32 [2, 6, 1600], P('section'), may hold values from -3 to 3
- fc_in_bias: float32 [2, 6400], P('section'), may hold values from -3 to 3
Outputs:
- edge: float32 [2, 2, 4, 1024, 1600], P('section', None, 'replica', 'shard')
- attn_weight_grad: float32 [2, 1600, 4800], P('section', 'shard')
- proj_weight_grad: float32 [2, 1600, 1600], P('section', 'shard')
- fc_in_weight_grad: float32 [2, 1600, 6400], P('section', 'shard')
- fc_out_weight_grad: float32 [2, 6400, 1600], P('section', 'shard')
- norm_gains_grad: float32 [2, 2, 1600], P('section')
- vector_bias_grad: float32 [2, 6, 1600], P('section')
- fc_in_bias_grad: float32 [2, 6400], P('section')
Inputs may be any that keep to these rules, and one draw needn't show every extreme that they name: `segments`: each sequence holds three documents numbered 0, 1, 2 in order, none empty; the longest has exactly 768 tokens.
All inputs are finite; a program needn't handle non-finite values.
Results may differ from a plain program's by a relative error of at most 0.025.
Values may be sent and summed in bfloat16 or wider, within the bound.
No kernel may reach another device: no remote copies, remote signals or barrier semaphores. Data moves between devices by JAX's collectives and lax.ppermute only.
A program may use at most 448 MiB of HBM per device.

v0:
```python
from functools import partial

import jax
import jax.numpy as jnp
from jax import lax
from jax.sharding import PartitionSpec as P

HEADS = 25
HEAD = 64


EPSILON = 1e-05
MASKED = -1e30


def as_sent(value):

    def short(part):
        return part.astype(jnp.bfloat16) if part.dtype == jnp.float32 else part

    return jax.tree.map(short, value)


def shifted(value, axis, by):
    size = lax.axis_size(axis)
    pairs = [(i, i + by) for i in range(size) if 0 <= i + by < size]
    return lax.ppermute(value, axis, pairs)


def layer_norm(value, gain, shift):
    centred = value - jnp.mean(value, axis=-1, keepdims=True)
    variance = jnp.mean(centred * centred, axis=-1, keepdims=True)
    return centred * lax.rsqrt(variance + EPSILON) * gain + shift


def times_plain(left, right):
    return jnp.dot(left, right, preferred_element_type=jnp.float32)


def times_first(left, right):
    return lax.dot_general(
        left, right, (((0,), (0,)), ((), ())), preferred_element_type=jnp.float32
    )


def times_last(left, right):
    return lax.dot_general(
        left, right, (((1,), (1,)), ((), ())), preferred_element_type=jnp.float32
    )


def allowed(row_ids, col_ids, row_first, col_first):
    shape = (row_ids.shape[1], col_ids.shape[1])
    row_places = row_first + lax.broadcasted_iota(jnp.int32, shape, 0)
    col_places = col_first + lax.broadcasted_iota(jnp.int32, shape, 1)
    same = row_ids[:, :, None] == col_ids[:, None, :]
    return (same & (col_places <= row_places)[None])[:, None]


def probabilities(query, keys, logsum, mask, scale):
    scores = jnp.einsum("sqhe,skhe->shqk", query, keys, preferred_element_type=jnp.float32) * scale
    return jnp.where(mask, jnp.exp(scores - logsum[..., None]), 0.0)


def score_grads(probs, grad_rows, values, delta):
    inner = jnp.einsum("sqhe,skhe->shqk", grad_rows, values, preferred_element_type=jnp.float32)
    return (probs * (inner - delta[..., None])).astype(jnp.bfloat16)


def body(
    boundary,
    segments,
    attn_weight,
    proj_weight,
    fc_in_weight,
    fc_out_weight,
    norm_gains,
    vector_bias,
    fc_in_bias,
):
    section = lax.axis_index("section")
    first = section == 0
    micro = boundary.shape[1]
    seqs = boundary.shape[2]
    local = boundary.shape[3]
    width = boundary.shape[4]
    rows = seqs * local
    row_start = lax.axis_index("shard") * local
    scale = HEAD ** (-0.5)
    gains = norm_gains[0]
    biases = vector_bias[0]
    hid_bias = fc_in_bias[0]
    own = boundary[0].astype(jnp.float32).reshape(micro, rows, width)
    heads_shape = (seqs, local, HEADS, HEAD)
    zeros_heads = jnp.zeros(heads_shape, jnp.float32)
    gelu_tanh = partial(jax.nn.gelu, approximate=True)
    gathered = (
        lax.all_gather(attn_weight, "shard", axis=1, tiled=True),
        lax.all_gather(proj_weight, "shard", axis=1, tiled=True),
        lax.all_gather(fc_in_weight, "shard", axis=1, tiled=True),
        lax.all_gather(fc_out_weight, "shard", axis=1, tiled=True),
    )
    weights_fwd = tuple((weight[0] for weight in gathered))

    def attend_back(query, keys, values, attended, logsum, grad_attended, segment_ids):
        row_ids = lax.dynamic_slice_in_dim(segment_ids, row_start, local, 1)
        query_heads = query.reshape(heads_shape)
        key_heads = keys.reshape(heads_shape)
        value_heads = values.reshape(heads_shape)
        grad_heads = grad_attended.reshape(heads_shape)
        delta = jnp.sum(
            grad_heads.astype(jnp.float32) * attended.reshape(heads_shape), axis=-1
        ).transpose(0, 2, 1)
        start = jnp.int32(0)
        key_piece = lax.all_gather(as_sent(key_heads), "shard", axis=1, tiled=True)
        value_piece = lax.all_gather(as_sent(value_heads), "shard", axis=1, tiled=True)
        count = key_piece.shape[1]
        mask = allowed(
            row_ids, lax.dynamic_slice_in_dim(segment_ids, start, count, 1), row_start, start
        )
        probs = probabilities(query_heads, key_piece, logsum, mask, scale)
        dscore = score_grads(probs, grad_heads, value_piece, delta)
        folded = (
            zeros_heads
            + jnp.einsum("shqk,skhe->sqhe", dscore, key_piece, preferred_element_type=jnp.float32)
            * scale
        )
        logsum_all, delta_all = (
            lax.all_gather(logsum, "shard", axis=2, tiled=True),
            lax.all_gather(delta, "shard", axis=2, tiled=True),
        )
        start = jnp.int32(0)
        grad_keys = zeros_heads
        grad_values = zeros_heads
        query_piece = lax.all_gather(as_sent(query_heads), "shard", axis=1, tiled=True)
        grad_piece = lax.all_gather(grad_heads, "shard", axis=1, tiled=True)
        count = query_piece.shape[1]
        mask = allowed(
            lax.dynamic_slice_in_dim(segment_ids, start, count, 1), row_ids, start, row_start
        )
        probs = probabilities(
            query_piece,
            key_heads,
            lax.dynamic_slice_in_dim(logsum_all, start, count, 2),
            mask,
            scale,
        )
        dscore = score_grads(
            probs, grad_piece, value_heads, lax.dynamic_slice_in_dim(delta_all, start, count, 2)
        )
        grad_keys = (
            grad_keys
            + jnp.einsum("shqk,sqhe->skhe", dscore, query_piece, preferred_element_type=jnp.float32)
            * scale
        )
        grad_values = grad_values + jnp.einsum(
            "shqk,sqhe->skhe",
            probs.astype(jnp.bfloat16),
            grad_piece,
            preferred_element_type=jnp.float32,
        )
        grad_keys, grad_values = (grad_keys, grad_values)
        return (
            folded.reshape(rows, width),
            grad_keys.reshape(rows, width),
            grad_values.reshape(rows, width),
        )

    def layer_backward(grad_out, kept, weights):
        (
            hidden,
            normed,
            query,
            keys,
            values,
            attended,
            logsum,
            attended_low,
            middle,
            normed_two,
            pre,
            activated,
            segment_ids,
        ) = kept
        w_attn, w_proj, w_in, w_out = weights
        grad_low = grad_out.astype(jnp.bfloat16)
        grad_act = times_last(grad_low, w_out)
        gelu_back = jax.vjp(gelu_tanh, pre)[1]
        grad_pre = gelu_back(grad_act)[0].astype(jnp.bfloat16)
        norm_two_back = jax.vjp(layer_norm, middle, gains[1], biases[4])[1]
        grad_mid_norm, grad_gain_two, grad_shift_two = norm_two_back(times_last(grad_pre, w_in))
        grad_middle = grad_out + grad_mid_norm
        grad_branch = grad_middle.astype(jnp.bfloat16)
        grad_attended = times_last(grad_branch, w_proj).astype(jnp.bfloat16)
        grad_query, grad_keys, grad_values = attend_back(
            query, keys, values, attended, logsum, grad_attended, segment_ids
        )
        grad_mixed = jnp.concatenate([grad_query, grad_keys, grad_values], axis=1).astype(
            jnp.bfloat16
        )
        norm_back = jax.vjp(layer_norm, hidden, gains[0], biases[0])[1]
        grad_hid_norm, grad_gain_one, grad_shift_one = norm_back(times_last(grad_mixed, w_attn))
        grad_hidden = grad_middle + grad_hid_norm
        mixed_sums = jnp.sum(grad_mixed.astype(jnp.float32), axis=0)
        gain_grad = jnp.stack([grad_gain_one, grad_gain_two])
        bias_grad = jnp.stack(
            [
                grad_shift_one,
                mixed_sums[:width],
                mixed_sums[2 * width :],
                jnp.sum(grad_branch.astype(jnp.float32), axis=0),
                grad_shift_two,
                jnp.sum(grad_low.astype(jnp.float32), axis=0),
            ]
        )
        hid_grad = jnp.sum(grad_pre.astype(jnp.float32), axis=0)
        pairs = (
            normed,
            grad_mixed,
            attended_low,
            grad_branch,
            normed_two,
            grad_pre,
            activated,
            grad_low,
        )
        return (grad_hidden, (gain_grad, bias_grad, hid_grad), pairs)

    kept_ticks = []
    outputs_fwd = []
    received = jnp.zeros((rows, width), jnp.bfloat16)
    for tick in range(micro + 1):
        index_fwd = jnp.clip(tick - section, 0, micro - 1)
        segment_ids = lax.dynamic_index_in_dim(segments, index_fwd, 0, keepdims=False)
        source = jnp.where(first, own[min(tick, micro - 1)], received.astype(jnp.float32))
        layer_w_attn, layer_w_proj, layer_w_in, layer_w_out = weights_fwd
        layer_normed = layer_norm(source, gains[0], biases[0]).astype(jnp.bfloat16)
        mixed = times_plain(layer_normed, layer_w_attn)
        layer_query = (mixed[:, :width] + biases[1]).astype(jnp.bfloat16)
        layer_keys = mixed[:, width : 2 * width].astype(jnp.bfloat16)
        layer_values = (mixed[:, 2 * width :] + biases[2]).astype(jnp.bfloat16)
        attend_row_ids = lax.dynamic_slice_in_dim(segment_ids, row_start, local, 1)
        attend_query_heads = layer_query.reshape(heads_shape)
        stats_shape = (seqs, HEADS, local)
        best = jnp.full(stats_shape, MASKED, jnp.float32)
        absorb_key_piece = lax.all_gather(
            layer_keys.reshape(heads_shape), "shard", axis=1, tiled=True
        )
        absorb_value_piece = lax.all_gather(
            layer_values.reshape(heads_shape), "shard", axis=1, tiled=True
        )
        absorb_mask = allowed(attend_row_ids, segment_ids, row_start, jnp.int32(0))
        scores = (
            jnp.einsum(
                "sqhe,skhe->shqk",
                attend_query_heads,
                absorb_key_piece,
                preferred_element_type=jnp.float32,
            )
            * scale
        )
        scores = jnp.where(absorb_mask, scores, MASKED)
        new_best = jnp.maximum(best, jnp.max(scores, axis=-1))
        absorb_weights = jnp.where(absorb_mask, jnp.exp(scores - new_best[..., None]), 0.0)
        total = jnp.sum(absorb_weights, axis=-1)
        accum = jnp.einsum(
            "shqk,skhe->shqe",
            absorb_weights.astype(jnp.bfloat16),
            absorb_value_piece,
            preferred_element_type=jnp.float32,
        )
        best, total, accum = (new_best, total, accum)
        attend_attended = (accum / total[..., None]).transpose(0, 2, 1, 3).reshape(rows, width)
        layer_logsum = best + jnp.log(total)
        layer_attended_low = attend_attended.astype(jnp.bfloat16)
        layer_middle = source + times_plain(layer_attended_low, layer_w_proj) + biases[3]
        layer_normed_two = layer_norm(layer_middle, gains[1], biases[4]).astype(jnp.bfloat16)
        layer_pre = times_plain(layer_normed_two, layer_w_in) + hid_bias
        layer_activated = gelu_tanh(layer_pre).astype(jnp.bfloat16)
        result = layer_middle + times_plain(layer_activated, layer_w_out) + biases[5]
        layer_kept = (
            source,
            layer_normed,
            layer_query,
            layer_keys,
            layer_values,
            attend_attended,
            layer_logsum,
            layer_attended_low,
            layer_middle,
            layer_normed_two,
            layer_pre,
            layer_activated,
            segment_ids,
        )
        result, kept = (result, layer_kept)
        kept_ticks.append(kept)
        outputs_fwd.append(result)
        if tick < micro:
            received = shifted(result.astype(jnp.bfloat16), "section", 1)
    stacked = jax.tree.map(lambda *values: jnp.stack(values), *kept_ticks)
    received_grad = jnp.zeros((rows, width), jnp.bfloat16)
    grads_in = []
    pairs_list = []
    gain_total = jnp.zeros((2, width), jnp.float32)
    bias_total = jnp.zeros((6, width), jnp.float32)
    hid_total = jnp.zeros(hid_bias.shape, jnp.float32)
    for tick in range(micro + 1):
        index_kept = jnp.clip(tick - 1 + 2 * section, 0, micro)
        kept = jax.tree.map(
            lambda values: lax.dynamic_index_in_dim(values, index_kept, 0, keepdims=False), stacked
        )
        micro_index = tick - 1 + section
        valid = ((micro_index >= 0) & (micro_index < micro)).astype(jnp.float32)
        source = jnp.where(first, received_grad.astype(jnp.float32), own[min(tick, micro - 1)])
        grad_hidden, smalls, pairs = layer_backward(source, kept, weights_fwd)
        gain_total = gain_total + valid * smalls[0]
        bias_total = bias_total + valid * smalls[1]
        hid_total = hid_total + valid * smalls[2]
        pairs_list.append(pairs)
        grads_in.append(grad_hidden)
        if tick < micro:
            received_grad = shifted(grad_hidden.astype(jnp.bfloat16), "section", -1)
    start_tick = 1 - section

    def valid_rows(values):
        picked = lax.dynamic_slice_in_dim(jnp.stack(values), start_tick, micro, 0)
        return picked.reshape((micro * rows,) + picked.shape[2:])

    columns = [valid_rows([pairs[index] for pairs in pairs_list]) for index in range(8)]
    shard_count = lax.axis_size("shard")
    replica_count = lax.axis_size("replica")

    def weight_grad(inputs, grads):
        count_rows = inputs.shape[0]
        total_cols = inputs.shape[1]
        share = total_cols // (shard_count * replica_count)
        reordered = (
            inputs.reshape(count_rows, shard_count, replica_count, share)
            .transpose(0, 2, 1, 3)
            .reshape(count_rows, total_cols)
        )
        return lax.psum_scatter(
            times_first(
                lax.slice_in_dim(reordered, 0, lax.axis_size(("replica", "shard")) * share, axis=1),
                grads,
            ),
            ("replica", "shard"),
            scatter_dimension=0,
            tiled=True,
        )

    attn_part = weight_grad(columns[0], columns[1])
    proj_part = weight_grad(columns[2], columns[3])
    in_part = weight_grad(columns[4], columns[5])
    out_part = weight_grad(columns[6], columns[7])
    attn_sum, proj_sum, in_sum, out_sum = (
        lax.all_gather(attn_part.astype(jnp.bfloat16), "replica", axis=0, tiled=True).astype(
            attn_part.dtype
        ),
        lax.all_gather(proj_part.astype(jnp.bfloat16), "replica", axis=0, tiled=True).astype(
            proj_part.dtype
        ),
        lax.all_gather(in_part.astype(jnp.bfloat16), "replica", axis=0, tiled=True).astype(
            in_part.dtype
        ),
        lax.all_gather(out_part.astype(jnp.bfloat16), "replica", axis=0, tiled=True).astype(
            out_part.dtype
        ),
    )
    gain_sum, bias_sum, hid_sum = lax.psum(
        (gain_total, bias_total, hid_total), ("replica", "shard")
    )
    edge = jnp.stack(
        [jnp.where(first, grads_in[index + 1], outputs_fwd[index + 1]) for index in range(micro)]
    )
    edge = edge.reshape(1, micro, seqs, local, width)
    return (
        edge,
        attn_sum[None],
        proj_sum[None],
        in_sum[None],
        out_sum[None],
        gain_sum[None],
        bias_sum[None],
        hid_sum[None],
    )


def solution(mesh):
    return jax.shard_map(
        body,
        mesh=mesh,
        in_specs=(
            P("section", None, "replica", "shard", None),
            P(None, "replica", None),
            P("section", "shard", None),
            P("section", "shard", None),
            P("section", "shard", None),
            P("section", "shard", None),
            P("section", None, None),
            P("section", None, None),
            P("section", None),
        ),
        out_specs=(
            P("section", None, "replica", "shard", None),
            P("section", "shard", None),
            P("section", "shard", None),
            P("section", "shard", None),
            P("section", "shard", None),
            P("section", None, None),
            P("section", None, None),
            P("section", None),
        ),
        check_vma=False,
    )
```

profile of v0, /device:TPU:1, one launch (start us, length us, event | category | flops | bytes accessed | tf_op | source)
XLA Modules:
  0.0 5418.0 jit_solution(1483918912909434669)
XLA Ops:
  11.9 266.9 %all-gather.35.cloned.1.call-done = bf16[1,1600,4800]{2,1,0:T(8,128)(2,1)} async-done(((bf16[1,400,4800]{2,1,0:T(8,128)(2,1)}), bf16[1,1600,4800]{2,1,0:T(8,128)(2,1)}) %all-gather.35.cloned.1.call-update) | async-done | bytes 15360016 | tf_op jit(solution)/shard_map/all_gather | solution.py:98
  278.9 14.8 fusion.49
  305.6 54.3 %all-gather.37.cloned.1.call-done = bf16[1,1024,25,64]{1,3,2,0:T(8,128)(2,1)} async-done(((bf16[1,256,25,64]{1,3,2,0:T(8,128)(2,1)}), bf16[1,1024,25,64]{1,3,2,0:T(8,128)(2,1)}) %all-gather.37.cloned.1.call-update) | async-done | bytes 3276816 | tf_op jit(solution)/shard_map/all_gather | solution.py:246
  359.9 15.8 fusion.3
  376.9 14.3 fusion.33
  391.2 34.0 all-gather.39.cloned.1.call-done
  425.3 15.5 bitcast_convert_fusion.3
  440.7 83.6 %all-gather.41.cloned.1.call-done = bf16[1,1600,1600]{2,1,0:T(8,128)(2,1)} async-done(((bf16[1,400,1600]{2,1,0:T(8,128)(2,1)}), bf16[1,1600,1600]{2,1,0:T(8,128)(2,1)}) %all-gather.41.cloned.1.call-update) | async-done | bytes 5120016 | tf_op jit(solution)/shard_map/all_gather | solution.py:99
  531.5 341.3 %all-gather.43.cloned.1.call-done = bf16[1,1600,6400]{2,1,0:T(8,128)(2,1)} async-done(((bf16[1,400,6400]{2,1,0:T(8,128)(2,1)}), bf16[1,1600,6400]{2,1,0:T(8,128)(2,1)}) %all-gather.43.cloned.1.call-update) | async-done | bytes 20480016 | tf_op jit(solution)/shard_map/all_gather | solution.py:100
  885.9 349.2 %all-gather.33.cloned.1.call-done = bf16[1,6400,1600]{2,1,0:T(8,128)(2,1)} async-done(((bf16[1,1600,1600]{2,1,0:T(8,128)(2,1)}), bf16[1,6400,1600]{2,1,0:T(8,128)(2,1)}) %all-gather.33.cloned.1.call-update) | async-done | bytes 20480016 | tf_op jit(solution)/shard_map/all_gather | solution.py:101
  1235.1 16.2 fusion.243
  1258.1 15.2 fusion.47
  1279.5 60.2 %all-gather.45.cloned.1.call-done = bf16[1,1024,25,64]{1,3,2,0:T(8,128)(2,1)} async-done(((bf16[1,256,25,64]{1,3,2,0:T(8,128)(2,1)}), bf16[1,1024,25,64]{1,3,2,0:T(8,128)(2,1)}) %all-gather.45.cloned.1.call-update) | async-done | bytes 3276816 | tf_op jit(solution)/shard_map/all_gather | solution.py:246
  1339.7 15.8 fusion.4
  1356.7 14.8 fusion.35
  1371.4 33.6 all-gather.47.cloned.1.call-done
  1405.0 13.9 bitcast_convert_fusion.2
  1437.6 16.9 fusion.436
  1460.9 15.2 fusion.45
  1501.6 40.5 all-gather.49.cloned.1.call-done
  1542.2 15.7 fusion.5
  1559.1 14.3 fusion.37
  1573.4 33.9 all-gather.51.cloned.1.call-done
  1607.4 14.5 bitcast_convert_fusion.1
  1651.0 14.5 convert_reduce_fusion.2
  1671.2 15.8 multiply_reduce_fusion.4
  1703.5 14.3 all_gather.111
  1717.8 16.1 all-gather
  1734.5 14.8 fusion.184
  1749.3 14.7 fusion.179
  1764.0 43.5 all-gather.55.cloned.1.call-done
  1807.4 18.4 multiply_convert_fusion.11
  1825.8 46.8 all-gather.59.cloned.1.call-done
  1872.6 17.0 multiply_convert_fusion.10
  1928.6 14.7 convert_reduce_fusion.1
  1943.2 15.9 multiply_reduce_fusion.15
  1984.4 16.6 all-gather.1
  2000.9 15.2 fusion.173
  2016.1 14.7 fusion.168
  2031.1 17.6 all_gather.117
  2048.7 23.8 all-gather.63.cloned.1.call-done
  2072.5 18.0 multiply_convert_fusion.9
  2090.6 47.1 all-gather.67.cloned.1.call-done
  2150.7 16.6 multiply_convert_fusion.8
  2194.2 14.9 convert_reduce_fusion
  2209.1 15.8 multiply_reduce_fusion
  2252.6 16.7 copy.58
  2269.3 15.2 reshape_reshape.15
  2293.2 21.8 fusion.441
  2383.8 13.9 all-gather.2
  2397.7 13.3 fusion.162
  2411.1 14.5 fusion.157
  2465.2 16.8 multiply_convert_fusion.7
  2483.5 14.7 all_gather.123
  2513.0 17.2 multiply_convert_fusion.6
  2556.3 13.6 fusion.438
  2569.9 1597.1 %fusion.420 = (f32[104,4800]{1,0:T(8,128)}, f32[112,1600]{1,0:T(8,128)S(1)}) fusion(f32[1600,4800]{1,0:T(8,128)} %fusion.438, f32[1600,1600]{1,0:T(8,128)} %fusion.439), kind=kCustom, calls=%all-reduce-scatter.3 | all-reduce-scatter fusion | flops 10854402 | bytes 43674112
  4169.7 20.0 fusion.440
  4194.9 877.6 %fusion.2 = f32[104,6400]{1,0:T(8,128)S(1)} fusion(f32[1600,6400]{1,0:T(8,128)} %fusion.440), kind=kCustom, calls=%all-reduce-scatter.2 | all-reduce-scatter fusion | flops 10649601 | bytes 43622912
  5075.4 14.5 collective-permute-done.7
  5155.3 17.9 select_bitcast_fusion
  5189.0 44.0 all-gather.79.cloned.1.call-done
  5238.5 59.0 %all-gather.77.cloned.1.call-done = bf16[1600,1600]{1,0:T(8,128)(2,1)} async-done(((bf16[400,1600]{1,0:T(8,128)(2,1)}), bf16[1600,1600]{1,0:T(8,128)(2,1)}) %all-gather.77.cloned.1.call-update) | async-done | bytes 5120016 | tf_op jit(solution)/shard_map/all_gather | solution.py:367
  5304.8 102.0 %all-reduce.10.cloned.1.call-done = (f32[1,2,1600]{2,1,0:T(2,128)}, f32[1,6,1600]{2,0,1:T(1,128)}, f32[1,6400]{1,0:T(1,128)}) async-done(((f32[1,2,1600]{2,1,0:T(2,128)}, f32[1,6,1600]{2,0,1:T(1,128)}, f32[1,6400]{1,0:T(1,128)}), (f32[1,2,1600]{2,1,0:T(2,128)}, f32[1,6,1600]{2,0,1:T(1,128)}, f32[1,6400]{1,0:T(1,128)})) %all-reduce.10.cloned.1.call-update) | async-done | bytes 76816 | tf_op jit(solution)/shard_map/psum | solution.py:371
  (667 shorter events, 552.9 us)
Async XLA Ops:
  7.2 271.7 %all-gather.35.cloned.1.call-start = ((), (), s32[]{:S(2)}) async-start(), calls=%async_computation.2 | async-start | bytes 19456000 | tf_op jit(solution)/shard_map/all_gather | solution.py:98
  7.9 352.0 %all-gather.37.cloned.1.call-start = ((), (), s32[]{:S(2)}) async-start(), calls=%async_computation.3 | async-start | bytes 4096000 | tf_op jit(solution)/shard_map/all_gather | solution.py:246
  9.7 2217.3 %copy-start = (f32[1,2,1,256,1600]{3,4,2,1,0:T(8,128)}, f32[1,2,1,256,1600]{3,4,2,1,0:T(8,128)S(1)}, u32[]{:S(2)}) copy-start(f32[1,2,1,256,1600]{3,4,2,1,0:T(8,128)S(1)} %convert_element_type.372) | copy-start | bytes 9830404
  9.7 283.9 %copy-start.79 = (f32[1600]{0:T(1024)}, f32[1600]{0:T(1024)S(1)}, u32[]{:S(2)}) copy-start(f32[1600]{0:T(1024)S(1)} %get-tuple-element.73) | copy-start | bytes 19204
  10.7 283.0 %copy-start.107 = (f32[1600]{0:T(1024)}, f32[1600]{0:T(1024)S(1)}, u32[]{:S(2)}) copy-start(f32[1600]{0:T(1024)S(1)} %get-tuple-element.70) | copy-start | bytes 19204
  10.7 285.5 %copy-start.92 = (f32[1600]{0:T(1024)}, f32[1600]{0:T(1024)S(1)}, u32[]{:S(2)}) copy-start(f32[1600]{0:T(1024)S(1)} %get-tuple-element.68) | copy-start | bytes 19204
  10.7 285.5 %copy-start.94 = (f32[1600]{0:T(1024)}, f32[1600]{0:T(1024)S(1)}, u32[]{:S(2)}) copy-start(f32[1600]{0:T(1024)S(1)} %get-tuple-element.69) | copy-start | bytes 19204
  10.9 282.7 %copy-start.149 = (f32[256]{0:T(256)}, f32[256]{0:T(256)S(1)}, u32[]{:S(2)}) copy-start(f32[256]{0:T(256)S(1)} %broadcast_multiply_fusion.11) | copy-start | bytes 3076
  11.9 281.7 %copy-start.166 = (f32[256]{0:T(256)}, f32[256]{0:T(256)S(1)}, u32[]{:S(2)}) copy-start(f32[256]{0:T(256)S(1)} %add_rsqrt_fusion.5) | copy-start | bytes 3076
  296.1 129.2 %all-gather.39.cloned.1.call-start = ((), (), s32[]{:S(2)}) async-start(), calls=%async_computation.4 | async-start | bytes 4096000 | tf_op jit(solution)/shard_map/all_gather | solution.py:249
  299.8 224.6 %all-gather.41.cloned.1.call-start = ((), (), s32[]{:S(2)}) async-start(), calls=%async_computation.5 | async-start | bytes 6656000 | tf_op jit(solution)/shard_map/all_gather | solution.py:99
  300.3 572.5 %all-gather.43.cloned.1.call-start = ((), (), s32[]{:S(2)}) async-start(), calls=%async_computation.6 | async-start | bytes 25600000 | tf_op jit(solution)/shard_map/all_gather | solution.py:100
  301.0 934.2 %all-gather.33.cloned.1.call-start = ((), (), s32[]{:S(2)}) async-start(), calls=%async_computation.1 | async-start | bytes 26624000 | tf_op jit(solution)/shard_map/all_gather | solution.py:101
  301.5 1038.2 %all-gather.45.cloned.1.call-start = ((), (), s32[]{:S(2)}) async-start(), calls=%async_computation.7 | async-start | bytes 4096000 | tf_op jit(solution)/shard_map/all_gather | solution.py:246
  359.9 17.0 copy-start.73
  1251.3 4.4 collective-permute-start
  1275.7 129.3 %all-gather.47.cloned.1.call-start = ((), (), s32[]{:S(2)}) async-start(), calls=%async_computation.8 | async-start | bytes 4096000 | tf_op jit(solution)/shard_map/all_gather | solution.py:249
  1279.4 262.7 %all-gather.49.cloned.1.call-start = ((), (), s32[]{:S(2)}) async-start(), calls=%async_computation.9 | async-start | bytes 4096000 | tf_op jit(solution)/shard_map/all_gather | solution.py:246
  1454.5 4.6 collective-permute-start.1
  1459.4 16.7 copy-start.140
  1460.9 17.7 copy-start.93
  1460.9 17.7 copy-start.95
  1478.6 128.8 %all-gather.51.cloned.1.call-start = ((), (), s32[]{:S(2)}) async-start(), calls=%async_computation.10 | async-start | bytes 4096000 | tf_op jit(solution)/shard_map/all_gather | solution.py:249
  1482.3 252.2 %all-gather.53.cloned.1.call-start = ((), (), s32[]{:S(2)}) async-start(), calls=%async_computation.11 | async-start | bytes 4096000 | tf_op jit(solution)/shard_map/all_gather | solution.py:115
  1489.1 260.3 %all-gather.57.cloned.1.call-start = ((), (), s32[]{:S(2)}) async-start(), calls=%async_computation.13 | async-start | bytes 4096000 | tf_op jit(solution)/shard_map/all_gather | solution.py:135
  1494.1 313.3 %all-gather.55.cloned.1.call-start = ((), (), s32[]{:S(2)}) async-start(), calls=%async_computation.12 | async-start | bytes 4096000 | tf_op jit(solution)/shard_map/all_gather | solution.py:116
  1496.1 376.6 %all-gather.59.cloned.1.call-start = ((), (), s32[]{:S(2)}) async-start(), calls=%async_computation.14 | async-start | bytes 4096000 | tf_op jit(solution)/shard_map/all_gather | solution.py:136
  1496.5 45.6 copy-start.72
  1669.3 17.7 copy-start.2
  1671.1 15.9 copy-start.7
  1671.2 15.9 copy-start.9
  1671.2 15.9 copy-start.112
  1695.4 305.6 %all-gather.61.cloned.1.call-start = ((), (), s32[]{:S(2)}) async-start(), calls=%async_computation.15 | async-start | bytes 4096000 | tf_op jit(solution)/shard_map/all_gather | solution.py:115
  1696.0 320.1 %all-gather.65.cloned.1.call-start = ((), (), s32[]{:S(2)}) async-start(), calls=%async_computation.17 | async-start | bytes 4096000 | tf_op jit(solution)/shard_map/all_gather | solution.py:135
  1697.7 374.9 %all-gather.63.cloned.1.call-start = ((), (), s32[]{:S(2)}) async-start(), calls=%async_computation.16 | async-start | bytes 4096000 | tf_op jit(solution)/shard_map/all_gather | solution.py:116
  1700.5 33.5 copy-start.172
  1700.5 34.0 copy-start.171
  1702.8 46.5 copy-start.97
  1703.5 45.8 copy-start.106
  1807.4 65.2 %copy-start.90 = (pred[1024,256]{1,0:T(8,128)(4,1)S(1)}, pred[1024,256]{1,0:T(8,128)(4,1)}, u32[]{:S(2)}) copy-start(pred[1024,256]{1,0:T(8,128)(4,1)} %get-tuple-element.175) | copy-start | bytes 786436
  1921.1 4.7 collective-permute-start.2
  1924.4 213.3 %all-gather.67.cloned.1.call-start = ((), (), s32[]{:S(2)}) async-start(), calls=%async_computation.18 | async-start | bytes 4096000 | tf_op jit(solution)/shard_map/all_gather | solution.py:136
  1971.5 426.3 %all-gather.69.cloned.1.call-start = ((), (), s32[]{:S(2)}) async-start(), calls=%async_computation.19 | async-start | bytes 4096000 | tf_op jit(solution)/shard_map/all_gather | solution.py:115
  1972.2 438.9 %all-gather.73.cloned.1.call-start = ((), (), s32[]{:S(2)}) async-start(), calls=%async_computation.21 | async-start | bytes 4096000 | tf_op jit(solution)/shard_map/all_gather | solution.py:135
  1972.8 492.4 %all-gather.71.cloned.1.call-start = ((), (), s32[]{:S(2)}) async-start(), calls=%async_computation.20 | async-start | bytes 4096000 | tf_op jit(solution)/shard_map/all_gather | solution.py:116
  1984.3 528.7 %all-gather.75.cloned.1.call-start = ((), (), s32[]{:S(2)}) async-start(), calls=%async_computation.22 | async-start | bytes 4096000 | tf_op jit(solution)/shard_map/all_gather | solution.py:136
  2184.0 7.7 collective-permute-start.3
  2233.5 2893.8 %reduce-scatter.8.cloned.1.call-start = ((), (), s32[]{:S(2)}) async-start(), calls=%async_computation.23 | async-start | bytes 45260800 | tf_op jit(solution)/shard_map/reduce_scatter | solution.py:343
  2315.0 2860.2 %all-gather.81.cloned.1.call-start = ((), (), s32[]{:S(2)}) async-start(), calls=%async_computation.26 | async-start | bytes 1730560 | tf_op jit(solution)/shard_map/all_gather | solution.py:361
  2316.7 16.2 copy-start.28
  2325.0 16.0 copy-start.37
  2325.0 16.0 copy-start.38
  2325.0 16.0 copy-start.39
  2381.1 16.6 copy-start.18
  2569.9 1599.8 %copy-start.74 = (bf16[512,1600]{0,1:T(8,128)(2,1)S(1)}, bf16[512,1600]{0,1:T(8,128)(2,1)}, u32[]{:S(2)}) copy-start(bf16[512,1600]{0,1:T(8,128)(2,1)} %reshape.1999) | copy-start | bytes 4915204
  4167.1 22.7 collective-permute-start.5
  4168.4 21.4 collective-permute-start.6
  4194.8 985.0 %all-gather.83.cloned.1.call-start = ((), (), s32[]{:S(2)}) async-start(), calls=%async_computation.27 | async-start | bytes 6656000 | tf_op jit(solution)/shard_map/all_gather | solution.py:364
  5073.5 16.4 collective-permute-start.7
  5102.6 130.4 %all-gather.79.cloned.1.call-start = ((), (), s32[]{:S(2)}) async-start(), calls=%async_computation.25 | async-start | bytes 5058560 | tf_op jit(solution)/shard_map/all_gather | solution.py:358
  5102.8 13.6 collective-permute-start.4
  5127.2 170.2 %all-gather.77.cloned.1.call-start = ((), (), s32[]{:S(2)}) async-start(), calls=%async_computation.24 | async-start | bytes 6656000 | tf_op jit(solution)/shard_map/all_gather | solution.py:367
  5130.5 276.4 %all-reduce.10.cloned.1.call-start = ((), (), s32[]{:S(2)}) async-start(), calls=%async_computation.28 | async-start | bytes 157696 | tf_op jit(solution)/shard_map/psum | solution.py:371
  5155.3 17.9 copy-start.31
  (152 other events, 832.6 us)
Sparse Core Ops, SparseCore 0:
  9.6 269.2 all-gather.34
  296.2 63.6 all-gather.36
  361.5 63.7 all-gather.38
  426.7 97.6 all-gather.40
  525.8 347.0 all-gather.42
  874.3 360.8 all-gather.32
  1275.8 63.8 all-gather.44
  1341.3 63.7 all-gather.46
  1478.7 63.4 all-gather.48
  1543.6 63.7 all-gather.50
  1608.9 63.7 all-gather.52
  1674.1 67.7 all-gather.56
  1743.5 63.8 all-gather.54
  1808.9 63.7 all-gather.58
  1874.1 65.3 all-gather.60
  1940.9 64.3 all-gather.64
  2006.7 65.8 all-gather.62
  2074.0 63.6 all-gather.66
  2139.3 63.7 all-gather.68
  2204.4 63.7 all-gather.72
  2269.8 63.7 all-gather.70
  2335.1 65.8 all-gather.74
  2403.4 1556.3 reduce-scatter.7
  4194.9 42.8 all-gather.80
  5102.7 77.0 all-gather.82
  5181.5 51.4 all-gather.78
  5235.3 62.1 all-gather.76
  5303.9 102.8 all-reduce.9
where the time goes:
time: 5430 us; the launch traced here: 5420 us
  blocking collectives  2570 us (47%)
  waiting for transfers between devices  1700 us (31%)
  matrix products  675 us (12%)
  local copies, waits for them, and re-layouts  222 us (4%)
  other arithmetic  215 us (4%)
    unnamed x2, blocking collectives  2470 us
    all_gather x1, waiting for transfers between devices, body(): lax.all_gather(fc_out_weight, 'shard', axis=1, tiled=True)  349 us
    all_gather x1, waiting for transfers between devices, body(): lax.all_gather(fc_in_weight, 'shard', axis=1, tiled=True)  341 us
    all_gather x1, waiting for transfers between devices, body(): lax.all_gather(attn_weight, 'shard', axis=1, tiled=True)  267 us
    all_gather x3, waiting for transfers between devices, body(): lax.all_gather(layer_keys.reshape(heads_shape), 'shard', axis=1, tiled=True)  155 us
    dot_general x12, matrix products, times_plain(): return jnp.dot(left, right, preferred_element_type=jnp.float32)  148 us
    dot_general x12, matrix products, times_last(): lax.dot_general(left, right, (((1,), (1,)), ((), ())), preferred_element_...  142 us
  transfers between devices with their start and end apart: 36, of which 23 were waited for; matrix products, arithmetic and copies ran while one was open for 64% of the time, Pallas kernels for 0%

commit v1 on v0

v1 whole, which is shorter than its diff:
```python
from functools import partial

import jax
import jax.numpy as jnp
from jax import lax
from jax.experimental import pallas as pl
from jax.experimental.pallas import tpu as pltpu
from jax.sharding import Mesh, PartitionSpec as P

HEADS = 25
HEAD = 64
EPSILON = 1e-05
MASKED = -1e30
BF = jnp.bfloat16
F32 = jnp.float32
SWAP = [(0, 1), (1, 0)]
SIDE = [(0, 1), (1, 0), (2, 3), (3, 2)]
ACROSS = [(0, 2), (2, 0), (1, 3), (3, 1)]
CORNER = [(0, 3), (3, 0), (1, 2), (2, 1)]


def dot(left, right, contract):
    return lax.dot_general(
        left, right, ((contract[:1], contract[1:]), ((), ())), preferred_element_type=F32
    )


def norm_stats(value):
    centred = value - jnp.mean(value, axis=-1, keepdims=True)
    variance = jnp.mean(centred * centred, axis=-1, keepdims=True)
    inverse = lax.rsqrt(variance + EPSILON)
    return centred * inverse, inverse


def norm_back(grad, value, gain):
    unit, inverse = norm_stats(value)
    grad_unit = grad * gain
    mean_one = jnp.mean(grad_unit, axis=-1, keepdims=True)
    mean_two = jnp.mean(grad_unit * unit, axis=-1, keepdims=True)
    grad_value = inverse * (grad_unit - mean_one - unit * mean_two)
    return grad_value, jnp.sum(grad * unit, axis=0), jnp.sum(grad, axis=0)


def gelu_pair(x):
    c = 0.7978845608028654
    square = x * x
    th = jnp.tanh(c * x * (1.0 + 0.044715 * square))
    value = 0.5 * x * (1.0 + th)
    slope = 0.5 * (1.0 + th) + 0.5 * x * (1.0 - th * th) * c * (1.0 + 3 * 0.044715 * square)
    return value, slope


def spots(chunk, piece, block, n, teams):
    order = ((0, 2, 1, 3), (0, 1, 2, 3))[chunk]
    return [
        (index * n, order[piece * (block // n) + index], chunk * n) for index in range(block // n)
    ]


def attend_kernel(grouped, q_ref, k_ref, v_ref, bias_ref, *out_refs):
    *outs, lse_ref = out_refs
    length = q_ref.shape[1]
    half = length // 2
    n = half // 4
    block = min(256, half)
    for chunk in range(2):
        extent = half * (chunk + 1)
        for piece in range(half // block):
            at = chunk * half + piece * block
            query = q_ref[:, at : at + block] * jnp.asarray(HEAD ** (-0.5), BF)
            scores = dot(k_ref[:, :extent], query, (0, 0)) + bias_ref[:extent, at : at + block]
            best = jnp.max(scores, axis=0, keepdims=True)
            weights = jnp.exp(scores - best)
            total = jnp.sum(weights, axis=0, keepdims=True)
            out = dot(v_ref[:, :extent], weights.astype(BF), (1, 0)) / total
            out = out.astype(BF)
            if grouped:
                for here, owner, there in spots(chunk, piece, block, n, 4):
                    outs[owner][:, there : there + n] = out[:, here : here + n]
            else:
                outs[0][:, at : at + block] = out
            lse_ref[0, :, at : at + block] = best + jnp.log(total)


def attend_back_kernel(grouped, q_ref, k_ref, v_ref, bias_ref, lse_ref, *refs):
    *g_refs, dq_ref, dk_ref, dv_ref, keys, values = refs
    length = q_ref.shape[1]
    half = length // 2
    n = half // 4
    block = min(256, half)
    scale = HEAD ** (-0.5)
    keys[...] = jnp.zeros_like(keys)
    values[...] = jnp.zeros_like(values)
    for chunk in range(2):
        extent = half * (chunk + 1)
        for piece in range(half // block):
            at = chunk * half + piece * block
            query = q_ref[:, at : at + block] * jnp.asarray(scale, BF)
            if grouped:
                grad = jnp.concatenate(
                    [
                        g_refs[owner][:, there : there + n]
                        for _, owner, there in spots(chunk, piece, block, n, 4)
                    ],
                    axis=1,
                )
            else:
                grad = g_refs[0][:, at : at + block]
            scores = dot(k_ref[:, :extent], query, (0, 0)) + bias_ref[:extent, at : at + block]
            probs = jnp.exp(scores - lse_ref[0, :, at : at + block])
            inner = dot(v_ref[:, :extent], grad, (0, 0))
            rowdot = jnp.sum(probs * inner, axis=0, keepdims=True)
            dscore = (probs * (inner - rowdot)).astype(BF)
            values[:, :extent] += dot(grad, probs.astype(BF), (1, 1))
            keys[:, :extent] += dot(query, dscore, (1, 1))
            dq_ref[:, at : at + block] = (dot(k_ref[:, :extent], dscore, (1, 0)) * scale).astype(BF)
    dk_ref[...] = keys[...].astype(BF)
    dv_ref[...] = values[...].astype(BF)


def attend(mixed, bias, slots, grouped):
    length = mixed.shape[1]
    part = lambda first: pl.BlockSpec((HEAD, length), lambda h: (first + h, 0))
    whole = pl.BlockSpec((length, length), lambda h: (0, 0))
    count, span = (4, length // 4) if grouped else (1, length)
    *outs, lse = pl.pallas_call(
        partial(attend_kernel, grouped),
        grid=(slots,),
        in_specs=[part(0), part(slots), part(2 * slots), whole],
        out_specs=[pl.BlockSpec((HEAD, span), lambda h: (h, 0))] * count
        + [pl.BlockSpec((1, 1, length), lambda h: (h, 0, 0))],
        out_shape=[jax.ShapeDtypeStruct((slots * HEAD, span), BF)] * count
        + [jax.ShapeDtypeStruct((slots, 1, length), F32)],
        compiler_params=pltpu.CompilerParams(vmem_limit_bytes=40 * 2**20),
        cost_estimate=pl.CostEstimate(
            flops=3 * slots * length * length * HEAD,
            bytes_accessed=4 * length * length + 8 * slots * HEAD * length,
            transcendentals=slots * length * length,
        ),
    )(mixed, mixed, mixed, bias)
    return outs, lse


def attend_back(mixed, grads, bias, lse, slots, grouped):
    length = mixed.shape[1]
    part = lambda first: pl.BlockSpec((HEAD, length), lambda h: (first + h, 0))
    whole = pl.BlockSpec((length, length), lambda h: (0, 0))
    one = jax.ShapeDtypeStruct((slots * HEAD, length), BF)
    count, span = (4, length // 4) if grouped else (1, length)
    return pl.pallas_call(
        partial(attend_back_kernel, grouped),
        grid=(slots,),
        in_specs=[
            part(0),
            part(slots),
            part(2 * slots),
            whole,
            pl.BlockSpec((1, 1, length), lambda h: (h, 0, 0)),
        ]
        + [pl.BlockSpec((HEAD, span), lambda h: (h, 0))] * count,
        out_specs=[part(0), part(0), part(0)],
        out_shape=[one, one, one],
        scratch_shapes=[pltpu.VMEM((HEAD, length), F32), pltpu.VMEM((HEAD, length), F32)],
        compiler_params=pltpu.CompilerParams(vmem_limit_bytes=40 * 2**20),
        cost_estimate=pl.CostEstimate(
            flops=8 * slots * length * length * HEAD,
            bytes_accessed=4 * length * length + 14 * slots * HEAD * length,
            transcendentals=slots * length * length,
        ),
    )(mixed, mixed, mixed, bias, lse, *grads)


TOPS = (0, 2, 1, 3)
LOWS = (0, 1, 2, 3)


def kernel_call(kernel, member, inputs, outputs, scratch=()):
    count = len(inputs)
    size = sum(x.size * x.dtype.itemsize for x in inputs)
    size += sum(x.size * x.dtype.itemsize for x in outputs)
    return pl.pallas_call(
        kernel,
        in_specs=[pl.BlockSpec(memory_space=pltpu.SMEM)]
        + [pl.BlockSpec(memory_space=pltpu.VMEM)] * count,
        out_specs=[pl.BlockSpec(memory_space=pltpu.VMEM)] * len(outputs),
        out_shape=outputs,
        scratch_shapes=list(scratch),
        compiler_params=pltpu.CompilerParams(vmem_limit_bytes=48 * 2**20),
        cost_estimate=pl.CostEstimate(flops=0, bytes_accessed=size, transcendentals=0),
    )(member.reshape(1), *inputs)


def slab_places(member, rows, step, slab):
    found = []
    for part, order in enumerate((TOPS, LOWS)):
        for turn in order:
            owner = member ^ turn
            for block in (2 * part, 2 * part + 1):
                found.append((owner, block * rows + owner * step))
    return found


def sort_heads_kernel(slots, rows, step, slab, member_ref, *refs):
    *got, out_ref, whole = refs
    member = member_ref[0]
    width = whole.shape[0]
    high = slots * HEAD
    for turn in range(4):
        owner = member ^ turn
        at = jnp.minimum(owner * high, width - high)
        spare = (owner * high - at) // HEAD
        if turn == 0:
            pass
        for slot in range(slots):

            @pl.when(slot >= spare)
            def _(turn=turn, slot=slot, at=at):
                to = pl.multiple_of(at + slot * HEAD, HEAD)
                whole[pl.ds(to, HEAD), :] = got[turn][slot * HEAD : (slot + 1) * HEAD, :]

    line = lax.broadcasted_iota(jnp.int32, (slab, 1), 0)
    for index, (owner, at) in enumerate(slab_places(member, rows, step, slab)):
        rows_here = whole[pl.ds(pl.multiple_of(at, 16), slab), :]
        keep = (line < step) | (owner == 3)
        out_ref[index * slab : (index + 1) * slab, :] = jnp.where(
            keep, rows_here, jnp.zeros_like(rows_here)
        )


def split_heads_kernel(slots, rows, step, slab, member_ref, value_ref, *refs):
    *outs, whole = refs
    member = member_ref[0]
    width = whole.shape[0]
    high = slots * HEAD
    for index, (owner, at) in enumerate(slab_places(member, rows, step, slab)):
        first = index * slab
        whole[pl.ds(pl.multiple_of(at, 16), step), :] = value_ref[first : first + step, :]

        @pl.when(owner == 3)
        def _(first=first, at=at):
            to = pl.multiple_of(at + step, 16)
            whole[pl.ds(to, slab - step), :] = value_ref[first + step : first + slab, :]

    for turn in range(4):
        owner = member ^ turn
        at = jnp.minimum(owner * high, width - high)
        spare = owner * high - at
        line = lax.broadcasted_iota(jnp.int32, (high, 1), 0)
        rows_here = whole[pl.ds(pl.multiple_of(at, HEAD), high), :]
        outs[turn][...] = jnp.where(line >= spare, rows_here, jnp.zeros_like(rows_here))


def member_rows(refs, member, owner, cut, rows):
    turn = member ^ owner
    twin = (turn & 1) * 2 + turn // 2
    found = []
    for ref in refs:
        top = ref[pl.ds(pl.multiple_of(twin * cut, 16), cut), :]
        low = ref[pl.ds(pl.multiple_of(4 * cut + turn * (rows - cut), 16), rows - cut), :]
        found.append((top.astype(F32), low.astype(F32)))
    return found


def finish_attn_kernel(slots, cut, member_ref, left_ref, right_ref, out_ref):
    member = member_ref[0]
    rows = out_ref.shape[0]
    width = out_ref.shape[1] // 3
    high = slots * HEAD
    for owner in range(4):
        start = min(owner * high, width - high)
        spare = owner * high - start
        (left, right) = member_rows((left_ref, right_ref), member, owner, cut, rows)
        for lines, place in ((0, slice(0, cut)), (1, slice(cut, rows))):
            both = jnp.concatenate([left[lines], right[lines]], axis=1)
            for third in range(3):
                to = third * width + start + spare
                out_ref[place, to : to + high - spare] = both[
                    :, third * high + spare : (third + 1) * high
                ]


def finish_proj_kernel(step, slab, cut, member_ref, left_ref, right_ref, out_ref):
    member = member_ref[0]
    rows = out_ref.shape[0]
    for owner in range(4):
        size = slab if owner == 3 else step
        (left, right) = member_rows((left_ref, right_ref), member, owner, cut, slab)
        both = [jnp.concatenate([left[i], right[i]], axis=1) for i in range(2)]
        whole = jnp.concatenate(both)
        out_ref[owner * step : owner * step + size, :] = whole[:size]


def finish_in_kernel(cut, member_ref, value_ref, out_ref):
    member = member_ref[0]
    rows = out_ref.shape[0]
    part = out_ref.shape[1] // 16
    for owner in range(4):
        ((top, low),) = member_rows((value_ref,), member, owner, cut, rows)
        for block in range(4):
            to = (block * 4 + owner) * part
            out_ref[:cut, to : to + part] = top[:, block * part : (block + 1) * part]
            out_ref[cut:, to : to + part] = low[:, block * part : (block + 1) * part]


def finish_out_kernel(cut, member_ref, value_ref, out_ref):
    member = member_ref[0]
    rows = out_ref.shape[0] // 4
    for owner in range(4):
        ((top, low),) = member_rows((value_ref,), member, owner, cut, rows)
        out_ref[owner * rows : owner * rows + cut, :] = top
        out_ref[owner * rows + cut : (owner + 1) * rows, :] = low


def tie(value, *others):
    return lax.optimization_barrier((value, others))[0]


def body(
    replicas,
    shards,
    boundary,
    segments,
    attn_weight,
    proj_weight,
    fc_in_weight,
    fc_out_weight,
    norm_gains,
    vector_bias,
    fc_in_bias,
):
    sub = shards // replicas
    team = replicas * sub
    fast = replicas == 4 and sub == 1
    team_axes = ("replica", "sub")
    row_axes = ("seq", "sub")
    chip_axes = ("replica", "seq", "sub")
    section = lax.axis_index("section")
    first = section == 0
    member = lax.axis_index(team_axes)
    local = boundary.shape[3]
    width = boundary.shape[4]
    hidden = fc_in_bias.shape[1]
    n = local // 2
    length = segments.shape[2]
    half = length // 2
    slots = -(-HEADS // team)
    heads_width = slots * HEAD
    hid = hidden // team
    cols = width // team

    def head_start(index):
        return jnp.minimum(index * slots, HEADS - slots)

    def spare_heads(index):
        return min(max(index * slots - (HEADS - slots), 0), slots)

    start = head_start(member) * HEAD

    def cross(value, pairs=SWAP):
        return lax.ppermute(value, "section", pairs)

    def side(value):
        return lax.ppermute(value, "replica", SIDE)

    def across(value):
        return lax.ppermute(value, "replica", ACROSS)

    def corner(value):
        return lax.ppermute(value, "replica", CORNER)

    def pick(a, b):
        return jnp.where(first, a, b)

    def flat(p, z):
        return p * shards + z

    rounds = []
    for turn in range(2):
        pairs = []
        for p in range(replicas):
            for z in range(shards):
                slot = z // (shards // 2)
                h = turn if slot == 0 else 1 - turn
                j = 2 * (z % (shards // 2)) + h
                target = flat(j // sub, p * sub + j % sub)
                pairs.append((flat(p, z), target))
        rounds.append(pairs)
    place = lax.axis_index(row_axes)
    early = place < shards // 2
    even = member % 2 == 0

    def to_team(value):
        top, low = value[:n], value[n:]
        one = lax.ppermute(jnp.where(early, top, low), chip_axes, rounds[0])
        two = lax.ppermute(jnp.where(early, low, top), chip_axes, rounds[1])
        return jnp.concatenate([jnp.where(even, one, two), jnp.where(even, two, one)])

    def from_team(value):
        top, low = value[:n], value[n:]
        one = lax.ppermute(
            jnp.where(even, top, low), chip_axes, [(b, a) for a, b in rounds[0]]
        )
        two = lax.ppermute(
            jnp.where(even, low, top), chip_axes, [(b, a) for a, b in rounds[1]]
        )
        return jnp.concatenate([jnp.where(early, one, two), jnp.where(early, two, one)])

    if fast:
        order_a = [member, member ^ 2, member ^ 1, member ^ 3]
        order_b = [member, member ^ 1, member ^ 2, member ^ 3]
    else:
        order_a = order_b = list(range(team))

    def gather(value, cut):
        a, b = value[:cut], value[cut:]
        if not fast:
            return jnp.concatenate(
                [
                    lax.all_gather(a, team_axes, axis=0, tiled=True),
                    lax.all_gather(b, team_axes, axis=0, tiled=True),
                ]
            )
        near_a, near_b = across(a), side(b)
        far_a = side(jnp.concatenate([a, near_a]))
        far_b = across(jnp.concatenate([b, near_b]))
        return jnp.concatenate([a, near_a, far_a, b, near_b, far_b])

    def scatter(value):
        middle_row = value.shape[0] // 2
        a, b = value[:middle_row], value[middle_row:]
        if not fast:
            return jnp.concatenate(
                [
                    lax.psum_scatter(a.astype(F32), team_axes, scatter_dimension=0, tiled=True),
                    lax.psum_scatter(b.astype(F32), team_axes, scatter_dimension=0, tiled=True),
                ]
            )
        m = middle_row // 4
        got_a, got_b = side(a[2 * m :]), across(b[2 * m :])
        sent_a = (a[m : 2 * m].astype(F32) + got_a[m:]).astype(BF)
        sent_b = (b[m : 2 * m].astype(F32) + got_b[m:]).astype(BF)
        last_a, last_b = across(sent_a), side(sent_b)
        sum_a = a[:m].astype(F32) + got_a[:m] + last_a
        sum_b = b[:m].astype(F32) + got_b[:m] + last_b
        return jnp.concatenate([sum_a, sum_b])

    if fast:
        rows = width // replicas
        slab = -(-rows // 64) * 16
        step = (rows - slab) // 3
        cut = (rows // 32) * 16
        wide = jax.ShapeDtypeStruct((16 * slab, 2 * n), BF)
        one = jax.ShapeDtypeStruct((heads_width, 2 * n), BF)
        scratch = [pltpu.VMEM((width, 2 * n), BF)]

    def heads_to_tokens(values):
        if fast:
            own, near, over, far = values
            got = [own, side(near), across(over), corner(far)]
            kernel = partial(sort_heads_kernel, slots, rows, step, slab)
            return kernel_call(kernel, member, got, [wide], scratch)[0]
        pieces = values[0].reshape(heads_width, 2, team, n).transpose(2, 0, 1, 3)
        got = lax.all_to_all(pieces, team_axes, 0, 0, tiled=True)
        got = got.reshape(team, heads_width, 2 * n)
        pieces = []
        for index in range(team):
            spare = spare_heads(index) * HEAD
            if spare < heads_width:
                pieces.append(got[index, spare:])
        return jnp.concatenate(pieces)

    def tokens_to_heads(value):
        if fast:
            kernel = partial(split_heads_kernel, slots, rows, step, slab)
            own, near, over, far = kernel_call(kernel, member, [value], [one] * 4, scratch)
            return [own, side(near), across(over), corner(far)]

        def of(index):
            return lax.dynamic_slice_in_dim(value, head_start(index) * HEAD, heads_width, 0)

        pieces = jnp.stack([of(index) for index in range(team)])
        got = lax.all_to_all(pieces, team_axes, 0, 0, tiled=True)
        got = got.reshape(team, heads_width, 2, n).transpose(1, 2, 0, 3)
        whole = got.reshape(heads_width, length)
        spare = member * slots - head_start(member)
        lines = lax.broadcasted_iota(jnp.int32, (heads_width, 1), 0)
        return [jnp.where(lines >= spare * HEAD, whole, jnp.zeros_like(whole))]

    def head_columns(weight):
        return [
            lax.dynamic_slice_in_dim(weight, third * width + start, heads_width, 1)
            for third in range(3)
        ]

    if fast:
        hid_part = hid // replicas
        own_attn = jnp.concatenate(head_columns(attn_weight[0]), axis=1)
        attn_half = own_attn.shape[1] // 2
        own_in = jnp.concatenate(
            [
                lax.dynamic_slice_in_dim(
                    fc_in_weight[0], block * hid + member * hid_part, hid_part, 1
                )
                for block in range(replicas)
            ],
            axis=1,
        )
        own_out = lax.dynamic_slice_in_dim(fc_out_weight[0], member * hid_part, hid_part, 0)

        def spread(own_0, own_1):
            got = cross(pick(own_1, own_0))
            return pick(own_0, got), pick(got, own_1)

        def full(piece):
            mine = lax.all_gather(piece, "seq", axis=0, tiled=True)
            other = cross(mine)
            return pick(mine, other), pick(other, mine)

        attn_pieces = spread(own_attn[:, :attn_half], own_attn[:, attn_half:])
        fc_pieces = spread(own_in, own_out)
        own_proj = lax.dynamic_slice_in_dim(proj_weight[0], member * step, slab, 0)

        def weights_whole():
            attn_0 = jnp.concatenate(full(attn_pieces[0]), axis=1)
            proj = lax.all_gather(own_proj, "seq", axis=0, tiled=True)
            proj = gather(proj, 2 * slab)
            other = cross(proj)
            fc_0 = full(fc_pieces[0])
            attn_1 = jnp.concatenate(full(attn_pieces[1]), axis=1)
            fc_1 = full(fc_pieces[1])
            return (attn_0, pick(proj, other), *fc_0), (attn_1, pick(other, proj), *fc_1)

        def hid_of(vector):
            return lax.dynamic_slice_in_dim(
                vector.reshape(replicas, replicas, hid_part), member, 1, 1
            ).reshape(hid)

        def hid_into(vector):
            zeros = jnp.zeros((replicas, replicas, hid_part), F32)
            return lax.dynamic_update_slice_in_dim(
                zeros, vector.reshape(replicas, 1, hid_part), member, 1
            ).reshape(hidden)

    else:

        def both(value):
            other = cross(value)
            return pick(value, other), pick(other, value)

        def weights_of(layer):
            def whole(weight):
                return lax.all_gather(both(weight[0])[layer], row_axes, axis=0, tiled=True)

            w_attn = jnp.concatenate(head_columns(whole(attn_weight)), axis=1)
            w_proj = whole(proj_weight)
            w_in = lax.dynamic_slice_in_dim(whole(fc_in_weight), member * hid, hid, 1)
            w_out = lax.dynamic_slice_in_dim(whole(fc_out_weight), member * hid, hid, 0)
            return w_attn, w_proj, w_in, w_out

        def weights_whole():
            return weights_of(0), weights_of(1)

        def hid_of(vector):
            return lax.dynamic_slice_in_dim(vector, member * hid, hid, 0)

        def hid_into(vector):
            return lax.dynamic_update_slice_in_dim(
                jnp.zeros((hidden,), F32), vector, member * hid, 0
            )

    def heads_into(vector):
        return lax.dynamic_update_slice_in_dim(jnp.zeros((width,), F32), vector, start, 0)

    block_0, block_1 = boundary[0, 0, 0], boundary[0, 1, 0]
    kept = pick(block_0, block_1)
    got = cross(pick(block_1, block_0))
    source = to_team(pick(kept, got))
    cotangent = pick(got, kept)
    vectors = jnp.concatenate([norm_gains[0].ravel(), vector_bias[0].ravel(), fc_in_bias[0]])
    other_vectors = cross(vectors)
    vectors = (pick(vectors, other_vectors), pick(other_vectors, vectors))

    ids = lax.dynamic_index_in_dim(segments, section, 0, keepdims=False)[0]
    swapped = [
        (flat(p, z * sub + k), flat(z, p * sub + k))
        for p in range(replicas)
        for z in range(replicas)
        for k in range(sub)
    ]
    ids = lax.ppermute(ids, chip_axes, swapped).reshape(2, team, n)
    places, names = [], []
    for chunk, order in enumerate((order_a, order_b)):
        for index in order:
            places.append(chunk * half + index * n + jnp.arange(n, dtype=jnp.int32))
            names.append(lax.dynamic_index_in_dim(ids[chunk], index, 0, keepdims=False))
    places, names = jnp.concatenate(places), jnp.concatenate(names)
    allowed = (names[:, None] == names[None, :]) & (places[:, None] <= places[None, :])
    bias = jnp.where(allowed, 0.0, MASKED).astype(F32)

    def parameters(layer):
        vector = vectors[layer]
        gains = vector[: 2 * width].reshape(2, width)
        biases = vector[2 * width : 8 * width].reshape(6, width)
        hid_bias = hid_of(vector[8 * width :])
        query_bias = lax.dynamic_slice_in_dim(biases[1], start, heads_width, 0)
        value_bias = lax.dynamic_slice_in_dim(biases[2], start, heads_width, 0)
        mixed_bias = jnp.concatenate([query_bias, jnp.zeros_like(query_bias), value_bias])
        return gains, biases, hid_bias, mixed_bias

    def forward(layer, value, weights):
        w_attn, w_proj, w_in, w_out = weights
        gains, biases, hid_bias, mixed_bias = parameters(layer)
        normed = (norm_stats(value)[0] * gains[0] + biases[0]).astype(BF)
        normed = gather(normed, n)
        mixed = (dot(w_attn, normed, (0, 1)) + mixed_bias[:, None]).astype(BF)
        attended, lse = attend(mixed, bias, slots, fast)
        attended = heads_to_tokens(attended)
        middle = value + dot(attended, w_proj, (0, 0)) + biases[3]
        normed_two = (norm_stats(middle)[0] * gains[1] + biases[4]).astype(BF)
        normed_two = gather(normed_two, n)
        activated, slope = gelu_pair(dot(normed_two, w_in, (1, 0)) + hid_bias)
        activated, slope = activated.astype(BF), slope.astype(BF)
        out = middle + scatter(dot(activated, w_out, (1, 0)).astype(BF)) + biases[5]
        return out, (value, normed, mixed, lse, attended, middle, normed_two, activated, slope)

    ones = lax.optimization_barrier(jnp.ones((16, length), BF))

    def backward(layer, grad_out, kept, weights, waiting):
        value, normed, mixed, lse, attended, middle, normed_two, activated, slope = kept
        w_attn, w_proj, w_in, w_out = weights
        gains = parameters(layer)[0]
        grad_low = grad_out.astype(BF)
        low_sum = jnp.sum(grad_low.astype(F32), axis=0)
        grad_low = tie(gather(grad_low, n), waiting)
        grad_pre = (dot(grad_low, w_out, (1, 1)) * slope).astype(BF)
        grad_two = scatter(dot(grad_pre, w_in, (1, 1)).astype(BF))
        fc_pair = split_pair(dot(normed_two, grad_pre, (0, 0)), dot(activated, grad_low, (0, 0)))
        grad_two = tie(grad_two, fc_pair)
        hid_sum = dot(ones, grad_pre, (1, 0))[0]
        grad_norm, gain_two, shift_two = norm_back(grad_two, middle, gains[1])
        grad_middle = grad_out + grad_norm
        grad_branch = grad_middle.astype(BF)
        branch_sum = jnp.sum(grad_branch.astype(F32), axis=0)
        grad_attended = dot(w_proj, grad_branch, (1, 1)).astype(BF)
        grad_attended = tokens_to_heads(grad_attended)
        fc_total = join_pair(fc_pair)
        most = width // 2
        proj_pair = split_pair(
            dot(attended, grad_branch[:, :most], (1, 0)),
            dot(attended, grad_branch[:, most:], (1, 0)),
        )
        grad_attended = tie(grad_attended, fc_total, proj_pair)
        grad_q, grad_k, grad_v = attend_back(mixed, grad_attended, bias, lse, slots, fast)
        grad_mixed = jnp.concatenate([grad_q, grad_k, grad_v])
        grad_one = scatter(dot(grad_mixed, w_attn, (0, 1)).astype(BF))
        proj_total = join_pair(proj_pair)
        most = grad_mixed.shape[0] // 2
        attn_pair = split_pair(
            dot(normed, grad_mixed[:most], (0, 1)), dot(normed, grad_mixed[most:], (0, 1))
        )
        grad_one = tie(grad_one, attn_pair, proj_total)
        query_sum = jnp.sum(grad_q.astype(F32), axis=1)
        value_sum = jnp.sum(grad_v.astype(F32), axis=1)
        grad_norm, gain_one, shift_one = norm_back(grad_one, value, gains[0])
        grad_in = grad_middle + grad_norm
        small = jnp.concatenate(
            [
                gain_one,
                gain_two,
                shift_one,
                heads_into(query_sum),
                heads_into(value_sum),
                branch_sum,
                shift_two,
                low_sum,
                hid_into(hid_sum),
            ]
        )
        return grad_in, small, fc_total, proj_total, join_pair(attn_pair)

    def split_pair(part_0, part_1):
        if not fast:
            return part_0.astype(BF), part_1.astype(BF)
        return pick(part_0, part_1), cross(pick(part_1, part_0).astype(BF))

    def join_pair(pair):
        if not fast:
            return pair
        return (pair[0] + pair[1]).astype(BF)

    if fast:

        def collect(layer, total, at):
            mine = lax.psum_scatter(total, "seq", scatter_dimension=0, tiled=True)
            mine = gather(mine, at)
            return mine, cross(mine, [(1 - layer, layer)])

        def finish(kernel, pairs, shape):
            (mine_0, other_0), (mine_1, other_1) = pairs
            left, right = pick(mine_0, other_1), pick(other_0, mine_1)
            out = jax.ShapeDtypeStruct(shape, F32)
            return kernel_call(kernel, member, [left, right], [out])[0]

        def finish_fc(pairs):
            (mine_0, other_0), (mine_1, other_1) = pairs
            left, right = pick(mine_0, other_1), pick(other_0, mine_1)
            w_in = kernel_call(
                partial(finish_in_kernel, cut),
                member,
                [left],
                [jax.ShapeDtypeStruct((rows, hidden), F32)],
            )[0]
            w_out = kernel_call(
                partial(finish_out_kernel, cut),
                member,
                [right],
                [jax.ShapeDtypeStruct((hid, width), F32)],
            )[0]
            return w_in, w_out

        def reduce_small(small):
            total = pick(small[0], small[1]) + cross(pick(small[1], small[0]))
            total = total.reshape(-1, 128)
            for axis, pairs in (
                ("replica", SIDE),
                ("replica", ACROSS),
                ("seq", SIDE),
                ("seq", CORNER),
            ):
                total = total + lax.ppermute(total, axis, pairs)
            return total.reshape(-1)

    values = source.astype(F32)
    weights = weights_whole()
    passed, kept_0 = forward(0, values, weights[0])
    out, kept_1 = forward(1, passed.astype(BF).astype(F32), weights[1])
    cotangent = to_team(tie(cotangent, kept_0[1])).astype(F32)
    grad, small_1, fc_1, proj_1, attn_1 = backward(1, cotangent, kept_1, weights[1], ())
    grad = grad.astype(BF).astype(F32)
    grad, small_0, fc_0, proj_0, attn_0 = backward(0, grad, kept_0, weights[0], (attn_1,))
    out = from_team(out.astype(BF))
    grad = from_team(grad.astype(BF))
    got_out, got_grad = cross(out, [(0, 1)]), cross(grad, [(1, 0)])
    edge = jnp.stack([pick(grad, got_out), pick(got_grad, out)]).astype(F32)
    edge = edge.reshape(1, 2, 1, local, width)
    if fast:
        fc = [collect(layer, total, cut) for layer, total in enumerate((fc_0, fc_1))]
        attn = [collect(layer, total, cut) for layer, total in enumerate((attn_0, attn_1))]
        proj_cut = (slab // 32) * 16
        proj = [
            collect(layer, scatter(total).astype(BF), proj_cut)
            for layer, total in enumerate((proj_0, proj_1))
        ]
        in_sum, out_sum = finish_fc(fc)
        proj_sum = finish(partial(finish_proj_kernel, step, slab, proj_cut), proj, (rows, width))
        attn_sum = finish(partial(finish_attn_kernel, slots, cut), attn, (rows, 3 * width))
        small = reduce_small((small_0, small_1))
    else:

        def summed(make, after):
            parts = [tie(make(layer), after) for layer in range(2)]
            mine = pick(parts[0], parts[1]) + cross(pick(parts[1], parts[0]))
            mine = lax.psum_scatter(mine, row_axes, scatter_dimension=0, tiled=True)
            return lax.psum(mine.astype(F32), ("replica",))

        def attn_whole(layer):
            value = jnp.concatenate((attn_0, attn_1)[layer], axis=1)
            zeros = jnp.zeros((width, width), BF)
            parts = [value[:, i * heads_width : (i + 1) * heads_width] for i in range(3)]
            return jnp.concatenate(
                [lax.dynamic_update_slice_in_dim(zeros, x, start, 1) for x in parts], axis=1
            )

        def proj_whole(layer):
            return jnp.concatenate((proj_0, proj_1)[layer], axis=1)

        def in_whole(layer):
            zeros = jnp.zeros((width, hidden), BF)
            part = (fc_0, fc_1)[layer][0]
            return lax.dynamic_update_slice_in_dim(zeros, part, member * hid, 1)

        def out_whole(layer):
            zeros = jnp.zeros((hidden, width), BF)
            part = (fc_0, fc_1)[layer][1]
            return lax.dynamic_update_slice_in_dim(zeros, part, member * hid, 0)

        attn_sum = summed(attn_whole, edge)
        proj_sum = summed(proj_whole, attn_sum)
        in_sum = summed(in_whole, proj_sum)
        out_sum = summed(out_whole, in_sum)
        small = pick(small_0, small_1) + cross(pick(small_1, small_0))
        small = lax.psum(small, chip_axes)
    return (
        edge,
        attn_sum[None],
        proj_sum[None],
        in_sum[None],
        out_sum[None],
        small[: 2 * width].reshape(1, 2, width),
        small[2 * width : 8 * width].reshape(1, 6, width),
        small[8 * width :][None],
    )


def solution(mesh):
    sections, replicas, shards = (mesh.shape[name] for name in ("section", "replica", "shard"))
    split = Mesh(
        mesh.devices.reshape(sections, replicas, replicas, shards // replicas),
        ("section", "replica", "seq", "sub"),
    )
    rows = ("seq", "sub")
    return jax.shard_map(
        partial(body, replicas, shards),
        mesh=split,
        in_specs=(
            P("section", None, "replica", rows, None),
            P(None, "replica", None),
            P("section", rows, None),
            P("section", rows, None),
            P("section", rows, None),
            P("section", rows, None),
            P("section", None, None),
            P("section", None, None),
            P("section", None),
        ),
        out_specs=(
            P("section", None, "replica", rows, None),
            P("section", rows, None),
            P("section", rows, None),
            P("section", rows, None),
            P("section", rows, None),
            P("section", None, None),
            P("section", None, None),
            P("section", None),
        ),
        check_vma=False,
    )
```

time: 5430 us -> 1540 us (0.28)
  blocking collectives: 2570 us -> 0 us
  waiting for transfers between devices: 1700 us -> 469 us
  matrix products: 675 us -> 210 us
  starting transfers between devices: 19 us -> 275 us
  Pallas kernels: 0 us -> 92.4 us
    unnamed x2 -> x0, blocking collectives: 2470 us -> none
    all_gather x26 -> x5, waiting for transfers between devices: 1560 us -> 44.9 us  [the longest x1 44.9 us: weights_whole(): proj = lax.all_gather(own_proj, 'seq', axis=0, tiled=True)]
    dot_general x49 -> x30, matrix products: 675 us -> 210 us  [dot(): lax.dot_general(left, right, ((contract[:1], contract[1:]), ((), ())), pr...]
    ppermute x4 -> x133, waiting for transfers between devices: 7.28 us -> 424 us  [the longest x46 189 us: across(): return lax.ppermute(value, 'replica', ACROSS)]
    ppermute x4 -> x133, starting transfers between devices: 8.76 us -> 274 us  [the longest x46 117 us: across(): return lax.ppermute(value, 'replica', ACROSS)]
    psum x1 -> x0, waiting for transfers between devices: 102 us -> none  [body(): lax.psum((gain_total, bias_total, hid_total), ('replica', 'shard'))]
    all_gather x6 -> x0, blocking collectives: 93.2 us -> none  [the longest x3 46.6 us: attend_back(): lax.all_gather(logsum, 'shard', axis=2, tiled=True)]
    pallas_call x0 -> x12, Pallas kernels: none -> 92.4 us  [the longest x2 39.7 us: attend_back(): pl.pallas_call(partial(attend_back_kernel, grouped), grid=(slots,), in_sp...]
  transfers between devices with their start and end apart: 36 -> 144, of which waited for: 23 -> 54; matrix products, arithmetic and copies ran while one was open for 64% -> 37% of each run, Pallas kernels for 0% -> 6%
where the time goes in v1:
time: 1540 us; the launch traced here: 1520 us
  waiting for transfers between devices  469 us (30%)
  starting transfers between devices  275 us (18%)
  local copies, waits for them, and re-layouts  266 us (17%)
  matrix products  210 us (14%)
  other arithmetic  195 us (13%)
  Pallas kernels  92.4 us (6%)
  between operations  16.9 us (1%)
    dot_general x30, matrix products, dot(): lax.dot_general(left, right, ((contract[:1], contract[1:]), ((), ())), pr...  210 us
    ppermute x46, waiting for transfers between devices, across(): return lax.ppermute(value, 'replica', ACROSS)  189 us
    ppermute x46, waiting for transfers between devices, side(): return lax.ppermute(value, 'replica', SIDE)  175 us
    ppermute x46, starting transfers between devices, across(): return lax.ppermute(value, 'replica', ACROSS)  117 us
    ppermute x24, starting transfers between devices, cross(): return lax.ppermute(value, 'section', pairs)  84.8 us
    unnamed x437, local copies, waits for them, and re-layouts  84.4 us
    ppermute x9, local copies, waits for them, and re-layouts, cross(): return lax.ppermute(value, 'section', pairs)  47.9 us
    all_gather x1, waiting for transfers between devices, weights_whole(): proj = lax.all_gather(own_proj, 'seq', axis=0, tiled=True)  44.9 us
  transfers between devices with their start and end apart: 144, of which 54 were waited for; matrix products, arithmetic and copies ran while one was open for 37% of the time, Pallas kernels for 6%

profile of v1, /device:TPU:1, one launch (start us, length us, event | category | flops | bytes accessed | tf_op | source)
XLA Modules:
  0.0 1524.5 jit_solution(6553055186505079926)
XLA Ops:
  37.6 6.7 collective-permute-start.2
  44.3 44.9 %all-gather.15.cloned.1.call-done = bf16[1,448,1600]{2,1,0:T(8,128)(2,1)} async-done(((bf16[1,112,1600]{2,1,0:T(8,128)(2,1)}), bf16[1,448,1600]{2,1,0:T(8,128)(2,1)}) %all-gather.15.cloned.1.call-update) | async-done | bytes 1433616 | tf_op jit(solution)/shard_map/all_gather | solution.py:525
  94.1 16.7 %collective-permute-done.16 = bf16[224,1600]{1,0:T(8,128)(2,1)S(1)} collective-permute-done((bf16[224,1600]{1,0:T(8,128)(2,1)S(1)}, bf16[224,1600]{1,0:T(8,128)(2,1)S(1)}, u32[]{:S(2)}, u32[]{:S(2)}) %collective-permute-start.16) | collective-permute-done | bytes 716832 | tf_op jit(solution)/shard_map/ppermute | solution.py:366
  120.9 10.1 collective-permute-start.19
  132.9 18.5 %collective-permute-done.17 = bf16[448,1600]{1,0:T(8,128)(2,1)} collective-permute-done((bf16[448,1600]{1,0:T(8,128)(2,1)}, bf16[448,1600]{1,0:T(8,128)(2,1)}, u32[]{:S(2)}, u32[]{:S(2)}) %collective-permute-start.17) | collective-permute-done | bytes 1433632 | tf_op jit(solution)/shard_map/ppermute | solution.py:363
  162.7 9.6 copy.146
  198.4 13.1 collective-permute-done.5
  225.1 8.1 add_convert_fusion.7.q_ref.k_ref.v_ref
  233.2 16.6 %shard_map.152 = (bf16[448,256]{1,0:T(8,128)(2,1)S(1)}, bf16[448,256]{1,0:T(8,128)(2,1)S(1)}, bf16[448,256]{1,0:T(8,128)(2,1)S(1)}, bf16[448,256]{1,0:T(8,128)(2,1)S(1)}, f32[7,1,1024]{2,1,0:T(1,128)S(1)}) custom-call(bf16[1344,1024]{1,0:T(8,128)(2,1)S(1)} %add_convert_fusion.7.q_ref.k_ref.v_ref, bf16[1344,1024]{1,0:T(8,128)(2,1)S(1)} %add_convert_fusion.7.q_ref.k_ref.v_ref, ...), custom_call_target="tpu_custom_call" | custom-call | flops 1409286144 | bytes 7864320 | tf_op jit(solution)/shard_map/pallas_call | solution.py:126
  264.9 9.8 copy.147
  283.1 9.6 collective-permute-done.21
  298.0 14.7 collective-permute-done.22
  317.6 10.8 fusion.12
  328.5 8.3 convolution_convert_fusion.5
  346.4 9.3 collective-permute-done.27
  357.0 17.6 %collective-permute-done.9 = bf16[128,1600]{0,1:T(8,128)(2,1)S(1)} collective-permute-done((bf16[128,1600]{0,1:T(8,128)(2,1)S(1)}, bf16[128,1600]{0,1:T(8,128)(2,1)S(1)}, u32[]{:S(2)}, u32[]{:S(2)}) %collective-permute-start.9) | collective-permute-done | bytes 409632 | tf_op jit(solution)/shard_map/ppermute | solution.py:395
  375.6 62.7 %collective-permute-start.39 = (bf16[128,1600]{0,1:T(8,128)(2,1)S(1)}, bf16[128,1600]{0,1:T(8,128)(2,1)S(1)}, u32[]{:S(2)}, u32[]{:S(2)}) collective-permute-start(bf16[128,1600]{0,1:T(8,128)(2,1)S(1)} %get-tuple-element.121), channel_id=1, source_target_pairs={{0,8},{8,0},{4,12},{12,4},{1,9},{9,1},{5,13},{13,5},{2,10},{10,2},... | collective-permute-start | bytes 1228808 | tf_op jit(solution)/shard_map/ppermute | solution.py:366
  449.9 13.5 collective-permute-start.31
  489.2 16.1 %collective-permute-done.33 = bf16[256,1600]{0,1:T(8,128)(2,1)S(1)} collective-permute-done((bf16[256,1600]{0,1:T(8,128)(2,1)S(1)}, bf16[256,1600]{0,1:T(8,128)(2,1)S(1)}, u32[]{:S(2)}, u32[]{:S(2)}) %collective-permute-start.33) | collective-permute-done | bytes 819232 | tf_op jit(solution)/shard_map/ppermute | solution.py:363
  507.6 8.1 add_convert_fusion.6.q_ref.k_ref.v_ref
  515.7 16.6 %shard_map.154 = (bf16[448,256]{1,0:T(8,128)(2,1)S(1)}, bf16[448,256]{1,0:T(8,128)(2,1)S(1)}, bf16[448,256]{1,0:T(8,128)(2,1)S(1)}, bf16[448,256]{1,0:T(8,128)(2,1)S(1)}, f32[7,1,1024]{2,1,0:T(1,128)S(1)}) custom-call(bf16[1344,1024]{1,0:T(8,128)(2,1)S(1)} %add_convert_fusion.6.q_ref.k_ref.v_ref, bf16[1344,1024]{1,0:T(8,128)(2,1)S(1)} %add_convert_fusion.6.q_ref.k_ref.v_ref, ...), custom_call_target="tpu_custom_call" | custom-call | flops 1409286144 | bytes 7864320 | tf_op jit(solution)/shard_map/pallas_call | solution.py:126
  561.5 11.7 collective-permute-done.42
  578.6 11.3 collective-permute-done.47
  590.0 9.4 fusion.13
  599.5 9.4 multiply_convert_fusion.2
  610.6 8.7 fusion.119
  619.3 15.9 %select_convert_fusion.1 = (bf16[1600,1600]{1,0:T(8,128)(2,1)}, f32[1600,1600]{1,0:T(8,128)}) fusion(f32[1600,1600]{1,0:T(8,128)} %fusion.119, pred[]{:T(512)S(6)} %eq.21, bf16[1024,1600]{0,1:T(8,128)(2,1)} %constant_dynamic-update-slice_fusion.26, f32[1024,1600]{0,1:T(8,128)} %copy-done.177, f32[1600]{0:T(1024)S(1)} %add.599), kind=kOutput, calls=%fused_computation.3 | convolution fusion | flops 5261824000 | bytes 35436800 | tf_op jit(solution)/shard_map/dot_general | solution.py:23
  635.2 10.1 collective-permute-start.52
  645.4 10.2 convolution_convert_fusion.3
  659.5 17.5 %collective-permute-done.48 = bf16[256,1600]{0,1:T(8,128)(2,1)S(1)} collective-permute-done((bf16[256,1600]{0,1:T(8,128)(2,1)S(1)}, bf16[256,1600]{0,1:T(8,128)(2,1)S(1)}, u32[]{:S(2)}, u32[]{:S(2)}) %collective-permute-start.48) | collective-permute-done | bytes 819232 | tf_op jit(solution)/shard_map/ppermute | solution.py:363
  679.7 8.5 collective-permute-done.49
  690.4 8.3 collective-permute-done.51
  701.2 6.9 add_convert_fusion.1
  720.7 5.7 copy.156
  729.3 11.9 convolution_convert_fusion.4
  761.1 6.5 add_convert_fusion.5
  784.6 19.3 %shard_map.157 = (bf16[448,1024]{1,0:T(8,128)(2,1)S(1)}, bf16[448,1024]{1,0:T(8,128)(2,1)S(1)}, bf16[448,1024]{1,0:T(8,128)(2,1)S(1)}) custom-call(bf16[1344,1024]{1,0:T(8,128)(2,1)S(1)} %copy-done.31, bf16[1344,1024]{1,0:T(8,128)(2,1)S(1)} %copy-done.31, bf16[1344,1024]{1,0:T(8,128)(2,1)S(1)} %copy-done.31, f32[1024,1024]{1,0:T(8,128)S(1)} %copy-done.6, ...), custom_call_target="tpu_custom_call" | custom-call | flops 3758096384 | bytes 10616832 | tf_op jit(solution)/shard_map/pallas_call | solution.py:150
  818.0 7.7 convolution_convert_fusion.2
  829.3 8.6 collective-permute-done.109
  842.2 14.6 collective-permute-done.111
  875.5 8.8 collective-permute-done.58
  887.9 6.9 collective-permute-done.60
  929.4 12.1 collective-permute-done.63
  945.3 13.7 collective-permute-done.65
  960.1 13.1 multiply_convert_fusion
  973.3 9.2 convolution_convert_fusion.1
  987.4 6.2 fusion.120
  993.6 18.0 %select_convert_fusion = (bf16[1600,1600]{1,0:T(8,128)(2,1)}, f32[1600,1600]{1,0:T(8,128)}) fusion(f32[1600,1600]{1,0:T(8,128)S(1)} %fusion.120, pred[]{:T(512)S(6)} %eq.21, bf16[1024,1600]{0,1:T(8,128)(2,1)} %constant_dynamic-update-slice_fusion.38, f32[1024,1600]{0,1:T(8,128)} %copy-done.176, f32[1600]{0:T(1024)S(1)} %copy-done.174), kind=kOutput, calls=%fused_computation.1 | convolution fusion | flops 5261824000 | bytes 35436800 | tf_op jit(solution)/shard_map/dot_general | solution.py:23
  1028.0 26.2 %collective-permute-done.94 = bf16[192,672]{1,0:T(8,128)(2,1)S(1)} collective-permute-done((bf16[192,672]{1,0:T(8,128)(2,1)S(1)}, bf16[192,672]{1,0:T(8,128)(2,1)S(1)}, u32[]{:S(2)}, u32[]{:S(2)}) %collective-permute-start.94) | collective-permute-done | bytes 258080 | tf_op jit(solution)/shard_map/ppermute | solution.py:366
  1060.3 7.3 collective-permute-done.95
  1091.5 9.3 add_convert_fusion
  1113.0 6.4 collective-permute-start.74
  1166.8 10.7 collective-permute-done.125
  1187.4 6.4 add_convert_fusion.4
  1199.9 20.3 %shard_map.159 = (bf16[448,1024]{1,0:T(8,128)(2,1)S(1)}, bf16[448,1024]{1,0:T(8,128)(2,1)S(1)}, bf16[448,1024]{1,0:T(8,128)(2,1)S(1)}) custom-call(bf16[1344,1024]{1,0:T(8,128)(2,1)S(1)} %copy-done.29, bf16[1344,1024]{1,0:T(8,128)(2,1)S(1)} %copy-done.29, bf16[1344,1024]{1,0:T(8,128)(2,1)S(1)} %copy-done.29, f32[1024,1024]{1,0:T(8,128)S(1)} %copy-done.7, ...), custom_call_target="tpu_custom_call" | custom-call | flops 3758096384 | bytes 10616832 | tf_op jit(solution)/shard_map/pallas_call | solution.py:150
  1251.6 10.2 collective-permute-done.100
  1268.7 8.3 collective-permute-done.102
  1276.9 8.6 collective-permute-done.101
  1303.9 5.7 collective-permute-start.128
  1326.9 10.1 collective-permute-done.118
  1345.5 33.6 %collective-permute-done.131 = f32[150,128]{1,0:T(8,128)S(1)} collective-permute-done((f32[150,128]{1,0:T(8,128)S(1)}, f32[150,128]{1,0:T(8,128)S(1)}, u32[]{:S(2)}, u32[]{:S(2)}) %collective-permute-start.131) | collective-permute-done | bytes 76832 | tf_op jit(solution)/shard_map/ppermute | solution.py:730
  1400.9 7.9 collective-permute-start.89
  1442.1 10.3 collective-permute-done.121
  1455.0 7.7 collective-permute-start.127
  (981 shorter events, 686.5 us)
Async XLA Ops:
  7.2 82.0 %all-gather.15.cloned.1.call-start = ((), (), s32[]{:S(2)}) async-start(), calls=%async_computation.16 | async-start | bytes 1863680 | tf_op jit(solution)/shard_map/all_gather | solution.py:525
  14.0 168.5 %all-gather.7.cloned.1.call-start = ((), (), s32[]{:S(2)}) async-start(), calls=%async_computation.6 | async-start | bytes 3072000 | tf_op jit(solution)/shard_map/all_gather | solution.py:515
  28.0 84.0 %collective-permute-start.25 = (bf16[400,1600]{1,0:T(8,128)(2,1)}, bf16[400,1600]{1,0:T(8,128)(2,1)}, u32[]{:S(2)}, u32[]{:S(2)}) collective-permute-start(bf16[400,1600]{1,0:T(8,128)(2,1)} %bitcast_select_fusion.1), channel_id=1, source_target_pairs={{0,16},{16,0},{1,17},{17,1},{2,18},{18,2},{3,19},{19,3},{4,20},{20... | collective-permute-start | bytes 3840008 | tf_op jit(solution)/shard_map/ppermute | solution.py:360
  34.5 227.1 %all-gather.9.cloned.1.call-start = ((), (), s32[]{:S(2)}) async-start(), calls=%async_computation.7 | async-start | bytes 6656000 | tf_op jit(solution)/shard_map/all_gather | solution.py:515
  36.9 54.6 %collective-permute-start.1 = (bf16[128,1600]{0,1:T(8,128)(2,1)S(1)}, bf16[128,1600]{0,1:T(8,128)(2,1)S(1)}, u32[]{:S(2)}, u32[]{:S(2)}) collective-permute-start(bf16[128,1600]{0,1:T(8,128)(2,1)S(1)} %get-tuple-element.214), channel_id=1, source_target_pairs={{0,0},{1,8},{2,4},{3,12},{4,1},{5,9},{6,5},{7,13},{8,2},{9,10},{10... | collective-permute-start | bytes 1228808 | tf_op jit(solution)/shard_map/ppermute | solution.py:394
  37.6 54.7 %collective-permute-start.2 = (bf16[128,1600]{0,1:T(8,128)(2,1)S(1)}, bf16[128,1600]{0,1:T(8,128)(2,1)}, u32[]{:S(2)}, u32[]{:S(2)}) collective-permute-start(bf16[128,1600]{0,1:T(8,128)(2,1)S(1)} %get-tuple-element.215), channel_id=1, source_target_pairs={{0,4},{1,12},{2,0},{3,8},{4,5},{5,13},{6,1},{7,9},{8,6},{9,14},{10... | collective-permute-start | bytes 1228808 | tf_op jit(solution)/shard_map/ppermute | solution.py:395
  112.0 39.4 %collective-permute-start.17 = (bf16[448,1600]{1,0:T(8,128)(2,1)}, bf16[448,1600]{1,0:T(8,128)(2,1)}, u32[]{:S(2)}, u32[]{:S(2)}) collective-permute-start(bf16[448,1600]{1,0:T(8,128)(2,1)} %pad_maximum_fusion.10), channel_id=1, source_target_pairs={{0,4},{4,0},{8,12},{12,8},{1,5},{5,1},{9,13},{13,9},{2,6},{6,2},{1... | collective-permute-start | bytes 4300808 | tf_op jit(solution)/shard_map/ppermute | solution.py:363
  115.8 329.8 %all-gather.11.cloned.1.call-start = ((), (), s32[]{:S(2)}) async-start(), calls=%async_computation.8 | async-start | bytes 3072000 | tf_op jit(solution)/shard_map/all_gather | solution.py:515
  120.9 40.6 %collective-permute-start.19 = (bf16[448,1600]{1,0:T(8,128)(2,1)S(1)}, bf16[448,1600]{1,0:T(8,128)(2,1)S(1)}, u32[]{:S(2)}, u32[]{:S(2)}) collective-permute-start(bf16[448,1600]{1,0:T(8,128)(2,1)S(1)} %pad_maximum_fusion.11), channel_id=1, source_target_pairs={{0,8},{8,0},{4,12},{12,4},{1,9},{9,1},{5,13},{13,5},{2,10},{10,2},... | collective-permute-start | bytes 4300808 | tf_op jit(solution)/shard_map/ppermute | solution.py:366
  172.4 92.5 %collective-permute-start.20 = (bf16[1792,1600]{0,1:T(8,128)(2,1)}, bf16[1792,1600]{0,1:T(8,128)(2,1)}, u32[]{:S(2)}, u32[]{:S(2)}) collective-permute-start(bf16[1792,1600]{0,1:T(8,128)(2,1)} %copy.146), channel_id=1, source_target_pairs={{0,16},{16,0},{1,17},{17,1},{2,18},{18,2},{3,19},{19,3},{4,20},{20... | collective-permute-start | bytes 17203208 | tf_op jit(solution)/shard_map/ppermute | solution.py:360
  186.9 29.5 %collective-permute-start.11 = (bf16[1600,672]{0,1:T(8,128)(2,1)}, bf16[1600,672]{0,1:T(8,128)(2,1)}, u32[]{:S(2)}, u32[]{:S(2)}) collective-permute-start(bf16[1600,672]{0,1:T(8,128)(2,1)} %copy.143), channel_id=1, source_target_pairs={{0,16},{16,0},{1,17},{17,1},{2,18},{18,2},{3,19},{19,3},{4,20},{20... | collective-permute-start | bytes 6451208 | tf_op jit(solution)/shard_map/ppermute | solution.py:360
  261.6 56.0 %collective-permute-start.26 = (bf16[1600,1600]{1,0:T(8,128)(2,1)}, bf16[1600,1600]{1,0:T(8,128)(2,1)}, u32[]{:S(2)}, u32[]{:S(2)}) collective-permute-start(bf16[1600,1600]{1,0:T(8,128)(2,1)} %all-gather.9.cloned.1.call-done), channel_id=1, source_target_pairs={{0,16},{16,0},{1,17},{17,1},{2,18},{18,2},{3,19},{19,3},{4,20},{20... | collective-permute-start | bytes 15360008 | tf_op jit(solution)/shard_map/ppermute | solution.py:360
  295.4 243.0 %all-gather.13.cloned.1.call-start = ((), (), s32[]{:S(2)}) async-start(), calls=%async_computation.9 | async-start | bytes 6656000 | tf_op jit(solution)/shard_map/all_gather | solution.py:515
  340.5 671.5 %reduce-scatter.13.cloned.1.call-start = ((), (), s32[]{:S(2)}) async-start(), calls=%async_computation.13 | async-start | bytes 1003520 | tf_op jit(solution)/shard_map/reduce_scatter | solution.py:694
  340.6 34.0 %collective-permute-start.9 = (bf16[128,1600]{0,1:T(8,128)(2,1)S(1)}, bf16[128,1600]{0,1:T(8,128)(2,1)S(1)}, u32[]{:S(2)}, u32[]{:S(2)}) collective-permute-start(bf16[128,1600]{0,1:T(8,128)(2,1)S(1)} %get-tuple-element.201), channel_id=1, source_target_pairs={{0,4},{1,12},{2,0},{3,8},{4,5},{5,13},{6,1},{7,9},{8,6},{9,14},{10... | collective-permute-start | bytes 1228808 | tf_op jit(solution)/shard_map/ppermute | solution.py:395
  341.4 33.2 %collective-permute-start.8 = (bf16[128,1600]{0,1:T(8,128)(2,1)S(1)}, bf16[128,1600]{0,1:T(8,128)(2,1)S(1)}, u32[]{:S(2)}, u32[]{:S(2)}) collective-permute-start(bf16[128,1600]{0,1:T(8,128)(2,1)S(1)} %get-tuple-element.202), channel_id=1, source_target_pairs={{0,0},{1,8},{2,4},{3,12},{4,1},{5,9},{6,5},{7,13},{8,2},{9,10},{10... | collective-permute-start | bytes 1228808 | tf_op jit(solution)/shard_map/ppermute | solution.py:394
  342.3 96.1 %collective-permute-start.29 = (bf16[256,1600]{0,1:T(8,128)(2,1)}, bf16[256,1600]{0,1:T(8,128)(2,1)S(1)}, u32[]{:S(2)}, u32[]{:S(2)}) collective-permute-start(bf16[256,1600]{0,1:T(8,128)(2,1)} %get-tuple-element.158), channel_id=1, source_target_pairs={{0,8},{8,0},{4,12},{12,4},{1,9},{9,1},{5,13},{13,5},{2,10},{10,2},... | collective-permute-start | bytes 2457608 | tf_op jit(solution)/shard_map/ppermute | solution.py:366
  356.9 81.5 %collective-permute-start.28 = (bf16[128,1600]{0,1:T(8,128)(2,1)S(1)}, bf16[128,1600]{0,1:T(8,128)(2,1)S(1)}, u32[]{:S(2)}, u32[]{:S(2)}) collective-permute-start(bf16[128,1600]{0,1:T(8,128)(2,1)S(1)} %add_convert_fusion.23), channel_id=1, source_target_pairs={{0,8},{8,0},{4,12},{12,4},{1,9},{9,1},{5,13},{13,5},{2,10},{10,2},... | collective-permute-start | bytes 1228808 | tf_op jit(solution)/shard_map/ppermute | solution.py:366
  375.6 68.8 %collective-permute-start.39 = (bf16[128,1600]{0,1:T(8,128)(2,1)S(1)}, bf16[128,1600]{0,1:T(8,128)(2,1)S(1)}, u32[]{:S(2)}, u32[]{:S(2)}) collective-permute-start(bf16[128,1600]{0,1:T(8,128)(2,1)S(1)} %get-tuple-element.121), channel_id=1, source_target_pairs={{0,8},{8,0},{4,12},{12,4},{1,9},{9,1},{5,13},{13,5},{2,10},{10,2},... | collective-permute-start | bytes 1228808 | tf_op jit(solution)/shard_map/ppermute | solution.py:366
  538.5 51.5 %collective-permute-start.43 = (bf16[1600,1600]{1,0:T(8,128)(2,1)}, bf16[1600,1600]{1,0:T(8,128)(2,1)}, u32[]{:S(2)}, u32[]{:S(2)}) collective-permute-start(bf16[1600,1600]{1,0:T(8,128)(2,1)} %all-gather.13.cloned.1.call-done), channel_id=1, source_target_pairs={{0,16},{16,0},{1,17},{17,1},{2,18},{18,2},{3,19},{19,3},{4,20},{20... | collective-permute-start | bytes 15360008 | tf_op jit(solution)/shard_map/ppermute | solution.py:360
  635.2 66.0 %collective-permute-start.52 = (bf16[1600,1600]{1,0:T(8,128)(2,1)}, bf16[1600,1600]{1,0:T(8,128)(2,1)}, u32[]{:S(2)}, u32[]{:S(2)}) collective-permute-start(bf16[1600,1600]{1,0:T(8,128)(2,1)} %get-tuple-element.256), channel_id=1, source_target_pairs={{0,16},{16,0},{1,17},{17,1},{2,18},{18,2},{3,19},{19,3},{4,20},{20... | collective-permute-start | bytes 15360008 | tf_op jit(solution)/shard_map/ppermute | solution.py:360
  742.5 97.7 %collective-permute-start.82 = (bf16[256,1600]{0,1:T(8,128)(2,1)}, bf16[256,1600]{0,1:T(8,128)(2,1)}, u32[]{:S(2)}, u32[]{:S(2)}) collective-permute-start(bf16[256,1600]{0,1:T(8,128)(2,1)} %get-tuple-element.137), channel_id=1, source_target_pairs={{0,4},{4,0},{8,12},{12,8},{1,5},{5,1},{9,13},{13,9},{2,6},{6,2},{1... | collective-permute-start | bytes 2457608 | tf_op jit(solution)/shard_map/ppermute | solution.py:363
  743.5 128.7 %collective-permute-start.84 = (bf16[256,1600]{0,1:T(8,128)(2,1)}, bf16[256,1600]{0,1:T(8,128)(2,1)}, u32[]{:S(2)}, u32[]{:S(2)}) collective-permute-start(bf16[256,1600]{0,1:T(8,128)(2,1)} %get-tuple-element.138), channel_id=1, source_target_pairs={{0,8},{8,0},{4,12},{12,4},{1,9},{9,1},{5,13},{13,5},{2,10},{10,2},... | collective-permute-start | bytes 2457608 | tf_op jit(solution)/shard_map/ppermute | solution.py:366
  776.2 49.6 %collective-permute-start.108 = (bf16[448,800]{1,0:T(8,128)(2,1)}, bf16[448,800]{1,0:T(8,128)(2,1)}, u32[]{:S(2)}, u32[]{:S(2)}) collective-permute-start(bf16[448,800]{1,0:T(8,128)(2,1)} %get-tuple-element.161), channel_id=1, source_target_pairs={{0,4},{4,0},{8,12},{12,8},{1,5},{5,1},{9,13},{13,9},{2,6},{6,2},{1... | collective-permute-start | bytes 2150408 | tf_op jit(solution)/shard_map/ppermute | solution.py:363
  776.9 51.7 %collective-permute-start.110 = (bf16[448,800]{1,0:T(8,128)(2,1)}, bf16[448,800]{1,0:T(8,128)(2,1)}, u32[]{:S(2)}, u32[]{:S(2)}) collective-permute-start(bf16[448,800]{1,0:T(8,128)(2,1)} %get-tuple-element.162), channel_id=1, source_target_pairs={{0,8},{8,0},{4,12},{12,4},{1,9},{9,1},{5,13},{13,5},{2,10},{10,2},... | collective-permute-start | bytes 2150408 | tf_op jit(solution)/shard_map/ppermute | solution.py:366
  816.4 45.9 %collective-permute-start.61 = (bf16[1600,672]{0,1:T(8,128)(2,1)}, bf16[1600,672]{0,1:T(8,128)(2,1)}, u32[]{:S(2)}, u32[]{:S(2)}) collective-permute-start(bf16[1600,672]{0,1:T(8,128)(2,1)} %copy.161), channel_id=1, source_target_pairs={{0,16},{16,0},{1,17},{17,1},{2,18},{18,2},{3,19},{19,3},{4,20},{20... | collective-permute-start | bytes 6451208 | tf_op jit(solution)/shard_map/ppermute | solution.py:360
  828.6 31.7 %collective-permute-start.57 = (bf16[256,1600]{0,1:T(8,128)(2,1)}, bf16[256,1600]{0,1:T(8,128)(2,1)S(1)}, u32[]{:S(2)}, u32[]{:S(2)}) collective-permute-start(bf16[256,1600]{0,1:T(8,128)(2,1)} %get-tuple-element.149), channel_id=1, source_target_pairs={{0,4},{4,0},{8,12},{12,8},{1,5},{5,1},{9,13},{13,9},{2,6},{6,2},{1... | collective-permute-start | bytes 2457608 | tf_op jit(solution)/shard_map/ppermute | solution.py:363
  842.1 30.1 %collective-permute-start.83 = (bf16[128,1600]{0,1:T(8,128)(2,1)}, bf16[128,1600]{0,1:T(8,128)(2,1)}, u32[]{:S(2)}, u32[]{:S(2)}) collective-permute-start(bf16[128,1600]{0,1:T(8,128)(2,1)} %add_convert_fusion.13), channel_id=1, source_target_pairs={{0,8},{8,0},{4,12},{12,4},{1,9},{9,1},{5,13},{13,5},{2,10},{10,2},... | collective-permute-start | bytes 1228808 | tf_op jit(solution)/shard_map/ppermute | solution.py:366
  860.3 163.2 %reduce-scatter.9.cloned.1.call-start = ((), (), s32[]{:S(2)}) async-start(), calls=%async_computation.11 | async-start | bytes 3072000 | tf_op jit(solution)/shard_map/reduce_scatter | solution.py:694
  872.1 199.7 %reduce-scatter.17.cloned.1.call-start = ((), (), s32[]{:S(2)}) async-start(), calls=%async_computation.15 | async-start | bytes 6656000 | tf_op jit(solution)/shard_map/reduce_scatter | solution.py:694
  908.0 409.3 %reduce-scatter.15.cloned.1.call-start = ((), (), s32[]{:S(2)}) async-start(), calls=%async_computation.14 | async-start | bytes 6656000 | tf_op jit(solution)/shard_map/reduce_scatter | solution.py:694
  914.5 27.0 %collective-permute-start.63 = (bf16[256,1600]{0,1:T(8,128)(2,1)S(1)}, bf16[256,1600]{0,1:T(8,128)(2,1)}, u32[]{:S(2)}, u32[]{:S(2)}) collective-permute-start(bf16[256,1600]{0,1:T(8,128)(2,1)S(1)} %pad_maximum_fusion.36), channel_id=1, source_target_pairs={{0,4},{4,0},{8,12},{12,8},{1,5},{5,1},{9,13},{13,9},{2,6},{6,2},{1... | collective-permute-start | bytes 2457608 | tf_op jit(solution)/shard_map/ppermute | solution.py:363
  915.5 100.2 %collective-permute-start.86 = (bf16[128,1600]{0,1:T(8,128)(2,1)}, bf16[128,1600]{0,1:T(8,128)(2,1)}, u32[]{:S(2)}, u32[]{:S(2)}) collective-permute-start(bf16[128,1600]{0,1:T(8,128)(2,1)} %get-tuple-element.189), channel_id=1, source_target_pairs={{0,0},{8,1},{4,2},{12,3},{1,4},{9,5},{5,6},{13,7},{2,8},{10,9},{6,... | collective-permute-start | bytes 1228808 | tf_op jit(solution)/shard_map/ppermute | solution.py:400
  920.5 95.3 %collective-permute-start.87 = (bf16[128,1600]{0,1:T(8,128)(2,1)}, bf16[128,1600]{0,1:T(8,128)(2,1)}, u32[]{:S(2)}, u32[]{:S(2)}) collective-permute-start(bf16[128,1600]{0,1:T(8,128)(2,1)} %get-tuple-element.190), channel_id=1, source_target_pairs={{4,0},{12,1},{0,2},{8,3},{5,4},{13,5},{1,6},{9,7},{6,8},{14,9},{2,... | collective-permute-start | bytes 1228808 | tf_op jit(solution)/shard_map/ppermute | solution.py:403
  924.0 35.1 %collective-permute-start.65 = (bf16[256,1600]{0,1:T(8,128)(2,1)S(1)}, bf16[256,1600]{0,1:T(8,128)(2,1)S(1)}, u32[]{:S(2)}, u32[]{:S(2)}) collective-permute-start(bf16[256,1600]{0,1:T(8,128)(2,1)S(1)} %pad_maximum_fusion.37), channel_id=1, source_target_pairs={{0,8},{8,0},{4,12},{12,4},{1,9},{9,1},{5,13},{13,5},{2,10},{10,2},... | collective-permute-start | bytes 2457608 | tf_op jit(solution)/shard_map/ppermute | solution.py:366
  985.0 36.2 %collective-permute-start.66 = (bf16[256,1600]{0,1:T(8,128)(2,1)}, bf16[256,1600]{0,1:T(8,128)(2,1)}, u32[]{:S(2)}, u32[]{:S(2)}) collective-permute-start(bf16[256,1600]{0,1:T(8,128)(2,1)} %get-tuple-element.145), channel_id=1, source_target_pairs={{0,4},{4,0},{8,12},{12,8},{1,5},{5,1},{9,13},{13,9},{2,6},{6,2},{1... | collective-permute-start | bytes 2457608 | tf_op jit(solution)/shard_map/ppermute | solution.py:363
  1011.6 79.9 %collective-permute-start.70 = (bf16[1600,1600]{1,0:T(8,128)(2,1)}, bf16[1600,1600]{1,0:T(8,128)(2,1)}, u32[]{:S(2)}, u32[]{:S(2)}) collective-permute-start(bf16[1600,1600]{1,0:T(8,128)(2,1)} %get-tuple-element.262), channel_id=1, source_target_pairs={{0,16},{16,0},{1,17},{17,1},{2,18},{18,2},{3,19},{19,3},{4,20},{20... | collective-permute-start | bytes 15360008 | tf_op jit(solution)/shard_map/ppermute | solution.py:360
  1020.1 36.8 %collective-permute-start.68 = (bf16[256,1600]{0,1:T(8,128)(2,1)}, bf16[256,1600]{0,1:T(8,128)(2,1)}, u32[]{:S(2)}, u32[]{:S(2)}) collective-permute-start(bf16[256,1600]{0,1:T(8,128)(2,1)} %get-tuple-element.146), channel_id=1, source_target_pairs={{0,8},{8,0},{4,12},{12,4},{1,9},{9,1},{5,13},{13,5},{2,10},{10,2},... | collective-permute-start | bytes 2457608 | tf_op jit(solution)/shard_map/ppermute | solution.py:366
  1023.2 33.7 %collective-permute-start.67 = (bf16[128,1600]{0,1:T(8,128)(2,1)}, bf16[128,1600]{0,1:T(8,128)(2,1)}, u32[]{:S(2)}, u32[]{:S(2)}) collective-permute-start(bf16[128,1600]{0,1:T(8,128)(2,1)} %add_convert_fusion.17), channel_id=1, source_target_pairs={{0,8},{8,0},{4,12},{12,4},{1,9},{9,1},{5,13},{13,5},{2,10},{10,2},... | collective-permute-start | bytes 1228808 | tf_op jit(solution)/shard_map/ppermute | solution.py:366
  1024.5 29.6 %collective-permute-start.94 = (bf16[192,672]{1,0:T(8,128)(2,1)S(1)}, bf16[192,672]{1,0:T(8,128)(2,1)S(1)}, u32[]{:S(2)}, u32[]{:S(2)}) collective-permute-start(bf16[192,672]{1,0:T(8,128)(2,1)S(1)} %get-tuple-element.218), channel_id=1, source_target_pairs={{0,8},{8,0},{4,12},{12,4},{1,9},{9,1},{5,13},{13,5},{2,10},{10,2},... | collective-permute-start | bytes 774152 | tf_op jit(solution)/shard_map/ppermute | solution.py:366
  1027.2 110.3 %collective-permute-start.114 = (bf16[64,800]{1,0:T(8,128)(2,1)}, bf16[64,800]{1,0:T(8,128)(2,1)S(1)}, u32[]{:S(2)}, u32[]{:S(2)}) collective-permute-start(bf16[64,800]{1,0:T(8,128)(2,1)} %get-tuple-element.224), channel_id=1, source_target_pairs={{0,4},{4,0},{8,12},{12,8},{1,5},{5,1},{9,13},{13,9},{2,6},{6,2},{1... | collective-permute-start | bytes 307208 | tf_op jit(solution)/shard_map/ppermute | solution.py:363
  1085.2 43.6 %collective-permute-start.97 = (bf16[416,672]{1,0:T(8,128)(2,1)}, bf16[416,672]{1,0:T(8,128)(2,1)}, u32[]{:S(2)}, u32[]{:S(2)}) collective-permute-start(bf16[416,672]{1,0:T(8,128)(2,1)} %pad_maximum_fusion.43), channel_id=1, source_target_pairs={{0,8},{8,0},{4,12},{12,4},{1,9},{9,1},{5,13},{13,5},{2,10},{10,2},... | collective-permute-start | bytes 1677320 | tf_op jit(solution)/shard_map/ppermute | solution.py:366
  1088.2 31.2 %collective-permute-start.123 = (bf16[384,1600]{0,1:T(8,128)(2,1)}, bf16[384,1600]{0,1:T(8,128)(2,1)}, u32[]{:S(2)}, u32[]{:S(2)}) collective-permute-start(bf16[384,1600]{0,1:T(8,128)(2,1)} %copy.186), channel_id=1, source_target_pairs={{0,4},{4,0},{8,12},{12,8},{1,5},{5,1},{9,13},{13,9},{2,6},{6,2},{1... | collective-permute-start | bytes 3686408 | tf_op jit(solution)/shard_map/ppermute | solution.py:363
  1113.0 68.9 %collective-permute-start.74 = (bf16[1792,800]{0,1:T(8,128)(2,1)}, bf16[1792,800]{0,1:T(8,128)(2,1)}, u32[]{:S(2)}, u32[]{:S(2)}) collective-permute-start(bf16[1792,800]{0,1:T(8,128)(2,1)} %copy.168), channel_id=1, source_target_pairs={{0,16},{16,0},{1,17},{17,1},{2,18},{18,2},{3,19},{19,3},{4,20},{20... | collective-permute-start | bytes 8601608 | tf_op jit(solution)/shard_map/ppermute | solution.py:360
  1133.8 27.2 %collective-permute-start.98 = (bf16[1600,672]{0,1:T(8,128)(2,1)}, bf16[1600,672]{0,1:T(8,128)(2,1)}, u32[]{:S(2)}, u32[]{:S(2)}) collective-permute-start(bf16[1600,672]{0,1:T(8,128)(2,1)} %copy.180), channel_id=1, source_target_pairs={{0,16},{1,17},{2,18},{3,19},{4,20},{5,21},{6,22},{7,23},{8,24},{9,... | collective-permute-start | bytes 6451208 | tf_op jit(solution)/shard_map/ppermute | solution.py:360
  1136.2 261.8 %collective-permute-start.88 = (bf16[256,1600]{0,1:T(8,128)(2,1)}, bf16[256,1600]{0,1:T(8,128)(2,1)}, u32[]{:S(2)}, u32[]{:S(2)}) collective-permute-start(bf16[256,1600]{0,1:T(8,128)(2,1)} %pad_maximum_fusion.39), channel_id=1, source_target_pairs={{0,16},{1,17},{2,18},{3,19},{4,20},{5,21},{6,22},{7,23},{8,24},{9,... | collective-permute-start | bytes 2457608 | tf_op jit(solution)/shard_map/ppermute | solution.py:360
  1140.7 247.0 %reduce-scatter.7.cloned.1.call-start = ((), (), s32[]{:S(2)}) async-start(), calls=%async_computation.10 | async-start | bytes 3072000 | tf_op jit(solution)/shard_map/reduce_scatter | solution.py:694
  1146.5 31.0 %collective-permute-start.125 = (bf16[416,1600]{1,0:T(8,128)(2,1)}, bf16[416,1600]{1,0:T(8,128)(2,1)}, u32[]{:S(2)}, u32[]{:S(2)}) collective-permute-start(bf16[416,1600]{1,0:T(8,128)(2,1)} %pad_maximum_fusion.13), channel_id=1, source_target_pairs={{0,8},{8,0},{4,12},{12,4},{1,9},{9,1},{5,13},{13,5},{2,10},{10,2},... | collective-permute-start | bytes 3993608 | tf_op jit(solution)/shard_map/ppermute | solution.py:366
  1157.6 36.3 %collective-permute-start.71 = (bf16[448,256]{1,0:T(8,128)(2,1)}, bf16[448,256]{1,0:T(8,128)(2,1)S(1)}, u32[]{:S(2)}, u32[]{:S(2)}) collective-permute-start(bf16[448,256]{1,0:T(8,128)(2,1)} %get-tuple-element.73), channel_id=1, source_target_pairs={{0,4},{4,0},{8,12},{12,8},{1,5},{5,1},{9,13},{13,9},{2,6},{6,2},{1... | collective-permute-start | bytes 688136 | tf_op jit(solution)/shard_map/ppermute | solution.py:363
  1161.0 33.6 %collective-permute-start.72 = (bf16[448,256]{1,0:T(8,128)(2,1)S(1)}, bf16[448,256]{1,0:T(8,128)(2,1)S(1)}, u32[]{:S(2)}, u32[]{:S(2)}) collective-permute-start(bf16[448,256]{1,0:T(8,128)(2,1)S(1)} %get-tuple-element.74), channel_id=1, source_target_pairs={{0,8},{8,0},{4,12},{12,4},{1,9},{9,1},{5,13},{13,5},{2,10},{10,2},... | collective-permute-start | bytes 688136 | tf_op jit(solution)/shard_map/ppermute | solution.py:366
  1233.8 28.1 %collective-permute-start.100 = (bf16[448,800]{1,0:T(8,128)(2,1)}, bf16[448,800]{1,0:T(8,128)(2,1)}, u32[]{:S(2)}, u32[]{:S(2)}) collective-permute-start(bf16[448,800]{1,0:T(8,128)(2,1)} %get-tuple-element.165), channel_id=1, source_target_pairs={{0,4},{4,0},{8,12},{12,8},{1,5},{5,1},{9,13},{13,9},{2,6},{6,2},{1... | collective-permute-start | bytes 2150408 | tf_op jit(solution)/shard_map/ppermute | solution.py:363
  1234.1 30.3 %collective-permute-start.77 = (bf16[256,1600]{0,1:T(8,128)(2,1)}, bf16[256,1600]{0,1:T(8,128)(2,1)S(1)}, u32[]{:S(2)}, u32[]{:S(2)}) collective-permute-start(bf16[256,1600]{0,1:T(8,128)(2,1)} %get-tuple-element.142), channel_id=1, source_target_pairs={{0,8},{8,0},{4,12},{12,4},{1,9},{9,1},{5,13},{13,5},{2,10},{10,2},... | collective-permute-start | bytes 2457608 | tf_op jit(solution)/shard_map/ppermute | solution.py:366
  1243.9 47.3 %collective-permute-start.79 = (bf16[1600,672]{0,1:T(8,128)(2,1)}, bf16[1600,672]{0,1:T(8,128)(2,1)}, u32[]{:S(2)}, u32[]{:S(2)}) collective-permute-start(bf16[1600,672]{0,1:T(8,128)(2,1)} %copy.173), channel_id=1, source_target_pairs={{0,16},{16,0},{1,17},{17,1},{2,18},{18,2},{3,19},{19,3},{4,20},{20... | collective-permute-start | bytes 6451208 | tf_op jit(solution)/shard_map/ppermute | solution.py:360
  1288.2 52.2 %collective-permute-start.103 = (bf16[224,800]{1,0:T(8,128)(2,1)}, bf16[224,800]{1,0:T(8,128)(2,1)}, u32[]{:S(2)}, u32[]{:S(2)}) collective-permute-start(bf16[224,800]{1,0:T(8,128)(2,1)} %get-tuple-element.164), channel_id=1, source_target_pairs={{0,4},{4,0},{8,12},{12,8},{1,5},{5,1},{9,13},{13,9},{2,6},{6,2},{1... | collective-permute-start | bytes 1075208 | tf_op jit(solution)/shard_map/ppermute | solution.py:363
  1300.5 108.2 %reduce-scatter.11.cloned.1.call-start = ((), (), s32[]{:S(2)}) async-start(), calls=%async_computation.12 | async-start | bytes 1003520 | tf_op jit(solution)/shard_map/reduce_scatter | solution.py:694
  1321.9 63.7 %collective-permute-start.80 = (bf16[128,1600]{0,1:T(8,128)(2,1)}, bf16[128,1600]{0,1:T(8,128)(2,1)}, u32[]{:S(2)}, u32[]{:S(2)}) collective-permute-start(bf16[128,1600]{0,1:T(8,128)(2,1)} %get-tuple-element.193), channel_id=1, source_target_pairs={{0,0},{8,1},{4,2},{12,3},{1,4},{9,5},{5,6},{13,7},{2,8},{10,9},{6,... | collective-permute-start | bytes 1228808 | tf_op jit(solution)/shard_map/ppermute | solution.py:400
  1326.8 58.8 %collective-permute-start.81 = (bf16[128,1600]{0,1:T(8,128)(2,1)}, bf16[128,1600]{0,1:T(8,128)(2,1)}, u32[]{:S(2)}, u32[]{:S(2)}) collective-permute-start(bf16[128,1600]{0,1:T(8,128)(2,1)} %get-tuple-element.194), channel_id=1, source_target_pairs={{4,0},{12,1},{0,2},{8,3},{5,4},{13,5},{1,6},{9,7},{6,8},{14,9},{2,... | collective-permute-start | bytes 1228808 | tf_op jit(solution)/shard_map/ppermute | solution.py:403
  1337.0 42.2 %collective-permute-start.131 = (f32[150,128]{1,0:T(8,128)S(1)}, f32[150,128]{1,0:T(8,128)S(1)}, u32[]{:S(2)}, u32[]{:S(2)}) collective-permute-start(f32[150,128]{1,0:T(8,128)S(1)} %fusion.150), channel_id=1, source_target_pairs={{0,1},{1,0},{2,3},{3,2},{4,5},{5,4},{6,7},{7,6},{8,9},{9,8},{10,11... | collective-permute-start | bytes 230408 | tf_op jit(solution)/shard_map/ppermute | solution.py:730
  1340.3 49.4 %collective-permute-start.119 = (bf16[384,1600]{0,1:T(8,128)(2,1)}, bf16[384,1600]{0,1:T(8,128)(2,1)}, u32[]{:S(2)}, u32[]{:S(2)}) collective-permute-start(bf16[384,1600]{0,1:T(8,128)(2,1)} %copy.184), channel_id=1, source_target_pairs={{0,4},{4,0},{8,12},{12,8},{1,5},{5,1},{9,13},{13,9},{2,6},{6,2},{1... | collective-permute-start | bytes 3686408 | tf_op jit(solution)/shard_map/ppermute | solution.py:363
  1384.3 116.8 %collective-permute-start.126 = (bf16[1600,1600]{1,0:T(8,128)(2,1)}, bf16[1600,1600]{1,0:T(8,128)(2,1)}, u32[]{:S(2)}, u32[]{:S(2)}) collective-permute-start(bf16[1600,1600]{1,0:T(8,128)(2,1)} %constant_dynamic-update-slice_fusion.74), channel_id=1, source_target_pairs={{0,16},{1,17},{2,18},{3,19},{4,20},{5,21},{6,22},{7,23},{8,24},{9,... | collective-permute-start | bytes 15360008 | tf_op jit(solution)/shard_map/ppermute | solution.py:360
  1400.9 81.0 %collective-permute-start.89 = (bf16[256,1600]{0,1:T(8,128)(2,1)}, bf16[256,1600]{0,1:T(8,128)(2,1)}, u32[]{:S(2)}, u32[]{:S(2)}) collective-permute-start(bf16[256,1600]{0,1:T(8,128)(2,1)} %get-tuple-element.186), channel_id=1, source_target_pairs={{16,0},{17,1},{18,2},{19,3},{20,4},{21,5},{22,6},{23,7},{24,8},{25... | collective-permute-start | bytes 2457608 | tf_op jit(solution)/shard_map/ppermute | solution.py:360
  1421.3 31.2 %collective-permute-start.121 = (bf16[416,1600]{1,0:T(8,128)(2,1)}, bf16[416,1600]{1,0:T(8,128)(2,1)}, u32[]{:S(2)}, u32[]{:S(2)}) collective-permute-start(bf16[416,1600]{1,0:T(8,128)(2,1)} %pad_maximum_fusion.12), channel_id=1, source_target_pairs={{0,8},{8,0},{4,12},{12,4},{1,9},{9,1},{5,13},{13,5},{2,10},{10,2},... | collective-permute-start | bytes 3993608 | tf_op jit(solution)/shard_map/ppermute | solution.py:366
  1436.6 28.1 %collective-permute-start.106 = (bf16[64,800]{1,0:T(8,128)(2,1)}, bf16[64,800]{1,0:T(8,128)(2,1)}, u32[]{:S(2)}, u32[]{:S(2)}) collective-permute-start(bf16[64,800]{1,0:T(8,128)(2,1)} %get-tuple-element.228), channel_id=1, source_target_pairs={{0,4},{4,0},{8,12},{12,8},{1,5},{5,1},{9,13},{13,9},{2,6},{6,2},{1... | collective-permute-start | bytes 307208 | tf_op jit(solution)/shard_map/ppermute | solution.py:363
  1455.0 54.9 %collective-permute-start.127 = (bf16[1600,1600]{1,0:T(8,128)(2,1)}, bf16[1600,1600]{1,0:T(8,128)(2,1)}, u32[]{:S(2)}, u32[]{:S(2)}) collective-permute-start(bf16[1600,1600]{1,0:T(8,128)(2,1)} %constant_dynamic-update-slice_fusion.68), channel_id=1, source_target_pairs={{16,0},{17,1},{18,2},{19,3},{20,4},{21,5},{22,6},{23,7},{24,8},{25... | collective-permute-start | bytes 15360008 | tf_op jit(solution)/shard_map/ppermute | solution.py:360
  (271 other events, 5001.7 us)
Sparse Core Ops, SparseCore 0:
  14.1 74.9 all-gather.14
  90.7 53.7 all-gather.6
  146.7 99.3 all-gather.8
  295.5 72.7 all-gather.10
  370.3 115.8 all-gather.12
  860.4 27.4 reduce-scatter.12
  890.8 73.0 reduce-scatter.8
  966.3 94.1 reduce-scatter.16
  1140.9 98.5 reduce-scatter.14
  1300.6 81.7 reduce-scatter.6
  1385.2 22.8 reduce-scatter.10

commit v2 on v1

--- a/solution.py
+++ b/solution.py
@@ -25,19 +25,22 @@
     )
 
 
-def norm_stats(value):
-    centred = value - jnp.mean(value, axis=-1, keepdims=True)
-    variance = jnp.mean(centred * centred, axis=-1, keepdims=True)
+def norm_stats(value, mask, width):
+    mean = jnp.sum(value, axis=-1, keepdims=True) * (1.0 / width)
+    centred = value - mean if mask is None else (value - mean) * mask
+    variance = jnp.sum(centred * centred, axis=-1, keepdims=True) * (1.0 / width)
     inverse = lax.rsqrt(variance + EPSILON)
     return centred * inverse, inverse
 
 
-def norm_back(grad, value, gain):
-    unit, inverse = norm_stats(value)
+def norm_back(grad, value, gain, mask, width):
+    unit, inverse = norm_stats(value, mask, width)
     grad_unit = grad * gain
-    mean_one = jnp.mean(grad_unit, axis=-1, keepdims=True)
-    mean_two = jnp.mean(grad_unit * unit, axis=-1, keepdims=True)
+    mean_one = jnp.sum(grad_unit, axis=-1, keepdims=True) * (1.0 / width)
+    mean_two = jnp.sum(grad_unit * unit, axis=-1, keepdims=True) * (1.0 / width)
     grad_value = inverse * (grad_unit - mean_one - unit * mean_two)
+    if mask is not None:
+        grad_value = grad_value * mask
     return grad_value, jnp.sum(grad * unit, axis=0), jnp.sum(grad, axis=0)
 
 
@@ -83,7 +86,9 @@
 
 
 def attend_back_kernel(grouped, q_ref, k_ref, v_ref, bias_ref, lse_ref, *refs):
-    *g_refs, dq_ref, dk_ref, dv_ref, keys, values = refs
+    *g_refs, out_ref, keys, values = refs
+    head = pl.program_id(0)
+    slots = pl.num_programs(0)
     length = q_ref.shape[1]
     half = length // 2
     n = half // 4
@@ -113,9 +118,20 @@
             dscore = (probs * (inner - rowdot)).astype(BF)
             values[:, :extent] += dot(grad, probs.astype(BF), (1, 1))
             keys[:, :extent] += dot(query, dscore, (1, 1))
-            dq_ref[:, at : at + block] = (dot(k_ref[:, :extent], dscore, (1, 0)) * scale).astype(BF)
-    dk_ref[...] = keys[...].astype(BF)
-    dv_ref[...] = values[...].astype(BF)
+            grad_query = (dot(k_ref[:, :extent], dscore, (1, 0)) * scale).astype(BF)
+            out_ref[pl.ds(pl.multiple_of(head * HEAD, HEAD), HEAD), at : at + block] = grad_query
+    key_rows = pl.ds(pl.multiple_of((slots + head) * HEAD, HEAD), HEAD)
+    value_rows = pl.ds(pl.multiple_of((2 * slots + head) * HEAD, HEAD), HEAD)
+    out_ref[key_rows, :] = keys[...].astype(BF)
+    out_ref[value_rows, :] = values[...].astype(BF)
+
+    @pl.when(head == 0)
+    def _():
+        used = 3 * HEAD * pl.num_programs(0)
+        spare = out_ref.shape[0] % (3 * HEAD)
+        if spare:
+            rest = pl.ds(pl.multiple_of(used, HEAD), spare)
+            out_ref[rest, :] = jnp.zeros((spare, length), BF)
 
 
 def attend(mixed, bias, slots, grouped):
@@ -133,7 +149,7 @@
         + [jax.ShapeDtypeStruct((slots, 1, length), F32)],
         compiler_params=pltpu.CompilerParams(vmem_limit_bytes=40 * 2**20),
         cost_estimate=pl.CostEstimate(
-            flops=3 * slots * length * length * HEAD,
+            flops=42 * slots * length * length * HEAD,
             bytes_accessed=4 * length * length + 8 * slots * HEAD * length,
             transcendentals=slots * length * length,
         ),
@@ -145,7 +161,6 @@
     length = mixed.shape[1]
     part = lambda first: pl.BlockSpec((HEAD, length), lambda h: (first + h, 0))
     whole = pl.BlockSpec((length, length), lambda h: (0, 0))
-    one = jax.ShapeDtypeStruct((slots * HEAD, length), BF)
     count, span = (4, length // 4) if grouped else (1, length)
     return pl.pallas_call(
         partial(attend_back_kernel, grouped),
@@ -158,12 +173,12 @@
             pl.BlockSpec((1, 1, length), lambda h: (h, 0, 0)),
         ]
         + [pl.BlockSpec((HEAD, span), lambda h: (h, 0))] * count,
-        out_specs=[part(0), part(0), part(0)],
-        out_shape=[one, one, one],
+        out_specs=pl.BlockSpec(mixed.shape, lambda h: (0, 0)),
+        out_shape=jax.ShapeDtypeStruct(mixed.shape, BF),
         scratch_shapes=[pltpu.VMEM((HEAD, length), F32), pltpu.VMEM((HEAD, length), F32)],
         compiler_params=pltpu.CompilerParams(vmem_limit_bytes=40 * 2**20),
         cost_estimate=pl.CostEstimate(
-            flops=8 * slots * length * length * HEAD,
+            flops=48 * slots * length * length * HEAD,
             bytes_accessed=4 * length * length + 14 * slots * HEAD * length,
             transcendentals=slots * length * length,
         ),
@@ -251,6 +266,12 @@
 
 
 def member_rows(refs, member, owner, cut, rows):
+    if member is None:
+        at = owner * rows
+        return [
+            (ref[at : at + cut, :].astype(F32), ref[at + cut : at + rows, :].astype(F32))
+            for ref in refs
+        ]
     turn = member ^ owner
     twin = (turn & 1) * 2 + turn // 2
     found = []
@@ -261,58 +282,159 @@
     return found
 
 
-def finish_attn_kernel(slots, cut, member_ref, left_ref, right_ref, out_ref):
-    member = member_ref[0]
+def blocks_into(out_ref, lines, value, block, padded):
+    for index in range(value.shape[1] // padded):
+        out_ref[lines, index * block : (index + 1) * block] = value[
+            :, index * padded : index * padded + block
+        ]
+
+
+def finish_attn_kernel(slots, cut, total, _, left_ref, right_ref, out_ref):
+    member = None
     rows = out_ref.shape[0]
     width = out_ref.shape[1] // 3
     high = slots * HEAD
+    held = left_ref.shape[0] // 4
     for owner in range(4):
         start = min(owner * high, width - high)
         spare = owner * high - start
-        (left, right) = member_rows((left_ref, right_ref), member, owner, cut, rows)
-        for lines, place in ((0, slice(0, cut)), (1, slice(cut, rows))):
-            both = jnp.concatenate([left[lines], right[lines]], axis=1)
+        (left, right) = member_rows((left_ref, right_ref), member, owner, cut, held)
+        for lines, first, size in ((0, 0, cut), (1, cut, rows - cut)):
+            shared = left[lines].shape[1] * 2 - total
+            both = jnp.concatenate([left[lines], right[lines][:, shared:]], axis=1)
             for third in range(3):
                 to = third * width + start + spare
-                out_ref[place, to : to + high - spare] = both[
-                    :, third * high + spare : (third + 1) * high
+                out_ref[first : first + size, to : to + high - spare] = both[
+                    :size, third * high + spare : (third + 1) * high
                 ]
 
 
-def finish_proj_kernel(step, slab, cut, member_ref, left_ref, right_ref, out_ref):
+def finish_proj_kernel(step, slab, cut, total, padded, member_ref, left_ref, right_ref, out_ref):
     member = member_ref[0]
-    rows = out_ref.shape[0]
+    block = out_ref.shape[1] // 4
     for owner in range(4):
         size = slab if owner == 3 else step
         (left, right) = member_rows((left_ref, right_ref), member, owner, cut, slab)
-        both = [jnp.concatenate([left[i], right[i]], axis=1) for i in range(2)]
-        whole = jnp.concatenate(both)
-        out_ref[owner * step : owner * step + size, :] = whole[:size]
-
-
-def finish_in_kernel(cut, member_ref, value_ref, out_ref):
-    member = member_ref[0]
+        for lines, first, count in ((0, 0, cut), (1, cut, size - cut)):
+            shared = left[lines].shape[1] * 2 - total
+            both = jnp.concatenate([left[lines], right[lines][:, shared:]], axis=1)[:count]
+            at = owner * step + first
+            blocks_into(out_ref, slice(at, at + count), both, block, padded)
+
+
+def finish_in_kernel(cut, padded, _, value_ref, out_ref):
+    member = None
     rows = out_ref.shape[0]
     part = out_ref.shape[1] // 16
     for owner in range(4):
-        ((top, low),) = member_rows((value_ref,), member, owner, cut, rows)
+        ((top, low),) = member_rows((value_ref,), member, owner, cut, padded)
         for block in range(4):
             to = (block * 4 + owner) * part
-            out_ref[:cut, to : to + part] = top[:, block * part : (block + 1) * part]
-            out_ref[cut:, to : to + part] = low[:, block * part : (block + 1) * part]
-
-
-def finish_out_kernel(cut, member_ref, value_ref, out_ref):
-    member = member_ref[0]
+            out_ref[:cut, to : to + part] = top[:, block * padded : block * padded + part]
+            out_ref[cut:, to : to + part] = low[
+                : rows - cut, block * padded : block * padded + part
+            ]
+
+
+def finish_out_kernel(cut, padded, _, value_ref, out_ref):
+    member = None
     rows = out_ref.shape[0] // 4
+    block = out_ref.shape[1] // 4
     for owner in range(4):
-        ((top, low),) = member_rows((value_ref,), member, owner, cut, rows)
-        out_ref[owner * rows : owner * rows + cut, :] = top
-        out_ref[owner * rows + cut : (owner + 1) * rows, :] = low
+        ((top, low),) = member_rows((value_ref,), member, owner, cut, padded)
+        at = owner * rows
+        blocks_into(out_ref, slice(at, at + cut), top, block, padded)
+        blocks_into(out_ref, slice(at + cut, at + rows), low[: rows - cut], block, padded)
+
+
+def expand_kernel(padded, _, *refs):
+    half = len(refs) // 2
+    for value_ref, out_ref in zip(refs[:half], refs[half:]):
+        block = value_ref.shape[1] // 4
+        out_ref[...] = jnp.zeros_like(out_ref)
+        for index in range(4):
+            out_ref[:, index * padded : index * padded + block] = value_ref[
+                :, index * block : (index + 1) * block
+            ]
+
+
+def edge_kernel(padded, section_ref, mine_ref, other_ref, edge_ref):
+    block = edge_ref.shape[2] // 4
+    wide = 4 * padded
+    for side, refs in enumerate(((mine_ref, other_ref), (other_ref, mine_ref))):
+
+        @pl.when(section_ref[0] == side)
+        def _(side=side, refs=refs):
+            for index, ref in enumerate(refs):
+                value = ref[:, side * wide : (side + 1) * wide].astype(F32)
+                blocks_into(edge_ref.at[index], slice(None), value, block, padded)
+
+
+def order_kernel(forth, place_ref, value_ref, out_ref):
+    n = value_ref.shape[0] // 8
+    at = 0
+    for part, order in enumerate((TOPS, LOWS)):
+        for turn in order:
+            rows = pl.ds(pl.multiple_of(((place_ref[0] ^ turn) * 2 + part) * n, n), n)
+            if forth:
+                out_ref[at : at + n, :] = value_ref[rows, :]
+            else:
+                out_ref[rows, :] = value_ref[at : at + n, :]
+            at += n
+
+
+def deal_kernel(whole_in, whole_out, places_ref, *refs):
+    place = places_ref[0]
+    count = 1 if whole_in else 4
+    inputs, outs = refs[:count], refs[count:]
+    size = inputs[0].shape[0] // (4 if whole_in else 1)
+    for turn in range(4):
+        at = pl.multiple_of((place ^ turn) * size, size)
+        if whole_in:
+            outs[turn][...] = inputs[0][pl.ds(at, size), :]
+        elif whole_out:
+            outs[0][pl.ds(at, size), :] = inputs[turn][...]
+        else:
+            for owner in range(4):
+
+                @pl.when((place ^ turn) == owner)
+                def _(turn=turn, owner=owner):
+                    outs[turn][...] = inputs[owner][...]
+
+
+def join_kernel(_, own, near_a, near_b, far_a, far_b, *out_refs):
+    n, m = near_a.shape[0], near_b.shape[0]
+    at = 0
+    for part, first, size in (
+        (own, 0, n),
+        (near_a, 0, n),
+        (far_a, 0, 2 * n),
+        (own, n, m),
+        (near_b, 0, m),
+        (far_b, 0, 2 * m),
+    ):
+        column = 0
+        for out_ref in out_refs:
+            width = out_ref.shape[1]
+            out_ref[at : at + size, :] = part[first : first + size, column : column + width]
+            column += width
+        at += size
+
+
+def same_kernel(*refs):
+    pass
 
 
 def tie(value, *others):
-    return lax.optimization_barrier((value, others))[0]
+    any_place = pl.BlockSpec(memory_space=pl.ANY)
+    return pl.pallas_call(
+        same_kernel,
+        in_specs=[any_place] * (1 + len(others)),
+        out_specs=any_place,
+        out_shape=jax.ShapeDtypeStruct(value.shape, value.dtype),
+        input_output_aliases={0: 0},
+        cost_estimate=pl.CostEstimate(flops=0, bytes_accessed=0, transcendentals=0),
+    )(value, *others)
 
 
 def body(
@@ -346,7 +468,15 @@
     slots = -(-HEADS // team)
     heads_width = slots * HEAD
     hid = hidden // team
-    cols = width // team
+    block = width // 4
+    padded = -(-block // 32) * 32 if fast else block
+    wide = 4 * padded
+    mask = None
+    if fast:
+        mask = (jnp.arange(wide) % padded < block).astype(F32)
+    mixed_rows = -(-3 * heads_width // 128) * 128 if fast else 3 * heads_width
+    attn_half = -(-mixed_rows // 256) * 128
+    proj_half = -(-wide // 256) * 128
 
     def head_start(index):
         return jnp.minimum(index * slots, HEADS - slots)
@@ -370,6 +500,26 @@
 
     def pick(a, b):
         return jnp.where(first, a, b)
+
+    def halves(value, half, axis):
+        size = value.shape[axis]
+        left = lax.slice_in_dim(value, 0, half, axis=axis)
+        right = lax.slice_in_dim(value, size - half, size, axis=axis)
+        return pick(left, right), pick(right, left)
+
+    def spaced(vector):
+        if not fast:
+            return vector
+        parts = vector.reshape(-1, 4, block)
+        parts = jnp.pad(parts, ((0, 0), (0, 0), (0, padded - block)))
+        return parts.reshape(vector.shape[:-1] + (wide,))
+
+    def dense(vector):
+        if not fast:
+            return vector
+        return vector.reshape(vector.shape[:-1] + (4, padded))[..., :block].reshape(
+            vector.shape[:-1] + (width,)
+        )
 
     def flat(p, z):
         return p * shards + z
@@ -389,13 +539,13 @@
     early = place < shards // 2
     even = member % 2 == 0
 
-    def to_team(value):
+    def to_team_far(value):
         top, low = value[:n], value[n:]
         one = lax.ppermute(jnp.where(early, top, low), chip_axes, rounds[0])
         two = lax.ppermute(jnp.where(early, low, top), chip_axes, rounds[1])
         return jnp.concatenate([jnp.where(even, one, two), jnp.where(even, two, one)])
 
-    def from_team(value):
+    def from_team_far(value):
         top, low = value[:n], value[n:]
         one = lax.ppermute(
             jnp.where(even, top, low), chip_axes, [(b, a) for a, b in rounds[0]]
@@ -405,27 +555,94 @@
         )
         return jnp.concatenate([jnp.where(early, one, two), jnp.where(early, two, one)])
 
+    plane = lax.axis_index("seq")
+
+    def turned(pieces, axis):
+        own, *others = pieces
+        return [own] + [
+            lax.ppermute(x, axis, pairs) for x, pairs in zip(others, (SIDE, ACROSS, CORNER))
+        ]
+
+    def dealt(place, pieces, whole_in, whole_out):
+        rows, columns = pieces[0].shape
+        if whole_in:
+            outs = [jax.ShapeDtypeStruct((rows // 4, columns), BF)] * 4
+        elif whole_out:
+            outs = [jax.ShapeDtypeStruct((rows * 4, columns), BF)]
+        else:
+            outs = [jax.ShapeDtypeStruct((rows, columns), BF)] * 4
+        return kernel_call(partial(deal_kernel, whole_in, whole_out), place, pieces, outs)
+
+    def to_team(value):
+        if not fast:
+            return to_team_far(value)
+        pieces = turned(dealt(member, [value], True, False), "replica")
+        pieces = turned(dealt(plane ^ member, pieces, False, False), "seq")
+        return dealt(plane, pieces, False, True)[0]
+
+    def from_team(value):
+        if not fast:
+            return from_team_far(value)
+        pieces = turned(dealt(plane, [value], True, False), "seq")
+        pieces = turned(dealt(plane ^ member, pieces, False, False), "replica")
+        return dealt(member, pieces, False, True)[0]
+
     if fast:
         order_a = [member, member ^ 2, member ^ 1, member ^ 3]
         order_b = [member, member ^ 1, member ^ 2, member ^ 3]
     else:
         order_a = order_b = list(range(team))
 
-    def gather(value, cut):
+    def gather_near(value, cut, widths=None):
         a, b = value[:cut], value[cut:]
         if not fast:
-            return jnp.concatenate(
+            whole = jnp.concatenate(
                 [
                     lax.all_gather(a, team_axes, axis=0, tiled=True),
                     lax.all_gather(b, team_axes, axis=0, tiled=True),
                 ]
             )
+            return whole, whole
         near_a, near_b = across(a), side(b)
+        return gather_far(value, cut, near_a, near_b, widths), near_b
+
+    def gather_far(value, cut, near_a, near_b, widths=None):
+        a, b = value[:cut], value[cut:]
         far_a = side(jnp.concatenate([a, near_a]))
         far_b = across(jnp.concatenate([b, near_b]))
-        return jnp.concatenate([a, near_a, far_a, b, near_b, far_b])
-
-    def scatter(value):
+        outs = [
+            jax.ShapeDtypeStruct((4 * value.shape[0], width), value.dtype)
+            for width in widths or [value.shape[1]]
+        ]
+        parts = [value, near_a, near_b, far_a, far_b]
+        outs = kernel_call(join_kernel, member, parts, outs)
+        return outs if widths else outs[0]
+
+    def gather(value, cut):
+        return gather_near(value, cut)[0]
+
+    def gather_many(values, cut):
+        whole = jnp.concatenate(values, axis=1)
+        return gather_near(whole, cut, [value.shape[1] for value in values])[0]
+
+    def ordered(forth, value):
+        out = jax.ShapeDtypeStruct(value.shape, value.dtype)
+        return kernel_call(partial(order_kernel, forth), member, [value], [out])[0]
+
+    def gather_late(value):
+        if not fast:
+            return gather(value, n)
+        whole = lax.all_gather(value, "replica", axis=0, tiled=True)
+        return ordered(True, whole)
+
+    def scatter_late(value):
+        if not fast:
+            return scatter(value)
+        whole = ordered(False, value)
+        return lax.psum_scatter(whole, "replica", scatter_dimension=0, tiled=True)
+
+
+    def scatter(value, got=None):
         middle_row = value.shape[0] // 2
         a, b = value[:middle_row], value[middle_row:]
         if not fast:
@@ -436,7 +653,7 @@
                 ]
             )
         m = middle_row // 4
-        got_a, got_b = side(a[2 * m :]), across(b[2 * m :])
+        got_a, got_b = got or scatter_first(value)
         sent_a = (a[m : 2 * m].astype(F32) + got_a[m:]).astype(BF)
         sent_b = (b[m : 2 * m].astype(F32) + got_b[m:]).astype(BF)
         last_a, last_b = across(sent_a), side(sent_b)
@@ -444,12 +661,17 @@
         sum_b = b[:m].astype(F32) + got_b[:m] + last_b
         return jnp.concatenate([sum_a, sum_b])
 
+    def scatter_first(value):
+        middle_row = value.shape[0] // 2
+        m = middle_row // 4
+        return side(value[2 * m : middle_row]), across(value[middle_row + 2 * m :])
+
     if fast:
         rows = width // replicas
         slab = -(-rows // 64) * 16
         step = (rows - slab) // 3
-        cut = (rows // 32) * 16
-        wide = jax.ShapeDtypeStruct((16 * slab, 2 * n), BF)
+        cut = padded // 2
+        sorted_heads = jax.ShapeDtypeStruct((16 * slab, 2 * n), BF)
         one = jax.ShapeDtypeStruct((heads_width, 2 * n), BF)
         scratch = [pltpu.VMEM((width, 2 * n), BF)]
 
@@ -458,7 +680,7 @@
             own, near, over, far = values
             got = [own, side(near), across(over), corner(far)]
             kernel = partial(sort_heads_kernel, slots, rows, step, slab)
-            return kernel_call(kernel, member, got, [wide], scratch)[0]
+            return kernel_call(kernel, member, got, [sorted_heads], scratch)[0]
         pieces = values[0].reshape(heads_width, 2, team, n).transpose(2, 0, 1, 3)
         got = lax.all_to_all(pieces, team_axes, 0, 0, tiled=True)
         got = got.reshape(team, heads_width, 2 * n)
@@ -494,51 +716,86 @@
 
     if fast:
         hid_part = hid // replicas
+        more = padded - rows
         own_attn = jnp.concatenate(head_columns(attn_weight[0]), axis=1)
-        attn_half = own_attn.shape[1] // 2
+        own_attn = jnp.pad(own_attn, ((0, more), (0, mixed_rows - 3 * heads_width)))
         own_in = jnp.concatenate(
             [
-                lax.dynamic_slice_in_dim(
-                    fc_in_weight[0], block * hid + member * hid_part, hid_part, 1
+                jnp.pad(
+                    lax.dynamic_slice_in_dim(
+                        fc_in_weight[0], part * hid + member * hid_part, hid_part, 1
+                    ),
+                    ((0, more), (0, padded - hid_part)),
                 )
-                for block in range(replicas)
+                for part in range(replicas)
             ],
             axis=1,
         )
         own_out = lax.dynamic_slice_in_dim(fc_out_weight[0], member * hid_part, hid_part, 0)
-
-        def spread(own_0, own_1):
-            got = cross(pick(own_1, own_0))
-            return pick(own_0, got), pick(got, own_1)
-
-        def full(piece):
-            mine = lax.all_gather(piece, "seq", axis=0, tiled=True)
+        own_proj = lax.dynamic_slice_in_dim(proj_weight[0], member * step, slab, 0)
+        own_out, own_proj = kernel_call(
+            partial(expand_kernel, padded),
+            member,
+            [own_out, own_proj],
+            [jax.ShapeDtypeStruct((hid_part, wide), BF), jax.ShapeDtypeStruct((slab, wide), BF)],
+        )
+        own_out = jnp.pad(own_out, ((0, padded - hid_part), (0, 0)))
+
+        def gathered(piece):
+            return lax.all_gather(piece, "seq", axis=0, tiled=True)
+
+        def full(mine):
             other = cross(mine)
             return pick(mine, other), pick(other, mine)
 
-        attn_pieces = spread(own_attn[:, :attn_half], own_attn[:, attn_half:])
-        fc_pieces = spread(own_in, own_out)
-        own_proj = lax.dynamic_slice_in_dim(proj_weight[0], member * step, slab, 0)
-
-        def weights_whole():
-            attn_0 = jnp.concatenate(full(attn_pieces[0]), axis=1)
-            proj = lax.all_gather(own_proj, "seq", axis=0, tiled=True)
-            proj = gather(proj, 2 * slab)
-            other = cross(proj)
-            fc_0 = full(fc_pieces[0])
-            attn_1 = jnp.concatenate(full(attn_pieces[1]), axis=1)
-            fc_1 = full(fc_pieces[1])
-            return (attn_0, pick(proj, other), *fc_0), (attn_1, pick(other, proj), *fc_1)
+        def spread(pair):
+            got = cross(pair[1])
+            return pick(pair[0], got), pick(got, pair[0])
+
+        attn_pieces = spread(halves(own_attn, attn_half, 1))
+        fc_pieces = spread((pick(own_in, own_out), pick(own_out, own_in)))
+        shared = 2 * attn_half - mixed_rows
+        attn_got = [gathered(attn_pieces[0])]
+        proj_got = []
+        fc_got = []
+        proj_whole = []
+
+        def fetch_proj(after):
+            proj_got.append(gathered(tie(own_proj, after)))
+
+        def fetch_fc(layer, after):
+            fc_got.append(gathered(tie(fc_pieces[layer], after)))
+
+        def fetch_attn(after):
+            attn_got.append(gathered(tie(attn_pieces[1], after)))
+
+        def get_attn(layer, after):
+            left, right = full(tie(attn_got[layer], after))
+            return jnp.concatenate([left, right[:, shared:]], axis=1)
+
+        def get_proj(layer, near=None, after=None):
+            if layer == 0:
+                mine = tie(proj_got[0], near)
+                near = across(mine[: 2 * slab]), side(mine[2 * slab :])
+                near = [tie(value, after) for value in near]
+                mine = gather_far(mine, 2 * slab, *near)
+                other = cross(mine)
+                proj_whole.extend([pick(mine, other), pick(other, mine)])
+            return proj_whole[layer]
+
+        def get_fc(layer, after):
+            return full(tie(fc_got[layer], after))
 
         def hid_of(vector):
-            return lax.dynamic_slice_in_dim(
+            mine = lax.dynamic_slice_in_dim(
                 vector.reshape(replicas, replicas, hid_part), member, 1, 1
-            ).reshape(hid)
+            )
+            return jnp.pad(mine[:, 0], ((0, 0), (0, padded - hid_part))).reshape(wide)
 
         def hid_into(vector):
             zeros = jnp.zeros((replicas, replicas, hid_part), F32)
             return lax.dynamic_update_slice_in_dim(
-                zeros, vector.reshape(replicas, 1, hid_part), member, 1
+                zeros, vector.reshape(replicas, 1, padded)[..., :hid_part], member, 1
             ).reshape(hidden)
 
     else:
@@ -557,8 +814,24 @@
             w_out = lax.dynamic_slice_in_dim(whole(fc_out_weight), member * hid, hid, 0)
             return w_attn, w_proj, w_in, w_out
 
-        def weights_whole():
-            return weights_of(0), weights_of(1)
+        whole_weights = [weights_of(0), weights_of(1)]
+
+        def fetch_proj(after):
+            pass
+
+        def fetch_fc(layer, after):
+            pass
+
+        fetch_attn = fetch_proj
+
+        def get_attn(layer, after):
+            return whole_weights[layer][0]
+
+        def get_proj(layer, *others):
+            return whole_weights[layer][1]
+
+        def get_fc(layer, after):
+            return whole_weights[layer][2:]
 
         def hid_of(vector):
             return lax.dynamic_slice_in_dim(vector, member * hid, hid, 0)
@@ -572,6 +845,13 @@
         return lax.dynamic_update_slice_in_dim(jnp.zeros((width,), F32), vector, start, 0)
 
     block_0, block_1 = boundary[0, 0, 0], boundary[0, 1, 0]
+    if fast:
+        block_0, block_1 = kernel_call(
+            partial(expand_kernel, padded),
+            member,
+            [block_0, block_1],
+            [jax.ShapeDtypeStruct((local, wide), BF)] * 2,
+        )
     kept = pick(block_0, block_1)
     got = cross(pick(block_1, block_0))
     source = to_team(pick(kept, got))
@@ -593,107 +873,142 @@
         for index in order:
             places.append(chunk * half + index * n + jnp.arange(n, dtype=jnp.int32))
             names.append(lax.dynamic_index_in_dim(ids[chunk], index, 0, keepdims=False))
+    if fast:
+        places, names = [], []
+        ids = ids.reshape(2, 2, team, n // 2)
+        for chunk, order in enumerate((order_a, order_b)):
+            for index in order:
+                for part in range(2):
+                    at = chunk * half + part * (half // 2) + index * (n // 2)
+                    places.append(at + jnp.arange(n // 2, dtype=jnp.int32))
+                    names.append(
+                        lax.dynamic_index_in_dim(ids[chunk, part], index, 0, keepdims=False)
+                    )
     places, names = jnp.concatenate(places), jnp.concatenate(names)
     allowed = (names[:, None] == names[None, :]) & (places[:, None] <= places[None, :])
     bias = jnp.where(allowed, 0.0, MASKED).astype(F32)
 
     def parameters(layer):
         vector = vectors[layer]
-        gains = vector[: 2 * width].reshape(2, width)
-        biases = vector[2 * width : 8 * width].reshape(6, width)
+        lines = vector[: 8 * width].reshape(8, width)
+        query_bias = lax.dynamic_slice_in_dim(lines[3], start, heads_width, 0)
+        value_bias = lax.dynamic_slice_in_dim(lines[4], start, heads_width, 0)
+        lines = spaced(lines)
+        gains, biases = lines[:2], lines[2:]
         hid_bias = hid_of(vector[8 * width :])
-        query_bias = lax.dynamic_slice_in_dim(biases[1], start, heads_width, 0)
-        value_bias = lax.dynamic_slice_in_dim(biases[2], start, heads_width, 0)
         mixed_bias = jnp.concatenate([query_bias, jnp.zeros_like(query_bias), value_bias])
+        mixed_bias = jnp.pad(mixed_bias, (0, mixed_rows - mixed_bias.shape[0]))
         return gains, biases, hid_bias, mixed_bias
 
-    def forward(layer, value, weights):
-        w_attn, w_proj, w_in, w_out = weights
-        gains, biases, hid_bias, mixed_bias = parameters(layer)
-        normed = (norm_stats(value)[0] * gains[0] + biases[0]).astype(BF)
-        normed = gather(normed, n)
-        mixed = (dot(w_attn, normed, (0, 1)) + mixed_bias[:, None]).astype(BF)
+    def enter(layer, value):
+        gains, biases, _, _ = parameters(layer)
+        normed = (norm_stats(value, mask, width)[0] * gains[0] + biases[0]).astype(BF)
+        return gather_near(normed, n)
+
+    def mix(layer, normed, w_attn, *others):
+        mixed_bias = parameters(layer)[3]
+        if fast and others:
+            mixed_bias = tie(mixed_bias, *others)
+        return (dot(w_attn, normed, (0, 1)) + mixed_bias[:, None]).astype(BF)
+
+    def forward(layer, value, normed, mixed, w_proj, hold):
+        gains, biases, hid_bias, _ = parameters(layer)
+        proj_bias = tie(biases[3], fc_got[0]) if fast and layer == 0 else biases[3]
         attended, lse = attend(mixed, bias, slots, fast)
+        if layer == 0:
+            w_proj.append(get_proj(0, near, lse))
+        w_proj = w_proj[layer]
         attended = heads_to_tokens(attended)
-        middle = value + dot(attended, w_proj, (0, 0)) + biases[3]
-        normed_two = (norm_stats(middle)[0] * gains[1] + biases[4]).astype(BF)
+        middle = value + dot(attended, w_proj, (0, 0)) + proj_bias
+        gain = hold(gains[1])
+        normed_two = (norm_stats(middle, mask, width)[0] * gain + biases[4]).astype(BF)
+        w_in, w_out = get_fc(layer, normed_two)
         normed_two = gather(normed_two, n)
         activated, slope = gelu_pair(dot(normed_two, w_in, (1, 0)) + hid_bias)
-        activated, slope = activated.astype(BF), slope.astype(BF)
-        out = middle + scatter(dot(activated, w_out, (1, 0)).astype(BF)) + biases[5]
-        return out, (value, normed, mixed, lse, attended, middle, normed_two, activated, slope)
+        activated, slope = lax.optimization_barrier((activated.astype(BF), slope.astype(BF)))
+        kept = (value, normed, mixed, lse, attended, middle, normed_two, activated, slope)
+        return kept, (w_in, w_out)
+
+    def leave(layer, middle, activated, w_out):
+        return dot(activated, w_out, (1, 0)).astype(BF)
 
     ones = lax.optimization_barrier(jnp.ones((16, length), BF))
 
-    def backward(layer, grad_out, kept, weights, waiting):
+    def backward(layer, grad_out, grad_low, kept, weights, fillers):
         value, normed, mixed, lse, attended, middle, normed_two, activated, slope = kept
         w_attn, w_proj, w_in, w_out = weights
         gains = parameters(layer)[0]
-        grad_low = grad_out.astype(BF)
-        low_sum = jnp.sum(grad_low.astype(F32), axis=0)
-        grad_low = tie(gather(grad_low, n), waiting)
+        low_sum = jnp.sum(grad_out, axis=0)
         grad_pre = (dot(grad_low, w_out, (1, 1)) * slope).astype(BF)
-        grad_two = scatter(dot(grad_pre, w_in, (1, 1)).astype(BF))
-        fc_pair = split_pair(dot(normed_two, grad_pre, (0, 0)), dot(activated, grad_low, (0, 0)))
-        grad_two = tie(grad_two, fc_pair)
+        part = dot(grad_pre, w_in, (1, 1)).astype(BF)
+        fillers[0](part)
+        grad_two = scatter(part)
+        if fast:
+            sent = dot(pick(activated, normed_two), pick(grad_low, grad_pre), (0, 0))
+            sent = cross(sent.astype(BF))
+            fc_pair = (pick(normed_two, activated), pick(grad_pre, grad_low), sent)
+        else:
+            fc_pair = (
+                dot(normed_two, grad_pre, (0, 0)).astype(BF),
+                dot(activated, grad_low, (0, 0)).astype(BF),
+            )
+        fillers[1](part)
         hid_sum = dot(ones, grad_pre, (1, 0))[0]
-        grad_norm, gain_two, shift_two = norm_back(grad_two, middle, gains[1])
+        gain = fillers[4](gains[1])
+        grad_norm, gain_two, shift_two = norm_back(grad_two, middle, gain, mask, width)
         grad_middle = grad_out + grad_norm
         grad_branch = grad_middle.astype(BF)
         branch_sum = jnp.sum(grad_branch.astype(F32), axis=0)
         grad_attended = dot(w_proj, grad_branch, (1, 1)).astype(BF)
         grad_attended = tokens_to_heads(grad_attended)
-        fc_total = join_pair(fc_pair)
-        most = width // 2
-        proj_pair = split_pair(
-            dot(attended, grad_branch[:, :most], (1, 0)),
-            dot(attended, grad_branch[:, most:], (1, 0)),
+        own, other = halves(grad_branch, proj_half, 1)
+        if fast:
+            sent = cross(dot(attended, other, (1, 0)).astype(BF))
+            fc_total = (dot(fc_pair[0], fc_pair[1], (0, 0)) + fc_pair[2]).astype(BF)
+            proj_total = (dot(attended, own, (1, 0)) + sent).astype(BF)
+        else:
+            fc_total = fc_pair
+            proj_total = dot(attended, grad_branch, (1, 0)).astype(BF)
+        fillers[2](grad_attended[-1], fc_total, proj_total)
+        lse = fillers[3](lse, proj_total)
+        grad_mixed = attend_back(mixed, grad_attended, bias, lse, slots, fast)
+        part = dot(grad_mixed, w_attn, (0, 1)).astype(BF)
+        grad_one = scatter(part)
+        own, other = halves(grad_mixed, attn_half, 0)
+        if fast:
+            attn_pair = (own, cross(dot(normed, other, (0, 1)).astype(BF)))
+            attn_total = (dot(normed, attn_pair[0], (0, 1)) + attn_pair[1]).astype(BF)
+        else:
+            attn_total = dot(normed, grad_mixed, (0, 1)).astype(BF)
+        mixed_sum = jnp.sum(grad_mixed.astype(F32), axis=1)
+        gain = fillers[5](gains[0])
+        grad_norm, gain_one, shift_one = norm_back(grad_one, value, gain, mask, width)
+        grad_in = grad_middle + grad_norm
+        query_sum = heads_into(mixed_sum[:heads_width])
+        value_sum = heads_into(mixed_sum[2 * heads_width : 3 * heads_width])
+        lines = dense(
+            jnp.stack([gain_one, gain_two, shift_one, branch_sum, shift_two, low_sum])
         )
-        grad_attended = tie(grad_attended, fc_total, proj_pair)
-        grad_q, grad_k, grad_v = attend_back(mixed, grad_attended, bias, lse, slots, fast)
-        grad_mixed = jnp.concatenate([grad_q, grad_k, grad_v])
-        grad_one = scatter(dot(grad_mixed, w_attn, (0, 1)).astype(BF))
-        proj_total = join_pair(proj_pair)
-        most = grad_mixed.shape[0] // 2
-        attn_pair = split_pair(
-            dot(normed, grad_mixed[:most], (0, 1)), dot(normed, grad_mixed[most:], (0, 1))
-        )
-        grad_one = tie(grad_one, attn_pair, proj_total)
-        query_sum = jnp.sum(grad_q.astype(F32), axis=1)
-        value_sum = jnp.sum(grad_v.astype(F32), axis=1)
-        grad_norm, gain_one, shift_one = norm_back(grad_one, value, gains[0])
-        grad_in = grad_middle + grad_norm
         small = jnp.concatenate(
             [
-                gain_one,
-                gain_two,
-                shift_one,
-                heads_into(query_sum),
-                heads_into(value_sum),
-                branch_sum,
-                shift_two,
-                low_sum,
+                lines[:3].ravel(),
+                query_sum,
+                value_sum,
+                lines[3:].ravel(),
                 hid_into(hid_sum),
             ]
         )
-        return grad_in, small, fc_total, proj_total, join_pair(attn_pair)
-
-    def split_pair(part_0, part_1):
-        if not fast:
-            return part_0.astype(BF), part_1.astype(BF)
-        return pick(part_0, part_1), cross(pick(part_1, part_0).astype(BF))
-
-    def join_pair(pair):
-        if not fast:
-            return pair
-        return (pair[0] + pair[1]).astype(BF)
+        return grad_in, small, fc_total, proj_total, attn_total, grad_mixed
 
     if fast:
 
-        def collect(layer, total, at):
-            mine = lax.psum_scatter(total, "seq", scatter_dimension=0, tiled=True)
-            mine = gather(mine, at)
-            return mine, cross(mine, [(1 - layer, layer)])
+        proj_cut = (slab // 32) * 16
+
+        def over_planes(total):
+            return lax.psum_scatter(total, "seq", scatter_dimension=0, tiled=True)
+
+        def both(mine_0, mine_1):
+            return (mine_0, cross(mine_0, [(1, 0)])), (mine_1, cross(mine_1, [(0, 1)]))
 
         def finish(kernel, pairs, shape):
             (mine_0, other_0), (mine_1, other_1) = pairs
@@ -705,13 +1020,13 @@
             (mine_0, other_0), (mine_1, other_1) = pairs
             left, right = pick(mine_0, other_1), pick(other_0, mine_1)
             w_in = kernel_call(
-                partial(finish_in_kernel, cut),
+                partial(finish_in_kernel, cut, padded),
                 member,
                 [left],
                 [jax.ShapeDtypeStruct((rows, hidden), F32)],
             )[0]
             w_out = kernel_call(
-                partial(finish_out_kernel, cut),
+                partial(finish_out_kernel, cut, padded),
                 member,
                 [right],
                 [jax.ShapeDtypeStruct((hid, width), F32)],
@@ -730,41 +1045,119 @@
                 total = total + lax.ppermute(total, axis, pairs)
             return total.reshape(-1)
 
+    held = {}
+
+    def nothing(*_):
+        pass
+
+    def same(value, *_):
+        return value
+
     values = source.astype(F32)
-    weights = weights_whole()
-    passed, kept_0 = forward(0, values, weights[0])
-    out, kept_1 = forward(1, passed.astype(BF).astype(F32), weights[1])
-    cotangent = to_team(tie(cotangent, kept_0[1])).astype(F32)
-    grad, small_1, fc_1, proj_1, attn_1 = backward(1, cotangent, kept_1, weights[1], ())
-    grad = grad.astype(BF).astype(F32)
-    grad, small_0, fc_0, proj_0, attn_0 = backward(0, grad, kept_0, weights[0], (attn_1,))
-    out = from_team(out.astype(BF))
-    grad = from_team(grad.astype(BF))
-    got_out, got_grad = cross(out, [(0, 1)]), cross(grad, [(1, 0)])
-    edge = jnp.stack([pick(grad, got_out), pick(got_grad, out)]).astype(F32)
+    fetch_proj(source)
+    normed, near = enter(0, values)
+    fetch_fc(0, near)
+    attn_weights = [get_attn(0, source)]
+    cotangent = to_team(cotangent)
+    mixed = mix(0, normed, attn_weights[0], cotangent)
+    proj_weights = []
+    fetch_attn(mixed)
+    fetch_fc(1, mixed)
+    kept_0, fc_0 = forward(0, values, normed, mixed, proj_weights, same)
+    part = leave(0, kept_0[5], kept_0[7], fc_0[1])
+    attn_weights.append(get_attn(1, part))
+    passed = kept_0[5] + scatter(part) + parameters(0)[1][5]
+    values = passed.astype(BF).astype(F32)
+    normed, near = enter(1, values)
+    mixed = mix(1, normed, attn_weights[1])
+    proj_weights.append(get_proj(1))
+    grad_low = gather_late(cotangent)
+
+    def hold_low(value):
+        return tie(value, grad_low) if fast else value
+
+    kept_1, fc_1 = forward(1, values, normed, mixed, proj_weights, hold_low)
+    weights_0 = (attn_weights[0], proj_weights[0], *fc_0)
+    weights_1 = (attn_weights[1], proj_weights[1], *fc_1)
+
+    def finish_forward(part):
+        held["out"] = scatter_late(leave(1, kept_1[5], kept_1[7], fc_1[1]))
+
+    def start_fc(layer):
+        def start(grad_attended, fc_total, proj_total):
+            if fast:
+                held[layer] = over_planes(fc_total)
+
+        return start
+
+    fillers = (nothing, finish_forward, start_fc(1), same, same, same)
+    grad, small_1, fc_1, proj_1, attn_1, _ = backward(
+        1, cotangent.astype(F32), grad_low, kept_1, weights_1, fillers
+    )
+    out = (kept_1[5] + held["out"] + parameters(1)[1][5]).astype(BF)
+    grad = grad.astype(BF)
+    grad_low = gather(grad, n)
+    fillers = (nothing, nothing, start_fc(0), same, same, same)
+    if fast:
+        attn_1 = over_planes(attn_1)
+
+        held["fc_1"] = lax.all_gather(held[1], "replica", axis=0, tiled=True)
+
+        held["attn_1"] = lax.all_gather(attn_1, "replica", axis=0, tiled=True)
+
+        def hold_sums(value, proj_0):
+            held["proj"] = whole = jnp.concatenate([proj_0, proj_1], axis=1)
+            held["got"] = scatter_first(whole)
+            return tie(value, *held["got"])
+
+        def hold_attn(value):
+            return tie(value, held["attn_1"])
+
+        def hold_gathered(value):
+            return tie(value, held["fc_1"])
+
+        fillers = (nothing, nothing, start_fc(0), hold_sums, hold_gathered, hold_attn)
+    grad, small_0, fc_0, proj_0, attn_0, grad_mixed = backward(
+        0, grad.astype(F32), grad_low, kept_0, weights_0, fillers
+    )
+    grad = grad.astype(BF)
+    if fast:
+        proj = scatter(held["proj"], held["got"]).astype(BF)
+        proj = over_planes(proj)
+        attn_0 = over_planes(attn_0)
+        mine = from_team(jnp.concatenate([grad, out], axis=1))
+        edge = kernel_call(
+            partial(edge_kernel, padded),
+            section,
+            [mine, cross(mine)],
+            [jax.ShapeDtypeStruct((2, local, width), F32)],
+        )[0]
+        fc_0 = ordered(False, gather(tie(held[0], grad), cut))
+        fc = both(fc_0, held["fc_1"])
+        attn = both(ordered(False, gather(attn_0, cut)), held["attn_1"])
+        proj = both(*gather_many([proj[:, :proj_half], proj[:, proj_half:]], proj_cut))
+    else:
+        out, grad = from_team(out), from_team(grad)
+        got_out, got_grad = cross(out, [(0, 1)]), cross(grad, [(1, 0)])
+        edge = jnp.stack([pick(grad, got_out), pick(got_grad, out)]).astype(F32)
     edge = edge.reshape(1, 2, 1, local, width)
     if fast:
-        fc = [collect(layer, total, cut) for layer, total in enumerate((fc_0, fc_1))]
-        attn = [collect(layer, total, cut) for layer, total in enumerate((attn_0, attn_1))]
-        proj_cut = (slab // 32) * 16
-        proj = [
-            collect(layer, scatter(total).astype(BF), proj_cut)
-            for layer, total in enumerate((proj_0, proj_1))
-        ]
         in_sum, out_sum = finish_fc(fc)
-        proj_sum = finish(partial(finish_proj_kernel, step, slab, proj_cut), proj, (rows, width))
-        attn_sum = finish(partial(finish_attn_kernel, slots, cut), attn, (rows, 3 * width))
+        kernel = partial(finish_proj_kernel, step, slab, proj_cut, wide, padded)
+        proj_sum = finish(kernel, proj, (rows, width))
+        kernel = partial(finish_attn_kernel, slots, cut, mixed_rows)
+        attn_sum = finish(kernel, attn, (rows, 3 * width))
         small = reduce_small((small_0, small_1))
     else:
 
         def summed(make, after):
-            parts = [tie(make(layer), after) for layer in range(2)]
+            parts = [lax.optimization_barrier((make(layer), after))[0] for layer in range(2)]
             mine = pick(parts[0], parts[1]) + cross(pick(parts[1], parts[0]))
             mine = lax.psum_scatter(mine, row_axes, scatter_dimension=0, tiled=True)
             return lax.psum(mine.astype(F32), ("replica",))
 
         def attn_whole(layer):
-            value = jnp.concatenate((attn_0, attn_1)[layer], axis=1)
+            value = (attn_0, attn_1)[layer]
             zeros = jnp.zeros((width, width), BF)
             parts = [value[:, i * heads_width : (i + 1) * heads_width] for i in range(3)]
             return jnp.concatenate(
@@ -772,7 +1165,7 @@
             )
 
         def proj_whole(layer):
-            return jnp.concatenate((proj_0, proj_1)[layer], axis=1)
+            return (proj_0, proj_1)[layer]
 
         def in_whole(layer):
             zeros = jnp.zeros((width, hidden), BF)

time: 1540 us -> 1340 us (0.87)
  local copies, waits for them, and re-layouts: 266 us -> 94.7 us
  waiting for transfers between devices: 469 us -> 572 us
  starting transfers between devices: 275 us -> 177 us
  other arithmetic: 195 us -> 120 us
  Pallas kernels: 92.4 us -> 137 us
    ppermute x46 -> x34, starting transfers between devices: 117 us -> 23.4 us  [across(): return lax.ppermute(value, 'replica', ACROSS)]
    ppermute x46 -> x34, waiting for transfers between devices: 175 us -> 244 us  [side(): return lax.ppermute(value, 'replica', SIDE)]
    ppermute x13 -> x0, local copies, waits for them, and re-layouts: 56.3 us -> none  [the longest x9 47.9 us: cross(): return lax.ppermute(value, 'section', pairs)]
    ppermute x8 -> x18, waiting for transfers between devices: 17.6 us -> 71.7 us  [turned(): lax.ppermute(x, axis, pairs)]
    pallas_call x8 -> x33, Pallas kernels: 19.5 us -> 63.3 us  [kernel_call(): pl.pallas_call(kernel, in_specs=[pl.BlockSpec(memory_space=pltpu.SMEM)] +...]
    unnamed x437 -> x356, local copies, waits for them, and re-layouts: 84.4 us -> 43.1 us
    convert_element_type x12 -> x6, other arithmetic: 46.6 us -> 7.36 us  [the longest x1 3.09 us: body(): grad = grad.astype(BF)]
    concatenate x23 -> x6, local copies, waits for them, and re-layouts: 44.1 us -> 6.96 us  [the longest x1 2.77 us: body(): jnp.concatenate([jnp.pad(lax.dynamic_slice_in_dim(fc_in_weight[0], part *...]
  transfers between devices with their start and end apart: 144 -> 132, of which waited for: 54 -> 68; matrix products, arithmetic and copies ran while one was open for 37% -> 26% of each run, Pallas kernels for 6% -> 10%
where the time goes in v2:
time: 1340 us; the launch traced here: 1320 us
  waiting for transfers between devices  572 us (43%)
  matrix products  208 us (16%)
  starting transfers between devices  177 us (13%)
  Pallas kernels  137 us (10%)
  other arithmetic  120 us (9%)
  local copies, waits for them, and re-layouts  94.7 us (7%)
  between operations  16.8 us (1%)
    ppermute x34, waiting for transfers between devices, side(): return lax.ppermute(value, 'replica', SIDE)  244 us
    dot_general x30, matrix products, dot(): lax.dot_general(left, right, ((contract[:1], contract[1:]), ((), ())), pr...  208 us
    ppermute x34, waiting for transfers between devices, across(): return lax.ppermute(value, 'replica', ACROSS)  207 us
    ppermute x18, waiting for transfers between devices, turned(): lax.ppermute(x, axis, pairs)  71.7 us
    ppermute x23, starting transfers between devices, cross(): return lax.ppermute(value, 'section', pairs)  71.1 us
    pallas_call x33, Pallas kernels, kernel_call(): pl.pallas_call(kernel, in_specs=[pl.BlockSpec(memory_space=pltpu.SMEM)] +...  63.3 us
    unnamed x356, local copies, waits for them, and re-layouts  43.1 us
    all_gather x5, waiting for transfers between devices, gathered(): return lax.all_gather(piece, 'seq', axis=0, tiled=True)  40.4 us
  transfers between devices with their start and end apart: 132, of which 68 were waited for; matrix products, arithmetic and copies ran while one was open for 26% of the time, Pallas kernels for 10%

profile of v2, /device:TPU:1, one launch (start us, length us, event | category | flops | bytes accessed | tf_op | source)
XLA Modules:
  0.0 1324.5 jit_solution(17200555741780707214)
XLA Ops:
  52.1 6.0 collective-permute-done.8.refs_2_
  68.5 12.4 collective-permute-done.10.refs_1_
  82.2 8.3 collective-permute-done.12.refs_3_
  115.8 11.6 collective-permute-start.4
  130.6 15.8 %collective-permute-done.4.refs_1_ = bf16[64,1664]{1,0:T(8,128)(2,1)S(1)} collective-permute-done((bf16[64,1664]{1,0:T(8,128)(2,1)S(1)}, bf16[64,1664]{1,0:T(8,128)(2,1)S(1)}, u32[]{:S(2)}, u32[]{:S(2)}) %collective-permute-start.4) | collective-permute-done | bytes 213024 | tf_op jit(solution)/shard_map/ppermute | solution.py:563
  185.0 16.6 %shard_map.162 = (bf16[448,256]{1,0:T(8,128)(2,1)S(1)}, bf16[448,256]{1,0:T(8,128)(2,1)S(1)}, bf16[448,256]{1,0:T(8,128)(2,1)S(1)}, bf16[448,256]{1,0:T(8,128)(2,1)S(1)}, f32[7,1,1024]{2,1,0:T(1,128)S(1)}) custom-call(bf16[1408,1024]{1,0:T(8,128)(2,1)S(1)} %add_convert_fusion.7.q_ref.k_ref.v_ref.refs_1_, ...), custom_call_target="tpu_custom_call" | custom-call | flops 19730006016 | bytes 7864320 | tf_op jit(solution)/shard_map/pallas_call | solution.py:142
  208.8 28.7 %collective-permute-done.27.far_b = bf16[448,1664]{1,0:T(8,128)(2,1)} collective-permute-done((bf16[448,1664]{1,0:T(8,128)(2,1)}, bf16[448,1664]{1,0:T(8,128)(2,1)}, u32[]{:S(2)}, u32[]{:S(2)}) %collective-permute-start.27) | collective-permute-done | bytes 1490976 | tf_op jit(solution)/shard_map/ppermute | solution.py:496
  260.9 6.2 all-gather.13.cloned.1.call-done.refs_1_.refs_0_
  278.1 8.6 collective-permute-done.31.near_b
  295.0 12.3 collective-permute-done.33.far_b
  311.2 14.0 %add_convert_fusion.3 = (bf16[1024,1664]{1,0:T(8,128)(2,1)}, bf16[1024,1664]{1,0:T(8,128)(2,1)S(1)}) fusion(f32[1664]{0:T(1024)S(1)} %add.701, bf16[1024,1664]{1,0:T(8,128)(2,1)} %shard_map.172, bf16[1664,1664]{1,0:T(8,128)(2,1)} %shard_map.173, bf16[1664,1664]{1,0:T(8,128)(2,1)} %collective-permute-done.34, pred[]{:T(512)S(6)} %eq.18), kind=kOutput, calls=%fused_computation.19 | convolution fusion | flops 5707546624 | bytes 21305856 | tf_op jit(solution)/shard_map/dot_general | solution.py:23
  325.2 7.4 convolution_convert_fusion.7.refs_1_
  334.3 24.9 %collective-permute-done.35 = bf16[256,1664]{1,0:T(8,128)(2,1)S(1)} collective-permute-done((bf16[256,1664]{1,0:T(8,128)(2,1)S(1)}, bf16[256,1664]{1,0:T(8,128)(2,1)S(1)}, u32[]{:S(2)}, u32[]{:S(2)}) %collective-permute-start.35) | collective-permute-done | bytes 852000 | tf_op jit(solution)/shard_map/ppermute | solution.py:493
  360.8 18.7 %collective-permute-done.36 = bf16[128,1664]{1,0:T(8,128)(2,1)S(1)} collective-permute-done((bf16[128,1664]{1,0:T(8,128)(2,1)S(1)}, bf16[128,1664]{1,0:T(8,128)(2,1)S(1)}, u32[]{:S(2)}, u32[]{:S(2)}) %collective-permute-start.36) | collective-permute-done | bytes 426016 | tf_op jit(solution)/shard_map/ppermute | solution.py:496
  383.4 6.0 collective-permute-start.39
  406.2 13.2 collective-permute-done.43.far_b
  421.4 7.8 add_convert_fusion.6.q_ref.k_ref.v_ref
  429.2 16.6 %shard_map.177 = (bf16[448,256]{1,0:T(8,128)(2,1)S(1)}, bf16[448,256]{1,0:T(8,128)(2,1)S(1)}, bf16[448,256]{1,0:T(8,128)(2,1)S(1)}, bf16[448,256]{1,0:T(8,128)(2,1)S(1)}, f32[7,1,1024]{2,1,0:T(1,128)S(1)}) custom-call(bf16[1408,1024]{1,0:T(8,128)(2,1)S(1)} %add_convert_fusion.6.q_ref.k_ref.v_ref, bf16[1408,1024]{1,0:T(8,128)(2,1)S(1)} %add_convert_fusion.6.q_ref.k_ref.v_ref, ...), custom_call_target="tpu_custom_call" | custom-call | flops 19730006016 | bytes 7864320 | tf_op jit(solution)/shard_map/pallas_call | solution.py:142
  462.7 29.9 %all-gather.19.cloned.1.call-done.refs_0_ = bf16[1664,1664]{1,0:T(8,128)(2,1)} async-done(((bf16[416,1664]{1,0:T(8,128)(2,1)}), bf16[1664,1664]{1,0:T(8,128)(2,1)}) %all-gather.19.cloned.1.call-update) | async-done | bytes 5537808 | tf_op jit(solution)/shard_map/all_gather | solution.py:745
  495.6 9.0 collective-permute-done.49.near_b
  509.2 16.4 %collective-permute-done.51.far_b = bf16[256,1664]{1,0:T(8,128)(2,1)S(1)} collective-permute-done((bf16[256,1664]{1,0:T(8,128)(2,1)}, bf16[256,1664]{1,0:T(8,128)(2,1)S(1)}, u32[]{:S(2)}, u32[]{:S(2)}) %collective-permute-start.51) | collective-permute-done | bytes 852000 | tf_op jit(solution)/shard_map/ppermute | solution.py:496
  529.5 14.8 %add_convert_fusion.2 = (bf16[1024,1664]{1,0:T(8,128)(2,1)S(1)}, bf16[1024,1664]{1,0:T(8,128)(2,1)}) fusion(f32[1664]{0:T(1024)S(1)} %add.732, bf16[1024,1664]{1,0:T(8,128)(2,1)} %shard_map.183, bf16[1664,1664]{1,0:T(8,128)(2,1)S(1)} %copy-done.76, bf16[1664,1664]{1,0:T(8,128)(2,1)} %collective-permute-done.47, pred[]{:T(512)S(6)} %eq.18), kind=kOutput, calls=%fused_computation.16 | convolution fusion | flops 5707546624 | bytes 21305856 | tf_op jit(solution)/shard_map/dot_general | solution.py:23
  544.3 7.4 multiply_convert_fusion.1
  551.8 9.5 convolution_convert_fusion.1
  561.2 6.3 collective-permute-start.71
  567.5 10.1 convolution_convert_fusion.2.value_ref
  581.6 10.3 convolution_convert_fusion.6
  596.5 12.1 add_convert_fusion.1
  610.3 14.7 %collective-permute-done.52 = bf16[256,1664]{1,0:T(8,128)(2,1)} collective-permute-done((bf16[256,1664]{1,0:T(8,128)(2,1)}, bf16[256,1664]{1,0:T(8,128)(2,1)}, u32[]{:S(2)}, u32[]{:S(2)}) %collective-permute-start.52) | collective-permute-done | bytes 852000 | tf_op jit(solution)/shard_map/ppermute | solution.py:493
  630.6 17.2 %collective-permute-done.53 = bf16[128,1664]{1,0:T(8,128)(2,1)S(1)} collective-permute-done((bf16[128,1664]{1,0:T(8,128)(2,1)S(1)}, bf16[128,1664]{1,0:T(8,128)(2,1)S(1)}, u32[]{:S(2)}, u32[]{:S(2)}) %collective-permute-start.53) | collective-permute-done | bytes 426016 | tf_op jit(solution)/shard_map/ppermute | solution.py:496
  652.1 8.7 collective-permute-done.55
  685.8 19.5 %shard_map.185 = bf16[1408,1024]{1,0:T(8,128)(2,1)S(1)} custom-call(bf16[1408,1024]{1,0:T(8,128)(2,1)S(1)} %copy-done.55, bf16[1408,1024]{1,0:T(8,128)(2,1)S(1)} %copy-done.55, bf16[1408,1024]{1,0:T(8,128)(2,1)S(1)} %copy-done.55, f32[1024,1024]{1,0:T(8,128)S(1)} %copy-done.25, f32[7,1,1024]{2,1,0:T(1,128)S(1)} %get-tuple-element.91.lse_ref, ...), custom_call_target="tpu_custom_call" | custom-call | flops 22548578304 | bytes 10616832 | tf_op jit(solution)/shard_map/pallas_call | solution.py:165
  712.5 6.3 convolution_convert_fusion.5
  726.0 14.5 %collective-permute-done.59 = bf16[256,1664]{1,0:T(8,128)(2,1)} collective-permute-done((bf16[256,1664]{1,0:T(8,128)(2,1)}, bf16[256,1664]{1,0:T(8,128)(2,1)}, u32[]{:S(2)}, u32[]{:S(2)}) %collective-permute-start.59) | collective-permute-done | bytes 852000 | tf_op jit(solution)/shard_map/ppermute | solution.py:493
  745.2 9.0 collective-permute-done.60
  757.0 8.5 collective-permute-done.62
  770.8 7.4 collective-permute-done.64.near_b
  781.9 15.5 %collective-permute-done.66.far_b = bf16[256,1664]{1,0:T(8,128)(2,1)S(1)} collective-permute-done((bf16[256,1664]{1,0:T(8,128)(2,1)}, bf16[256,1664]{1,0:T(8,128)(2,1)S(1)}, u32[]{:S(2)}, u32[]{:S(2)}) %collective-permute-start.66) | collective-permute-done | bytes 852000 | tf_op jit(solution)/shard_map/ppermute | solution.py:496
  800.3 10.8 multiply_convert_fusion
  811.2 9.3 convolution_convert_fusion
  820.4 7.5 collective-permute-start.106
  828.0 9.8 convolution_convert_fusion.4
  840.1 36.2 %collective-permute-done.67 = bf16[256,1664]{1,0:T(8,128)(2,1)S(1)} collective-permute-done((bf16[256,1664]{1,0:T(8,128)(2,1)S(1)}, bf16[256,1664]{1,0:T(8,128)(2,1)S(1)}, u32[]{:S(2)}, u32[]{:S(2)}) %collective-permute-start.67) | collective-permute-done | bytes 852000 | tf_op jit(solution)/shard_map/ppermute | solution.py:493
  877.3 18.6 %collective-permute-done.68 = bf16[128,1664]{1,0:T(8,128)(2,1)S(1)} collective-permute-done((bf16[128,1664]{1,0:T(8,128)(2,1)S(1)}, bf16[128,1664]{1,0:T(8,128)(2,1)S(1)}, u32[]{:S(2)}, u32[]{:S(2)}) %collective-permute-start.68) | collective-permute-done | bytes 426016 | tf_op jit(solution)/shard_map/ppermute | solution.py:496
  902.1 8.9 collective-permute-done.70
  925.1 12.0 add_convert_fusion
  962.8 24.0 %collective-permute-done.74.refs_1_ = bf16[448,1792]{1,0:T(8,128)(2,1)} collective-permute-done((bf16[448,1792]{1,0:T(8,128)(2,1)}, bf16[448,1792]{1,0:T(8,128)(2,1)}, u32[]{:S(2)}, u32[]{:S(2)}) %collective-permute-start.74) | collective-permute-done | bytes 1605664 | tf_op jit(solution)/shard_map/ppermute | solution.py:493
  989.1 6.2 collective-permute-done.75.refs_2_
  1003.1 20.5 %shard_map.190 = bf16[1408,1024]{1,0:T(8,128)(2,1)S(1)} custom-call(bf16[1408,1024]{1,0:T(8,128)(2,1)S(1)} %copy-done.18, bf16[1408,1024]{1,0:T(8,128)(2,1)S(1)} %copy-done.18, bf16[1408,1024]{1,0:T(8,128)(2,1)S(1)} %copy-done.18, f32[1024,1024]{1,0:T(8,128)S(1)} %copy-done.26, f32[7,1,1024]{2,1,0:T(1,128)S(1)} %copy-done.47, ...), custom_call_target="tpu_custom_call" | custom-call | flops 22548578304 | bytes 10616832 | tf_op jit(solution)/shard_map/pallas_call | solution.py:165
  1023.7 6.3 convolution_convert_fusion.3
  1041.6 11.0 collective-permute-done.99
  1055.4 15.4 %collective-permute-done.79 = bf16[256,1664]{1,0:T(8,128)(2,1)} collective-permute-done((bf16[256,1664]{1,0:T(8,128)(2,1)}, bf16[256,1664]{1,0:T(8,128)(2,1)}, u32[]{:S(2)}, u32[]{:S(2)}) %collective-permute-start.79) | collective-permute-done | bytes 852000 | tf_op jit(solution)/shard_map/ppermute | solution.py:493
  1073.6 9.5 collective-permute-done.80
  1098.7 7.2 add_convert_fusion.8
  1115.1 11.2 collective-permute-done.108.near_b
  1138.2 19.5 %collective-permute-done.110.far_b = bf16[416,1664]{1,0:T(8,128)(2,1)S(1)} collective-permute-done((bf16[416,1664]{1,0:T(8,128)(2,1)S(1)}, bf16[416,1664]{1,0:T(8,128)(2,1)S(1)}, u32[]{:S(2)}, u32[]{:S(2)}) %collective-permute-start.110) | collective-permute-done | bytes 1384480 | tf_op jit(solution)/shard_map/ppermute | solution.py:496
  1171.5 9.4 collective-permute-start.112
  1186.5 8.2 collective-permute-start.116
  1199.4 14.8 %collective-permute-done.88.refs_2_ = bf16[64,3328]{1,0:T(8,128)(2,1)S(1)} collective-permute-done((bf16[64,3328]{1,0:T(8,128)(2,1)}, bf16[64,3328]{1,0:T(8,128)(2,1)S(1)}, u32[]{:S(2)}, u32[]{:S(2)}) %collective-permute-start.88) | collective-permute-done | bytes 426016 | tf_op jit(solution)/shard_map/ppermute | solution.py:563
  1220.6 5.8 collective-permute-done.101.near_b
  1235.3 6.8 collective-permute-done.93.near_b
  1259.5 12.0 collective-permute-start.105
  1276.4 5.6 shard_map.205
  1290.7 5.8 collective-permute-start.97
  (888 shorter events, 512.9 us)
Async XLA Ops:
  7.2 94.2 %all-gather.9.cloned.1.call-start = ((), (), s32[]{:S(2)}) async-start(), calls=%async_computation.6 | async-start | bytes 3194880 | tf_op jit(solution)/shard_map/all_gather | solution.py:745
  14.4 23.8 %collective-permute-start = (bf16[256,1664]{1,0:T(8,128)(2,1)}, bf16[256,1664]{1,0:T(8,128)(2,1)}, u32[]{:S(2)}, u32[]{:S(2)}) collective-permute-start(bf16[256,1664]{1,0:T(8,128)(2,1)} %broadcast_select_fusion.31), channel_id=1, source_target_pairs={{0,16},{16,0},{1,17},{17,1},{2,18},{18,2},{3,19},{19,3},{4,20},{20... | collective-permute-start | bytes 2555912 | tf_op jit(solution)/shard_map/ppermute | solution.py:490
  22.2 41.8 %collective-permute-start.15 = (f32[19200]{0:T(1024)}, f32[19200]{0:T(1024)}, u32[]{:S(2)}, u32[]{:S(2)}) collective-permute-start(f32[19200]{0:T(1024)} %pad_maximum_fusion.31), channel_id=1, source_target_pairs={{0,16},{16,0},{1,17},{17,1},{2,18},{18,2},{3,19},{19,3},{4,20},{20... | collective-permute-start | bytes 230408 | tf_op jit(solution)/shard_map/ppermute | solution.py:490
  22.3 27.9 %collective-permute-start.20 = (s32[1024]{0:T(1024)S(1)}, s32[1024]{0:T(1024)S(1)}, u32[]{:S(2)}, u32[]{:S(2)}) collective-permute-start(s32[1024]{0:T(1024)S(1)} %bitcast.124), channel_id=1, source_target_pairs={{0,0},{1,4},{2,8},{3,12},{4,1},{5,5},{6,9},{7,13},{8,2},{9,6},{10,... | collective-permute-start | bytes 12296 | tf_op jit(solution)/shard_map/ppermute | solution.py:870
  25.9 144.3 %all-gather.11.cloned.1.call-start = ((), (), s32[]{:S(2)}) async-start(), calls=%async_computation.7 | async-start | bytes 1863680 | tf_op jit(solution)/shard_map/all_gather | solution.py:745
  50.2 109.9 %collective-permute-start.29 = (bf16[416,1664]{1,0:T(8,128)(2,1)}, bf16[416,1664]{1,0:T(8,128)(2,1)}, u32[]{:S(2)}, u32[]{:S(2)}) collective-permute-start(bf16[416,1664]{1,0:T(8,128)(2,1)} %broadcast_select_fusion.26), channel_id=1, source_target_pairs={{0,16},{16,0},{1,17},{17,1},{2,18},{18,2},{3,19},{19,3},{4,20},{20... | collective-permute-start | bytes 4153352 | tf_op jit(solution)/shard_map/ppermute | solution.py:490
  61.9 28.5 %collective-permute-start.12 = (bf16[64,1664]{1,0:T(8,128)(2,1)}, bf16[64,1664]{1,0:T(8,128)(2,1)S(1)}, u32[]{:S(2)}, u32[]{:S(2)}) collective-permute-start(bf16[64,1664]{1,0:T(8,128)(2,1)} %get-tuple-element.77), channel_id=1, source_target_pairs={{0,3},{3,0},{1,2},{2,1},{4,7},{7,4},{5,6},{6,5},{8,11},{11,8},{9,1... | collective-permute-start | bytes 638984 | tf_op jit(solution)/shard_map/ppermute | solution.py:563
  67.4 34.9 %collective-permute-start.1 = (bf16[64,1664]{1,0:T(8,128)(2,1)}, bf16[64,1664]{1,0:T(8,128)(2,1)S(1)}, u32[]{:S(2)}, u32[]{:S(2)}) collective-permute-start(bf16[64,1664]{1,0:T(8,128)(2,1)} %get-tuple-element.63), channel_id=1, source_target_pairs={{0,4},{4,0},{8,12},{12,8},{1,5},{5,1},{9,13},{13,9},{2,6},{6,2},{1... | collective-permute-start | bytes 638984 | tf_op jit(solution)/shard_map/ppermute | solution.py:563
  80.8 24.2 %collective-permute-start.2 = (bf16[64,1664]{1,0:T(8,128)(2,1)}, bf16[64,1664]{1,0:T(8,128)(2,1)}, u32[]{:S(2)}, u32[]{:S(2)}) collective-permute-start(bf16[64,1664]{1,0:T(8,128)(2,1)} %get-tuple-element.64), channel_id=1, source_target_pairs={{0,8},{8,0},{4,12},{12,4},{1,9},{9,1},{5,13},{13,5},{2,10},{10,2},... | collective-permute-start | bytes 638984 | tf_op jit(solution)/shard_map/ppermute | solution.py:563
  93.9 173.2 %all-gather.13.cloned.1.call-start = ((), (), s32[]{:S(2)}) async-start(), calls=%async_computation.8 | async-start | bytes 6922240 | tf_op jit(solution)/shard_map/all_gather | solution.py:745
  96.1 31.3 %collective-permute-start.17 = (bf16[128,1664]{1,0:T(8,128)(2,1)}, bf16[128,1664]{1,0:T(8,128)(2,1)S(1)}, u32[]{:S(2)}, u32[]{:S(2)}) collective-permute-start(bf16[128,1664]{1,0:T(8,128)(2,1)} %get-tuple-element.219), channel_id=1, source_target_pairs={{0,4},{4,0},{8,12},{12,8},{1,5},{5,1},{9,13},{13,9},{2,6},{6,2},{1... | collective-permute-start | bytes 1277960 | tf_op jit(solution)/shard_map/ppermute | solution.py:493
  101.4 72.1 %collective-permute-start.14 = (bf16[1664,768]{1,0:T(8,128)(2,1)}, bf16[1664,768]{1,0:T(8,128)(2,1)}, u32[]{:S(2)}, u32[]{:S(2)}) collective-permute-start(bf16[1664,768]{1,0:T(8,128)(2,1)} %shard_map.159), channel_id=1, source_target_pairs={{0,16},{16,0},{1,17},{17,1},{2,18},{18,2},{3,19},{19,3},{4,20},{20... | collective-permute-start | bytes 7667720 | tf_op jit(solution)/shard_map/ppermute | solution.py:490
  105.1 24.4 %collective-permute-start.16 = (bf16[128,1664]{1,0:T(8,128)(2,1)}, bf16[128,1664]{1,0:T(8,128)(2,1)S(1)}, u32[]{:S(2)}, u32[]{:S(2)}) collective-permute-start(bf16[128,1664]{1,0:T(8,128)(2,1)} %get-tuple-element.220), channel_id=1, source_target_pairs={{0,8},{8,0},{4,12},{12,4},{1,9},{9,1},{5,13},{13,5},{2,10},{10,2},... | collective-permute-start | bytes 1277960 | tf_op jit(solution)/shard_map/ppermute | solution.py:496
  115.8 30.6 %collective-permute-start.4 = (bf16[64,1664]{1,0:T(8,128)(2,1)S(1)}, bf16[64,1664]{1,0:T(8,128)(2,1)S(1)}, u32[]{:S(2)}, u32[]{:S(2)}) collective-permute-start(bf16[64,1664]{1,0:T(8,128)(2,1)S(1)} %get-tuple-element.67), channel_id=1, source_target_pairs={{0,1},{1,0},{2,3},{3,2},{4,5},{5,4},{6,7},{7,6},{8,9},{9,8},{10,11... | collective-permute-start | bytes 638984 | tf_op jit(solution)/shard_map/ppermute | solution.py:563
  127.4 22.4 %collective-permute-start.5 = (bf16[64,1664]{1,0:T(8,128)(2,1)S(1)}, bf16[64,1664]{1,0:T(8,128)(2,1)S(1)}, u32[]{:S(2)}, u32[]{:S(2)}) collective-permute-start(bf16[64,1664]{1,0:T(8,128)(2,1)S(1)} %get-tuple-element.68), channel_id=1, source_target_pairs={{0,2},{2,0},{1,3},{3,1},{4,6},{6,4},{5,7},{7,5},{8,10},{10,8},{9,1... | collective-permute-start | bytes 638984 | tf_op jit(solution)/shard_map/ppermute | solution.py:563
  129.5 34.4 %collective-permute-start.19 = (bf16[256,1664]{1,0:T(8,128)(2,1)}, bf16[256,1664]{1,0:T(8,128)(2,1)}, u32[]{:S(2)}, u32[]{:S(2)}) collective-permute-start(bf16[256,1664]{1,0:T(8,128)(2,1)} %pad_maximum_fusion.17), channel_id=1, source_target_pairs={{0,8},{8,0},{4,12},{12,4},{1,9},{9,1},{5,13},{13,5},{2,10},{10,2},... | collective-permute-start | bytes 2555912 | tf_op jit(solution)/shard_map/ppermute | solution.py:496
  163.6 219.7 %all-gather.15.cloned.1.call-start = ((), (), s32[]{:S(2)}) async-start(), calls=%async_computation.9 | async-start | bytes 3194880 | tf_op jit(solution)/shard_map/all_gather | solution.py:745
  172.7 29.5 %collective-permute-start.25 = (bf16[224,1664]{1,0:T(8,128)(2,1)S(1)}, bf16[224,1664]{1,0:T(8,128)(2,1)S(1)}, u32[]{:S(2)}, u32[]{:S(2)}) collective-permute-start(bf16[224,1664]{1,0:T(8,128)(2,1)S(1)} %get-tuple-element.206), channel_id=1, source_target_pairs={{0,4},{4,0},{8,12},{12,8},{1,5},{5,1},{9,13},{13,9},{2,6},{6,2},{1... | collective-permute-start | bytes 2236424 | tf_op jit(solution)/shard_map/ppermute | solution.py:493
  172.8 33.4 %collective-permute-start.24 = (bf16[224,1664]{1,0:T(8,128)(2,1)}, bf16[224,1664]{1,0:T(8,128)(2,1)}, u32[]{:S(2)}, u32[]{:S(2)}) collective-permute-start(bf16[224,1664]{1,0:T(8,128)(2,1)} %get-tuple-element.207), channel_id=1, source_target_pairs={{0,8},{8,0},{4,12},{12,4},{1,9},{9,1},{5,13},{13,5},{2,10},{10,2},... | collective-permute-start | bytes 2236424 | tf_op jit(solution)/shard_map/ppermute | solution.py:496
  205.4 32.1 %collective-permute-start.27 = (bf16[448,1664]{1,0:T(8,128)(2,1)}, bf16[448,1664]{1,0:T(8,128)(2,1)}, u32[]{:S(2)}, u32[]{:S(2)}) collective-permute-start(bf16[448,1664]{1,0:T(8,128)(2,1)} %pad_maximum_fusion.13), channel_id=1, source_target_pairs={{0,8},{8,0},{4,12},{12,4},{1,9},{9,1},{5,13},{13,5},{2,10},{10,2},... | collective-permute-start | bytes 4472840 | tf_op jit(solution)/shard_map/ppermute | solution.py:496
  207.7 31.7 %collective-permute-start.26 = (bf16[448,1664]{1,0:T(8,128)(2,1)S(1)}, bf16[448,1664]{1,0:T(8,128)(2,1)S(1)}, u32[]{:S(2)}, u32[]{:S(2)}) collective-permute-start(bf16[448,1664]{1,0:T(8,128)(2,1)S(1)} %pad_maximum_fusion.12), channel_id=1, source_target_pairs={{0,4},{4,0},{8,12},{12,8},{1,5},{5,1},{9,13},{13,9},{2,6},{6,2},{1... | collective-permute-start | bytes 4472840 | tf_op jit(solution)/shard_map/ppermute | solution.py:493
  244.0 23.1 %collective-permute-start.28 = (bf16[1792,1664]{1,0:T(8,128)(2,1)}, bf16[1792,1664]{1,0:T(8,128)(2,1)}, u32[]{:S(2)}, u32[]{:S(2)}) collective-permute-start(bf16[1792,1664]{1,0:T(8,128)(2,1)} %shard_map.169), channel_id=1, source_target_pairs={{0,16},{16,0},{1,17},{17,1},{2,18},{18,2},{3,19},{19,3},{4,20},{20... | collective-permute-start | bytes 17891336 | tf_op jit(solution)/shard_map/ppermute | solution.py:490
  274.5 36.7 %collective-permute-start.34 = (bf16[1664,1664]{1,0:T(8,128)(2,1)}, bf16[1664,1664]{1,0:T(8,128)(2,1)}, u32[]{:S(2)}, u32[]{:S(2)}) collective-permute-start(bf16[1664,1664]{1,0:T(8,128)(2,1)} %shard_map.173), channel_id=1, source_target_pairs={{0,16},{16,0},{1,17},{17,1},{2,18},{18,2},{3,19},{19,3},{4,20},{20... | collective-permute-start | bytes 16613384 | tf_op jit(solution)/shard_map/ppermute | solution.py:490
  275.0 174.3 %all-gather.17.cloned.1.call-start = ((), (), s32[]{:S(2)}) async-start(), calls=%async_computation.10 | async-start | bytes 4259840 | tf_op jit(solution)/shard_map/all_gather | solution.py:635
  294.9 197.7 %all-gather.19.cloned.1.call-start = ((), (), s32[]{:S(2)}) async-start(), calls=%async_computation.11 | async-start | bytes 6922240 | tf_op jit(solution)/shard_map/all_gather | solution.py:745
  332.8 26.4 %collective-permute-start.35 = (bf16[256,1664]{1,0:T(8,128)(2,1)S(1)}, bf16[256,1664]{1,0:T(8,128)(2,1)S(1)}, u32[]{:S(2)}, u32[]{:S(2)}) collective-permute-start(bf16[256,1664]{1,0:T(8,128)(2,1)S(1)} %get-tuple-element.197), channel_id=1, source_target_pairs={{0,4},{4,0},{8,12},{12,8},{1,5},{5,1},{9,13},{13,9},{2,6},{6,2},{1... | collective-permute-start | bytes 2555912 | tf_op jit(solution)/shard_map/ppermute | solution.py:493
  334.0 26.7 %collective-permute-start.37 = (bf16[256,1664]{1,0:T(8,128)(2,1)S(1)}, bf16[256,1664]{1,0:T(8,128)(2,1)S(1)}, u32[]{:S(2)}, u32[]{:S(2)}) collective-permute-start(bf16[256,1664]{1,0:T(8,128)(2,1)S(1)} %get-tuple-element.198), channel_id=1, source_target_pairs={{0,8},{8,0},{4,12},{12,4},{1,9},{9,1},{5,13},{13,5},{2,10},{10,2},... | collective-permute-start | bytes 2555912 | tf_op jit(solution)/shard_map/ppermute | solution.py:496
  383.1 281.1 %reduce-scatter.11.cloned.1.call-start = ((), (), s32[]{:S(2)}) async-start(), calls=%async_computation.16 | async-start | bytes 4259840 | tf_op jit(solution)/shard_map/reduce_scatter | solution.py:642
  492.6 36.8 %collective-permute-start.47 = (bf16[1664,1664]{1,0:T(8,128)(2,1)}, bf16[1664,1664]{1,0:T(8,128)(2,1)}, u32[]{:S(2)}, u32[]{:S(2)}) collective-permute-start(bf16[1664,1664]{1,0:T(8,128)(2,1)} %shard_map.182), channel_id=1, source_target_pairs={{0,16},{16,0},{1,17},{17,1},{2,18},{18,2},{3,19},{19,3},{4,20},{20... | collective-permute-start | bytes 16613384 | tf_op jit(solution)/shard_map/ppermute | solution.py:490
  561.2 35.1 %collective-permute-start.71 = (bf16[1664,1664]{1,0:T(8,128)(2,1)}, bf16[1664,1664]{1,0:T(8,128)(2,1)}, u32[]{:S(2)}, u32[]{:S(2)}) collective-permute-start(bf16[1664,1664]{1,0:T(8,128)(2,1)} %convolution_convert_fusion.1), channel_id=1, source_target_pairs={{0,16},{16,0},{1,17},{17,1},{2,18},{18,2},{3,19},{19,3},{4,20},{20... | collective-permute-start | bytes 16613384 | tf_op jit(solution)/shard_map/ppermute | solution.py:490
  581.6 200.2 %reduce-scatter.7.cloned.1.call-start = ((), (), s32[]{:S(2)}) async-start(), calls=%async_computation.12 | async-start | bytes 6922240 | tf_op jit(solution)/shard_map/reduce_scatter | solution.py:1008
  595.2 29.8 %collective-permute-start.52 = (bf16[256,1664]{1,0:T(8,128)(2,1)}, bf16[256,1664]{1,0:T(8,128)(2,1)}, u32[]{:S(2)}, u32[]{:S(2)}) collective-permute-start(bf16[256,1664]{1,0:T(8,128)(2,1)} %get-tuple-element.193), channel_id=1, source_target_pairs={{0,4},{4,0},{8,12},{12,8},{1,5},{5,1},{9,13},{13,9},{2,6},{6,2},{1... | collective-permute-start | bytes 2555912 | tf_op jit(solution)/shard_map/ppermute | solution.py:493
  608.6 290.1 %reduce-scatter.9.cloned.1.call-start = ((), (), s32[]{:S(2)}) async-start(), calls=%async_computation.14 | async-start | bytes 3194880 | tf_op jit(solution)/shard_map/reduce_scatter | solution.py:1008
  626.2 21.7 %collective-permute-start.53 = (bf16[128,1664]{1,0:T(8,128)(2,1)S(1)}, bf16[128,1664]{1,0:T(8,128)(2,1)S(1)}, u32[]{:S(2)}, u32[]{:S(2)}) collective-permute-start(bf16[128,1664]{1,0:T(8,128)(2,1)S(1)} %add_convert_fusion.24), channel_id=1, source_target_pairs={{0,8},{8,0},{4,12},{12,4},{1,9},{9,1},{5,13},{13,5},{2,10},{10,2},... | collective-permute-start | bytes 1277960 | tf_op jit(solution)/shard_map/ppermute | solution.py:496
  724.8 188.2 %all-gather.21.cloned.1.call-start = ((), (), s32[]{:S(2)}) async-start(), calls=%async_computation.13 | async-start | bytes 6922240 | tf_op jit(solution)/shard_map/all_gather | solution.py:1104
  781.8 310.0 %all-gather.23.cloned.1.call-start = ((), (), s32[]{:S(2)}) async-start(), calls=%async_computation.15 | async-start | bytes 3194880 | tf_op jit(solution)/shard_map/all_gather | solution.py:1106
  820.4 103.1 %collective-permute-start.106 = (bf16[1664,1664]{1,0:T(8,128)(2,1)}, bf16[1664,1664]{1,0:T(8,128)(2,1)}, u32[]{:S(2)}, u32[]{:S(2)}) collective-permute-start(bf16[1664,1664]{1,0:T(8,128)(2,1)} %convolution_convert_fusion), channel_id=1, source_target_pairs={{0,16},{16,0},{1,17},{17,1},{2,18},{18,2},{3,19},{19,3},{4,20},{20... | collective-permute-start | bytes 16613384 | tf_op jit(solution)/shard_map/ppermute | solution.py:490
  837.9 38.4 %collective-permute-start.67 = (bf16[256,1664]{1,0:T(8,128)(2,1)S(1)}, bf16[256,1664]{1,0:T(8,128)(2,1)S(1)}, u32[]{:S(2)}, u32[]{:S(2)}) collective-permute-start(bf16[256,1664]{1,0:T(8,128)(2,1)S(1)} %get-tuple-element.187), channel_id=1, source_target_pairs={{0,4},{4,0},{8,12},{12,8},{1,5},{5,1},{9,13},{13,9},{2,6},{6,2},{1... | collective-permute-start | bytes 2555912 | tf_op jit(solution)/shard_map/ppermute | solution.py:493
  838.8 38.6 %collective-permute-start.69 = (bf16[256,1664]{1,0:T(8,128)(2,1)S(1)}, bf16[256,1664]{1,0:T(8,128)(2,1)S(1)}, u32[]{:S(2)}, u32[]{:S(2)}) collective-permute-start(bf16[256,1664]{1,0:T(8,128)(2,1)S(1)} %get-tuple-element.188), channel_id=1, source_target_pairs={{0,8},{8,0},{4,12},{12,4},{1,9},{9,1},{5,13},{13,5},{2,10},{10,2},... | collective-permute-start | bytes 2555912 | tf_op jit(solution)/shard_map/ppermute | solution.py:496
  898.7 210.2 %reduce-scatter.17.cloned.1.call-start = ((), (), s32[]{:S(2)}) async-start(), calls=%async_computation.19 | async-start | bytes 6922240 | tf_op jit(solution)/shard_map/reduce_scatter | solution.py:1008
  902.1 35.1 %collective-permute-start.73 = (bf16[1792,896]{1,0:T(8,128)(2,1)}, bf16[1792,896]{1,0:T(8,128)(2,1)}, u32[]{:S(2)}, u32[]{:S(2)}) collective-permute-start(bf16[1792,896]{1,0:T(8,128)(2,1)} %convolution_convert_fusion.8), channel_id=1, source_target_pairs={{0,16},{16,0},{1,17},{17,1},{2,18},{18,2},{3,19},{19,3},{4,20},{20... | collective-permute-start | bytes 9633800 | tf_op jit(solution)/shard_map/ppermute | solution.py:490
  937.2 260.9 %reduce-scatter.15.cloned.1.call-start = ((), (), s32[]{:S(2)}) async-start(), calls=%async_computation.18 | async-start | bytes 2007040 | tf_op jit(solution)/shard_map/reduce_scatter | solution.py:1008
  948.9 37.9 %collective-permute-start.74 = (bf16[448,1792]{1,0:T(8,128)(2,1)}, bf16[448,1792]{1,0:T(8,128)(2,1)}, u32[]{:S(2)}, u32[]{:S(2)}) collective-permute-start(bf16[448,1792]{1,0:T(8,128)(2,1)} %get-tuple-element.173), channel_id=1, source_target_pairs={{0,4},{4,0},{8,12},{12,8},{1,5},{5,1},{9,13},{13,9},{2,6},{6,2},{1... | collective-permute-start | bytes 4816904 | tf_op jit(solution)/shard_map/ppermute | solution.py:493
  952.8 42.4 %collective-permute-start.75 = (bf16[448,1792]{1,0:T(8,128)(2,1)}, bf16[448,1792]{1,0:T(8,128)(2,1)}, u32[]{:S(2)}, u32[]{:S(2)}) collective-permute-start(bf16[448,1792]{1,0:T(8,128)(2,1)} %get-tuple-element.172), channel_id=1, source_target_pairs={{0,8},{8,0},{4,12},{12,4},{1,9},{9,1},{5,13},{13,5},{2,10},{10,2},... | collective-permute-start | bytes 4816904 | tf_op jit(solution)/shard_map/ppermute | solution.py:496
  960.1 35.1 %collective-permute-start.76 = (bf16[448,256]{1,0:T(8,128)(2,1)}, bf16[448,256]{1,0:T(8,128)(2,1)S(1)}, u32[]{:S(2)}, u32[]{:S(2)}) collective-permute-start(bf16[448,256]{1,0:T(8,128)(2,1)} %get-tuple-element.99), channel_id=1, source_target_pairs={{0,4},{4,0},{8,12},{12,8},{1,5},{5,1},{9,13},{13,9},{2,6},{6,2},{1... | collective-permute-start | bytes 688136 | tf_op jit(solution)/shard_map/ppermute | solution.py:493
  961.0 39.1 %collective-permute-start.77 = (bf16[448,256]{1,0:T(8,128)(2,1)}, bf16[448,256]{1,0:T(8,128)(2,1)}, u32[]{:S(2)}, u32[]{:S(2)}) collective-permute-start(bf16[448,256]{1,0:T(8,128)(2,1)} %get-tuple-element.100), channel_id=1, source_target_pairs={{0,8},{8,0},{4,12},{12,4},{1,9},{9,1},{5,13},{13,5},{2,10},{10,2},... | collective-permute-start | bytes 688136 | tf_op jit(solution)/shard_map/ppermute | solution.py:496
  961.9 38.3 %collective-permute-start.78 = (bf16[448,256]{1,0:T(8,128)(2,1)}, bf16[448,256]{1,0:T(8,128)(2,1)}, u32[]{:S(2)}, u32[]{:S(2)}) collective-permute-start(bf16[448,256]{1,0:T(8,128)(2,1)} %get-tuple-element.101), channel_id=1, source_target_pairs={{0,12},{12,0},{4,8},{8,4},{1,13},{13,1},{5,9},{9,5},{2,14},{14,2},... | collective-permute-start | bytes 688136 | tf_op jit(solution)/shard_map/ppermute | solution.py:499
  989.1 40.9 %collective-permute-start.98 = (bf16[224,1792]{1,0:T(8,128)(2,1)}, bf16[224,1792]{1,0:T(8,128)(2,1)}, u32[]{:S(2)}, u32[]{:S(2)}) collective-permute-start(bf16[224,1792]{1,0:T(8,128)(2,1)} %add_convert_fusion.16), channel_id=1, source_target_pairs={{0,8},{8,0},{4,12},{12,4},{1,9},{9,1},{5,13},{13,5},{2,10},{10,2},... | collective-permute-start | bytes 2408456 | tf_op jit(solution)/shard_map/ppermute | solution.py:496
  1035.7 35.1 %collective-permute-start.79 = (bf16[256,1664]{1,0:T(8,128)(2,1)}, bf16[256,1664]{1,0:T(8,128)(2,1)}, u32[]{:S(2)}, u32[]{:S(2)}) collective-permute-start(bf16[256,1664]{1,0:T(8,128)(2,1)} %get-tuple-element.184), channel_id=1, source_target_pairs={{0,4},{4,0},{8,12},{12,8},{1,5},{5,1},{9,13},{13,9},{2,6},{6,2},{1... | collective-permute-start | bytes 2555912 | tf_op jit(solution)/shard_map/ppermute | solution.py:493
  1040.6 33.0 %collective-permute-start.81 = (bf16[256,1664]{1,0:T(8,128)(2,1)}, bf16[256,1664]{1,0:T(8,128)(2,1)}, u32[]{:S(2)}, u32[]{:S(2)}) collective-permute-start(bf16[256,1664]{1,0:T(8,128)(2,1)} %get-tuple-element.185), channel_id=1, source_target_pairs={{0,8},{8,0},{4,12},{12,4},{1,9},{9,1},{5,13},{13,5},{2,10},{10,2},... | collective-permute-start | bytes 2555912 | tf_op jit(solution)/shard_map/ppermute | solution.py:496
  1040.6 58.0 %collective-permute-start.91 = (bf16[1664,768]{1,0:T(8,128)(2,1)}, bf16[1664,768]{1,0:T(8,128)(2,1)}, u32[]{:S(2)}, u32[]{:S(2)}) collective-permute-start(bf16[1664,768]{1,0:T(8,128)(2,1)} %convolution_convert_fusion.10), channel_id=1, source_target_pairs={{0,16},{16,0},{1,17},{17,1},{2,18},{18,2},{3,19},{19,3},{4,20},{20... | collective-permute-start | bytes 7667720 | tf_op jit(solution)/shard_map/ppermute | solution.py:490
  1055.3 174.7 %reduce-scatter.13.cloned.1.call-start = ((), (), s32[]{:S(2)}) async-start(), calls=%async_computation.17 | async-start | bytes 3194880 | tf_op jit(solution)/shard_map/reduce_scatter | solution.py:1008
  1092.2 167.3 %collective-permute-start.111 = (bf16[1664,1664]{1,0:T(8,128)(2,1)}, bf16[1664,1664]{1,0:T(8,128)(2,1)}, u32[]{:S(2)}, u32[]{:S(2)}) collective-permute-start(bf16[1664,1664]{1,0:T(8,128)(2,1)} %all-gather.21.cloned.1.call-done.refs_1_), channel_id=1, source_target_pairs={{0,16},{1,17},{2,18},{3,19},{4,20},{5,21},{6,22},{7,23},{8,24},{9,... | collective-permute-start | bytes 16613384 | tf_op jit(solution)/shard_map/ppermute | solution.py:490
  1127.7 30.0 %collective-permute-start.110 = (bf16[416,1664]{1,0:T(8,128)(2,1)S(1)}, bf16[416,1664]{1,0:T(8,128)(2,1)S(1)}, u32[]{:S(2)}, u32[]{:S(2)}) collective-permute-start(bf16[416,1664]{1,0:T(8,128)(2,1)S(1)} %pad_maximum_fusion.15), channel_id=1, source_target_pairs={{0,8},{8,0},{4,12},{12,4},{1,9},{9,1},{5,13},{13,5},{2,10},{10,2},... | collective-permute-start | bytes 4153352 | tf_op jit(solution)/shard_map/ppermute | solution.py:496
  1131.7 29.0 %collective-permute-start.109 = (bf16[416,1664]{1,0:T(8,128)(2,1)}, bf16[416,1664]{1,0:T(8,128)(2,1)S(1)}, u32[]{:S(2)}, u32[]{:S(2)}) collective-permute-start(bf16[416,1664]{1,0:T(8,128)(2,1)} %pad_maximum_fusion.14), channel_id=1, source_target_pairs={{0,4},{4,0},{8,12},{12,8},{1,5},{5,1},{9,13},{13,9},{2,6},{6,2},{1... | collective-permute-start | bytes 4153352 | tf_op jit(solution)/shard_map/ppermute | solution.py:493
  1137.0 44.0 %collective-permute-start.84 = (bf16[64,3328]{1,0:T(8,128)(2,1)S(1)}, bf16[64,3328]{1,0:T(8,128)(2,1)S(1)}, u32[]{:S(2)}, u32[]{:S(2)}) collective-permute-start(bf16[64,3328]{1,0:T(8,128)(2,1)S(1)} %get-tuple-element.103), channel_id=1, source_target_pairs={{0,1},{1,0},{2,3},{3,2},{4,5},{5,4},{6,7},{7,6},{8,9},{9,8},{10,11... | collective-permute-start | bytes 1277960 | tf_op jit(solution)/shard_map/ppermute | solution.py:563
  1137.6 43.4 %collective-permute-start.85 = (bf16[64,3328]{1,0:T(8,128)(2,1)S(1)}, bf16[64,3328]{1,0:T(8,128)(2,1)S(1)}, u32[]{:S(2)}, u32[]{:S(2)}) collective-permute-start(bf16[64,3328]{1,0:T(8,128)(2,1)S(1)} %get-tuple-element.104), channel_id=1, source_target_pairs={{0,2},{2,0},{1,3},{3,1},{4,6},{6,4},{5,7},{7,5},{8,10},{10,8},{9,1... | collective-permute-start | bytes 1277960 | tf_op jit(solution)/shard_map/ppermute | solution.py:563
  1157.7 26.5 %collective-permute-start.86 = (bf16[64,3328]{1,0:T(8,128)(2,1)S(1)}, bf16[64,3328]{1,0:T(8,128)(2,1)S(1)}, u32[]{:S(2)}, u32[]{:S(2)}) collective-permute-start(bf16[64,3328]{1,0:T(8,128)(2,1)S(1)} %get-tuple-element.105), channel_id=1, source_target_pairs={{0,3},{3,0},{1,2},{2,1},{4,7},{7,4},{5,6},{6,5},{8,11},{11,8},{9,1... | collective-permute-start | bytes 1277960 | tf_op jit(solution)/shard_map/ppermute | solution.py:563
  1171.5 131.4 %collective-permute-start.112 = (bf16[1664,1664]{1,0:T(8,128)(2,1)}, bf16[1664,1664]{1,0:T(8,128)(2,1)}, u32[]{:S(2)}, u32[]{:S(2)}) collective-permute-start(bf16[1664,1664]{1,0:T(8,128)(2,1)} %shard_map.204), channel_id=1, source_target_pairs={{16,0},{17,1},{18,2},{19,3},{20,4},{21,5},{22,6},{23,7},{24,8},{25... | collective-permute-start | bytes 16613384 | tf_op jit(solution)/shard_map/ppermute | solution.py:490
  1215.4 56.1 %collective-permute-start.90 = (bf16[256,3328]{1,0:T(8,128)(2,1)S(1)}, bf16[256,3328]{1,0:T(8,128)(2,1)S(1)}, u32[]{:S(2)}, u32[]{:S(2)}) collective-permute-start(bf16[256,3328]{1,0:T(8,128)(2,1)S(1)} %shard_map.195.mine_ref), channel_id=1, source_target_pairs={{0,16},{16,0},{1,17},{17,1},{2,18},{18,2},{3,19},{19,3},{4,20},{20... | collective-permute-start | bytes 5111816 | tf_op jit(solution)/shard_map/ppermute | solution.py:490
  1245.2 27.8 %collective-permute-start.95 = (bf16[416,768]{1,0:T(8,128)(2,1)}, bf16[416,768]{1,0:T(8,128)(2,1)}, u32[]{:S(2)}, u32[]{:S(2)}) collective-permute-start(bf16[416,768]{1,0:T(8,128)(2,1)} %pad_maximum_fusion.28), channel_id=1, source_target_pairs={{0,8},{8,0},{4,12},{12,4},{1,9},{9,1},{5,13},{13,5},{2,10},{10,2},... | collective-permute-start | bytes 1916936 | tf_op jit(solution)/shard_map/ppermute | solution.py:496
  1248.0 52.9 %collective-permute-start.96 = (bf16[1664,768]{1,0:T(8,128)(2,1)}, bf16[1664,768]{1,0:T(8,128)(2,1)}, u32[]{:S(2)}, u32[]{:S(2)}) collective-permute-start(bf16[1664,768]{1,0:T(8,128)(2,1)} %all-gather.23.cloned.1.call-done.refs_1_), channel_id=1, source_target_pairs={{0,16},{1,17},{2,18},{3,19},{4,20},{5,21},{6,22},{7,23},{8,24},{9,... | collective-permute-start | bytes 7667720 | tf_op jit(solution)/shard_map/ppermute | solution.py:490
  1259.5 37.0 %collective-permute-start.105 = (bf16[448,896]{1,0:T(8,128)(2,1)}, bf16[448,896]{1,0:T(8,128)(2,1)}, u32[]{:S(2)}, u32[]{:S(2)}) collective-permute-start(bf16[448,896]{1,0:T(8,128)(2,1)} %get-tuple-element.110), channel_id=1, source_target_pairs={{16,0},{17,1},{18,2},{19,3},{20,4},{21,5},{22,6},{23,7},{24,8},{25... | collective-permute-start | bytes 2408456 | tf_op jit(solution)/shard_map/ppermute | solution.py:490
  1271.5 26.3 %collective-permute-start.104 = (bf16[448,896]{1,0:T(8,128)(2,1)}, bf16[448,896]{1,0:T(8,128)(2,1)}, u32[]{:S(2)}, u32[]{:S(2)}) collective-permute-start(bf16[448,896]{1,0:T(8,128)(2,1)} %get-tuple-element.111), channel_id=1, source_target_pairs={{0,16},{1,17},{2,18},{3,19},{4,20},{5,21},{6,22},{7,23},{8,24},{9,... | collective-permute-start | bytes 2408456 | tf_op jit(solution)/shard_map/ppermute | solution.py:490
  (242 other events, 2923.5 us)
Sparse Core Ops, SparseCore 0:
  26.0 75.2 all-gather.8
  102.9 42.1 all-gather.10
  163.8 103.3 all-gather.12
  275.1 51.4 all-gather.14
  328.4 63.3 all-gather.16
  393.2 99.3 all-gather.18
  581.7 66.4 reduce-scatter.10
  651.1 97.6 reduce-scatter.6
  751.7 51.3 reduce-scatter.8
  805.0 90.5 all-gather.20
  898.9 37.8 all-gather.22
  939.6 98.5 reduce-scatter.16
  1055.5 33.3 reduce-scatter.14
  1106.0 64.7 reduce-scatter.12

commit v3 on v2

--- a/solution.py
+++ b/solution.py
@@ -309,8 +309,8 @@
                 ]
 
 
-def finish_proj_kernel(step, slab, cut, total, padded, member_ref, left_ref, right_ref, out_ref):
-    member = member_ref[0]
+def finish_proj_kernel(step, slab, cut, total, padded, _, left_ref, right_ref, out_ref):
+    member = None
     block = out_ref.shape[1] // 4
     for owner in range(4):
         size = slab if owner == 3 else step
@@ -359,7 +359,7 @@
 
 
 def edge_kernel(padded, section_ref, mine_ref, other_ref, edge_ref):
-    block = edge_ref.shape[2] // 4
+    block = edge_ref.shape[4] // 4
     wide = 4 * padded
     for side, refs in enumerate(((mine_ref, other_ref), (other_ref, mine_ref))):
 
@@ -367,7 +367,7 @@
         def _(side=side, refs=refs):
             for index, ref in enumerate(refs):
                 value = ref[:, side * wide : (side + 1) * wide].astype(F32)
-                blocks_into(edge_ref.at[index], slice(None), value, block, padded)
+                blocks_into(edge_ref.at[0, index, 0], slice(None), value, block, padded)
 
 
 def order_kernel(forth, place_ref, value_ref, out_ref):
@@ -419,6 +419,27 @@
             out_ref[at : at + size, :] = part[first : first + size, column : column + width]
             column += width
         at += size
+
+
+def place_kernel(widths, member_ref, *refs):
+    pieces, outs = refs[:4], refs[4:]
+    rows = pieces[0].shape[0]
+    for turn in range(4):
+        at = pl.multiple_of((member_ref[0] ^ turn) * rows, 16)
+        column = 0
+        for width, out_ref in zip(widths, outs):
+            out_ref[pl.ds(at, rows), :] = pieces[turn][:, column : column + width]
+            column += width
+
+
+def total_kernel(place_ref, *refs):
+    pieces, out_ref = refs[:4], refs[4]
+    for place in range(4):
+
+        @pl.when(place_ref[0] == place)
+        def _(place=place):
+            first, second, third, fourth = (pieces[place ^ turn][...] for turn in range(4))
+            out_ref[...] = ((first + second) + third) + fourth
 
 
 def same_kernel(*refs):
@@ -624,6 +645,16 @@
     def gather_many(values, cut):
         whole = jnp.concatenate(values, axis=1)
         return gather_near(whole, cut, [value.shape[1] for value in values])[0]
+
+    def gather_direct(value, widths=None):
+        pieces = [value, side(value), across(value), corner(value)]
+        widths = widths or [value.shape[1]]
+        rows = 4 * value.shape[0]
+        outs = [jax.ShapeDtypeStruct((rows, width), value.dtype) for width in widths]
+        return kernel_call(partial(place_kernel, widths), member, pieces, outs)
+
+    def edge_of(value):
+        return lax.slice(value, (0, 0), (16, 128))
 
     def ordered(forth, value):
         out = jax.ShapeDtypeStruct(value.shape, value.dtype)
@@ -1036,13 +1067,9 @@
         def reduce_small(small):
             total = pick(small[0], small[1]) + cross(pick(small[1], small[0]))
             total = total.reshape(-1, 128)
-            for axis, pairs in (
-                ("replica", SIDE),
-                ("replica", ACROSS),
-                ("seq", SIDE),
-                ("seq", CORNER),
-            ):
-                total = total + lax.ppermute(total, axis, pairs)
+            out = [jax.ShapeDtypeStruct(total.shape, F32)]
+            total = kernel_call(total_kernel, member, turned([total] * 4, "replica"), out)[0]
+            total = kernel_call(total_kernel, plane, turned([total] * 4, "seq"), out)[0]
             return total.reshape(-1)
 
     held = {}
@@ -1071,10 +1098,10 @@
     normed, near = enter(1, values)
     mixed = mix(1, normed, attn_weights[1])
     proj_weights.append(get_proj(1))
-    grad_low = gather_late(cotangent)
+    grad_low = gather_late(tie(cotangent, edge_of(mixed)) if fast else cotangent)
 
     def hold_low(value):
-        return tie(value, grad_low) if fast else value
+        return value
 
     kept_1, fc_1 = forward(1, values, normed, mixed, proj_weights, hold_low)
     weights_0 = (attn_weights[0], proj_weights[0], *fc_0)
@@ -1124,18 +1151,19 @@
     if fast:
         proj = scatter(held["proj"], held["got"]).astype(BF)
         proj = over_planes(proj)
+        attn_last = attn_0
         attn_0 = over_planes(attn_0)
         mine = from_team(jnp.concatenate([grad, out], axis=1))
         edge = kernel_call(
             partial(edge_kernel, padded),
             section,
             [mine, cross(mine)],
-            [jax.ShapeDtypeStruct((2, local, width), F32)],
+            [jax.ShapeDtypeStruct((1, 2, 1, local, width), F32)],
         )[0]
-        fc_0 = ordered(False, gather(tie(held[0], grad), cut))
+        fc_0 = lax.all_gather(tie(held[0], edge_of(attn_last)), "replica", axis=0, tiled=True)
         fc = both(fc_0, held["fc_1"])
-        attn = both(ordered(False, gather(attn_0, cut)), held["attn_1"])
-        proj = both(*gather_many([proj[:, :proj_half], proj[:, proj_half:]], proj_cut))
+        attn = both(gather_direct(attn_0)[0], held["attn_1"])
+        proj = both(*gather_direct(proj, [proj_half, proj_half]))
     else:
         out, grad = from_team(out), from_team(grad)
         got_out, got_grad = cross(out, [(0, 1)]), cross(grad, [(1, 0)])

time: 1340 us -> 1310 us (0.978)
  starting transfers between devices: 177 us -> 194 us
    ppermute x34 -> x30, waiting for transfers between devices: 207 us -> 165 us  [across(): return lax.ppermute(value, 'replica', ACROSS)]
    ppermute x18 -> x24, waiting for transfers between devices: 71.7 us -> 112 us  [turned(): lax.ppermute(x, axis, pairs)]
    ppermute x34 -> x30, waiting for transfers between devices: 244 us -> 207 us  [side(): return lax.ppermute(value, 'replica', SIDE)]
    reduce_scatter x5, waiting for transfers between devices: 0.01 us -> 15.2 us  [over_planes(): return lax.psum_scatter(total, 'seq', scatter_dimension=0, tiled=True)]
    ppermute x18 -> x24, starting transfers between devices: 32.3 us -> 44 us  [turned(): lax.ppermute(x, axis, pairs)]
    pallas_call x33 -> x32, Pallas kernels: 63.3 us -> 52.5 us  [kernel_call(): pl.pallas_call(kernel, in_specs=[pl.BlockSpec(memory_space=pltpu.SMEM)] +...]
    ppermute x34 -> x30, starting transfers between devices: 23.4 us -> 33.7 us  [across(): return lax.ppermute(value, 'replica', ACROSS)]
    unnamed x356 -> x340, local copies, waits for them, and re-layouts: 43.1 us -> 38.2 us
  transfers between devices with their start and end apart: 132 -> 129, of which waited for: 68 -> 69; matrix products, arithmetic and copies ran while one was open for 26% -> 25% of each run, Pallas kernels for 10% -> 9%
where the time goes in v3:
time: 1310 us; the launch traced here: 1300 us
  waiting for transfers between devices  560 us (43%)
  matrix products  217 us (17%)
  starting transfers between devices  194 us (15%)
  Pallas kernels  127 us (10%)
  other arithmetic  107 us (8%)
  local copies, waits for them, and re-layouts  82.8 us (6%)
  between operations  16.7 us (1%)
    dot_general x30, matrix products, dot(): lax.dot_general(left, right, ((contract[:1], contract[1:]), ((), ())), pr...  217 us
    ppermute x30, waiting for transfers between devices, side(): return lax.ppermute(value, 'replica', SIDE)  207 us
    ppermute x30, waiting for transfers between devices, across(): return lax.ppermute(value, 'replica', ACROSS)  165 us
    ppermute x24, waiting for transfers between devices, turned(): lax.ppermute(x, axis, pairs)  112 us
    ppermute x23, starting transfers between devices, cross(): return lax.ppermute(value, 'section', pairs)  74.3 us
    pallas_call x32, Pallas kernels, kernel_call(): pl.pallas_call(kernel, in_specs=[pl.BlockSpec(memory_space=pltpu.SMEM)] +...  52.5 us
    ppermute x24, starting transfers between devices, turned(): lax.ppermute(x, axis, pairs)  44 us
    pallas_call x2, Pallas kernels, attend_back(): pl.pallas_call(partial(attend_back_kernel, grouped), grid=(slots,), in_sp...  39.3 us
  transfers between devices with their start and end apart: 129, of which 69 were waited for; matrix products, arithmetic and copies ran while one was open for 25% of the time, Pallas kernels for 9%

profile of v3, /device:TPU:1, one launch (start us, length us, event | category | flops | bytes accessed | tf_op | source)
XLA Modules:
  0.0 1303.4 jit_solution(15958887716127357109)
XLA Ops:
  45.3 5.3 collective-permute-start.7
  72.1 13.2 %collective-permute-done.10.refs_1_ = bf16[64,1664]{1,0:T(8,128)(2,1)S(1)} collective-permute-done((bf16[64,1664]{1,0:T(8,128)(2,1)}, bf16[64,1664]{1,0:T(8,128)(2,1)S(1)}, u32[]{:S(2)}, u32[]{:S(2)}) %collective-permute-start.10) | collective-permute-done | bytes 213024 | tf_op jit(solution)/shard_map/ppermute | solution.py:584
  87.5 7.0 collective-permute-done.12.refs_3_
  106.7 6.3 collective-permute-done.3.refs_3_
  117.3 10.6 collective-permute-start.4
  131.5 15.6 %collective-permute-done.4.refs_1_ = bf16[64,1664]{1,0:T(8,128)(2,1)S(1)} collective-permute-done((bf16[64,1664]{1,0:T(8,128)(2,1)S(1)}, bf16[64,1664]{1,0:T(8,128)(2,1)S(1)}, u32[]{:S(2)}, u32[]{:S(2)}) %collective-permute-start.4) | collective-permute-done | bytes 213024 | tf_op jit(solution)/shard_map/ppermute | solution.py:584
  180.6 5.7 add_convert_fusion.7.q_ref.k_ref.v_ref.refs_1_
  186.3 17.6 %shard_map.162 = (bf16[448,256]{1,0:T(8,128)(2,1)S(1)}, bf16[448,256]{1,0:T(8,128)(2,1)}, bf16[448,256]{1,0:T(8,128)(2,1)S(1)}, bf16[448,256]{1,0:T(8,128)(2,1)S(1)}, f32[7,1,1024]{2,1,0:T(1,128)S(1)}) custom-call(bf16[1408,1024]{1,0:T(8,128)(2,1)S(1)} %add_convert_fusion.7.q_ref.k_ref.v_ref.refs_1_, ...), custom_call_target="tpu_custom_call" | custom-call | flops 19730006016 | bytes 7864320 | tf_op jit(solution)/shard_map/pallas_call | solution.py:142
  210.7 29.4 %collective-permute-done.27.far_b = bf16[448,1664]{1,0:T(8,128)(2,1)} collective-permute-done((bf16[448,1664]{1,0:T(8,128)(2,1)}, bf16[448,1664]{1,0:T(8,128)(2,1)}, u32[]{:S(2)}, u32[]{:S(2)}) %collective-permute-start.27) | collective-permute-done | bytes 1490976 | tf_op jit(solution)/shard_map/ppermute | solution.py:517
  278.9 8.5 collective-permute-done.31.near_b
  293.6 14.2 %collective-permute-done.33.far_b = bf16[256,1664]{1,0:T(8,128)(2,1)S(1)} collective-permute-done((bf16[256,1664]{1,0:T(8,128)(2,1)}, bf16[256,1664]{1,0:T(8,128)(2,1)S(1)}, u32[]{:S(2)}, u32[]{:S(2)}) %collective-permute-start.33) | collective-permute-done | bytes 852000 | tf_op jit(solution)/shard_map/ppermute | solution.py:517
  313.0 14.0 %add_convert_fusion.3 = (bf16[1024,1664]{1,0:T(8,128)(2,1)}, bf16[1024,1664]{1,0:T(8,128)(2,1)S(1)}) fusion(f32[1664]{0:T(1024)S(1)} %add.689, bf16[1024,1664]{1,0:T(8,128)(2,1)} %shard_map.172, bf16[1664,1664]{1,0:T(8,128)(2,1)} %shard_map.173, bf16[1664,1664]{1,0:T(8,128)(2,1)} %collective-permute-done.34, pred[]{:T(512)S(6)} %eq.18), kind=kOutput, calls=%fused_computation.19 | convolution fusion | flops 5707546624 | bytes 21305856 | tf_op jit(solution)/shard_map/dot_general | solution.py:23
  327.1 7.5 convolution_convert_fusion.7.refs_1_
  336.3 12.7 collective-permute-done.35
  349.9 11.2 collective-permute-done.36
  385.4 12.5 collective-permute-done.43.far_b
  399.8 7.8 add_convert_fusion.6.q_ref.k_ref.v_ref
  407.6 17.1 %shard_map.177 = (bf16[448,256]{1,0:T(8,128)(2,1)S(1)}, bf16[448,256]{1,0:T(8,128)(2,1)S(1)}, bf16[448,256]{1,0:T(8,128)(2,1)S(1)}, bf16[448,256]{1,0:T(8,128)(2,1)S(1)}, f32[7,1,1024]{2,1,0:T(1,128)S(1)}) custom-call(bf16[1408,1024]{1,0:T(8,128)(2,1)S(1)} %add_convert_fusion.6.q_ref.k_ref.v_ref, bf16[1408,1024]{1,0:T(8,128)(2,1)S(1)} %add_convert_fusion.6.q_ref.k_ref.v_ref, ...), custom_call_target="tpu_custom_call" | custom-call | flops 19730006016 | bytes 7864320 | tf_op jit(solution)/shard_map/pallas_call | solution.py:142
  443.7 24.8 %all-gather.20.cloned.1.call-done.refs_0_ = bf16[1664,1664]{1,0:T(8,128)(2,1)} async-done(((bf16[416,1664]{1,0:T(8,128)(2,1)}), bf16[1664,1664]{1,0:T(8,128)(2,1)}) %all-gather.20.cloned.1.call-update) | async-done | bytes 5537808 | tf_op jit(solution)/shard_map/all_gather | solution.py:776
  473.8 12.1 collective-permute-done.49.near_b
  491.2 27.2 %collective-permute-done.51.far_b = bf16[256,1664]{1,0:T(8,128)(2,1)} collective-permute-done((bf16[256,1664]{1,0:T(8,128)(2,1)}, bf16[256,1664]{1,0:T(8,128)(2,1)}, u32[]{:S(2)}, u32[]{:S(2)}) %collective-permute-start.51) | collective-permute-done | bytes 852000 | tf_op jit(solution)/shard_map/ppermute | solution.py:517
  521.8 8.5 all-gather.18.cloned.1.call-done.value_ref
  532.7 15.5 %add_convert_fusion.2 = (bf16[1024,1664]{1,0:T(8,128)(2,1)S(1)}, bf16[1024,1664]{1,0:T(8,128)(2,1)}) fusion(f32[1664]{0:T(1024)S(1)} %add.720, bf16[1024,1664]{1,0:T(8,128)(2,1)} %shard_map.183, bf16[1664,1664]{1,0:T(8,128)(2,1)} %shard_map.182, bf16[1664,1664]{1,0:T(8,128)(2,1)} %collective-permute-done.47, pred[]{:T(512)S(6)} %eq.18), kind=kOutput, calls=%fused_computation.16 | convolution fusion | flops 5707546624 | bytes 21305856 | tf_op jit(solution)/shard_map/dot_general | solution.py:23
  548.2 7.4 multiply_convert_fusion.1
  555.6 12.3 convolution_convert_fusion.1
  570.9 10.1 convolution_convert_fusion.2.value_ref
  585.1 10.3 convolution_convert_fusion.6
  597.9 30.4 %collective-permute-done.52 = bf16[256,1664]{1,0:T(8,128)(2,1)S(1)} collective-permute-done((bf16[256,1664]{1,0:T(8,128)(2,1)S(1)}, bf16[256,1664]{1,0:T(8,128)(2,1)S(1)}, u32[]{:S(2)}, u32[]{:S(2)}) %collective-permute-start.52) | collective-permute-done | bytes 852000 | tf_op jit(solution)/shard_map/ppermute | solution.py:514
  630.4 12.7 add_convert_fusion.1
  651.8 9.1 collective-permute-done.55
  689.8 19.6 %shard_map.185 = bf16[1408,1024]{1,0:T(8,128)(2,1)S(1)} custom-call(bf16[1408,1024]{1,0:T(8,128)(2,1)S(1)} %copy-done.61, bf16[1408,1024]{1,0:T(8,128)(2,1)S(1)} %copy-done.61, bf16[1408,1024]{1,0:T(8,128)(2,1)S(1)} %copy-done.61, f32[1024,1024]{1,0:T(8,128)S(1)} %copy-done.24, f32[7,1,1024]{2,1,0:T(1,128)S(1)} %get-tuple-element.91.lse_ref, ...), custom_call_target="tpu_custom_call" | custom-call | flops 22548578304 | bytes 10616832 | tf_op jit(solution)/shard_map/pallas_call | solution.py:165
  709.5 6.3 convolution_convert_fusion.5
  718.3 15.6 %collective-permute-done.59 = bf16[256,1664]{1,0:T(8,128)(2,1)S(1)} collective-permute-done((bf16[256,1664]{1,0:T(8,128)(2,1)S(1)}, bf16[256,1664]{1,0:T(8,128)(2,1)S(1)}, u32[]{:S(2)}, u32[]{:S(2)}) %collective-permute-start.59) | collective-permute-done | bytes 852000 | tf_op jit(solution)/shard_map/ppermute | solution.py:514
  735.4 8.6 collective-permute-done.60
  745.6 7.3 collective-permute-done.62
  767.8 6.9 convolution_convert_fusion.11
  774.7 10.0 collective-permute-start.83
  784.7 16.1 %collective-permute-done.66.far_b = bf16[256,1664]{1,0:T(8,128)(2,1)S(1)} collective-permute-done((bf16[256,1664]{1,0:T(8,128)(2,1)S(1)}, bf16[256,1664]{1,0:T(8,128)(2,1)S(1)}, u32[]{:S(2)}, u32[]{:S(2)}) %collective-permute-start.66) | collective-permute-done | bytes 852000 | tf_op jit(solution)/shard_map/ppermute | solution.py:517
  802.8 9.9 multiply_convert_fusion
  812.7 9.1 convolution_convert_fusion
  821.8 8.1 collective-permute-start.104
  829.8 6.2 add_convert_fusion.9
  838.9 13.5 %add_convert_fusion = bf16[1664,1664]{1,0:T(8,128)(2,1)} fusion(bf16[1664,1664]{1,0:T(8,128)(2,1)} %collective-permute-done.104, bf16[1024,1664]{1,0:T(8,128)(2,1)} %copy-done.95, bf16[1024,1664]{1,0:T(8,128)(2,1)} %shard_map.186, bf16[1024,1664]{1,0:T(8,128)(2,1)} %shard_map.172, bf16[1024,1664]{1,0:T(8,128)(2,1)} %copy-done.157, pred[]{:T(512)S(6)} %eq.18), kind=kOutput, calls=%fused_computation | convolution fusion | flops 5682413568 | bytes 24707072 | tf_op jit(solution)/shard_map/dot_general | solution.py:23
  852.8 10.2 convolution_convert_fusion.4
  866.1 17.4 %collective-permute-done.67 = bf16[256,1664]{1,0:T(8,128)(2,1)S(1)} collective-permute-done((bf16[256,1664]{1,0:T(8,128)(2,1)S(1)}, bf16[256,1664]{1,0:T(8,128)(2,1)S(1)}, u32[]{:S(2)}, u32[]{:S(2)}) %collective-permute-start.67) | collective-permute-done | bytes 852000 | tf_op jit(solution)/shard_map/ppermute | solution.py:514
  885.1 8.7 collective-permute-done.68
  927.4 33.7 %collective-permute-done.74.refs_1_ = bf16[448,1792]{1,0:T(8,128)(2,1)S(1)} collective-permute-done((bf16[448,1792]{1,0:T(8,128)(2,1)}, bf16[448,1792]{1,0:T(8,128)(2,1)S(1)}, u32[]{:S(2)}, u32[]{:S(2)}) %collective-permute-start.74) | collective-permute-done | bytes 1605664 | tf_op jit(solution)/shard_map/ppermute | solution.py:514
  973.1 14.3 %collective-permute-done.97 = bf16[224,1792]{1,0:T(8,128)(2,1)} collective-permute-done((bf16[224,1792]{1,0:T(8,128)(2,1)}, bf16[224,1792]{1,0:T(8,128)(2,1)}, u32[]{:S(2)}, u32[]{:S(2)}) %collective-permute-start.97) | collective-permute-done | bytes 802848 | tf_op jit(solution)/shard_map/ppermute | solution.py:517
  992.3 19.6 %shard_map.190 = bf16[1408,1024]{1,0:T(8,128)(2,1)S(1)} custom-call(bf16[1408,1024]{1,0:T(8,128)(2,1)S(1)} %copy-done.17, bf16[1408,1024]{1,0:T(8,128)(2,1)S(1)} %copy-done.17, bf16[1408,1024]{1,0:T(8,128)(2,1)S(1)} %copy-done.17, f32[1024,1024]{1,0:T(8,128)S(1)} %copy-done.25, f32[7,1,1024]{2,1,0:T(1,128)S(1)} %copy-done.49, ...), custom_call_target="tpu_custom_call" | custom-call | flops 22548578304 | bytes 10616832 | tf_op jit(solution)/shard_map/pallas_call | solution.py:165
  1024.3 8.0 add_convert_fusion.8
  1034.1 8.4 convolution_convert_fusion.3
  1044.2 18.7 %collective-permute-done.79 = bf16[256,1664]{1,0:T(8,128)(2,1)S(1)} collective-permute-done((bf16[256,1664]{1,0:T(8,128)(2,1)S(1)}, bf16[256,1664]{1,0:T(8,128)(2,1)S(1)}, u32[]{:S(2)}, u32[]{:S(2)}) %collective-permute-start.79) | collective-permute-done | bytes 852000 | tf_op jit(solution)/shard_map/ppermute | solution.py:514
  1064.5 9.0 collective-permute-done.80
  1094.7 11.4 collective-permute-done.84.refs_1_
  1106.1 9.2 collective-permute-done.86.refs_3_
  1125.7 8.0 collective-permute-done.87.refs_1_
  1136.3 15.2 %collective-permute-done.89.refs_3_ = bf16[64,3328]{1,0:T(8,128)(2,1)S(1)} collective-permute-done((bf16[64,3328]{1,0:T(8,128)(2,1)S(1)}, bf16[64,3328]{1,0:T(8,128)(2,1)S(1)}, u32[]{:S(2)}, u32[]{:S(2)}) %collective-permute-start.89) | collective-permute-done | bytes 426016 | tf_op jit(solution)/shard_map/ppermute | solution.py:584
  1151.6 7.3 collective-permute-start.90
  1187.3 9.6 collective-permute-start.106
  1200.4 15.2 %reduce-scatter.13.cloned.1.call-done.refs_0_ = bf16[416,768]{1,0:T(8,128)(2,1)} async-done(((bf16[1664,768]{1,0:T(8,128)(2,1)}), bf16[416,768]{1,0:T(8,128)(2,1)}) %reduce-scatter.13.cloned.1.call-update) | async-done | bytes 638992 | tf_op jit(solution)/shard_map/reduce_scatter | solution.py:1039
  1218.7 12.1 collective-permute-done.92.refs_1_
  1261.7 6.9 collective-permute-start.96
  1278.2 5.6 shard_map.202
  1290.8 5.5 shard_map.203
  (856 shorter events, 499.0 us)
Async XLA Ops:
  7.2 93.7 %all-gather.10.cloned.1.call-start = ((), (), s32[]{:S(2)}) async-start(), calls=%async_computation.6 | async-start | bytes 3194880 | tf_op jit(solution)/shard_map/all_gather | solution.py:776
  14.3 28.9 %collective-permute-start = (bf16[256,1664]{1,0:T(8,128)(2,1)}, bf16[256,1664]{1,0:T(8,128)(2,1)}, u32[]{:S(2)}, u32[]{:S(2)}) collective-permute-start(bf16[256,1664]{1,0:T(8,128)(2,1)} %broadcast_select_fusion.31), channel_id=1, source_target_pairs={{0,16},{16,0},{1,17},{17,1},{2,18},{18,2},{3,19},{19,3},{4,20},{20... | collective-permute-start | bytes 2555912 | tf_op jit(solution)/shard_map/ppermute | solution.py:511
  22.2 46.1 %collective-permute-start.15 = (f32[19200]{0:T(1024)}, f32[19200]{0:T(1024)}, u32[]{:S(2)}, u32[]{:S(2)}) collective-permute-start(f32[19200]{0:T(1024)} %pad_maximum_fusion.25), channel_id=1, source_target_pairs={{0,16},{16,0},{1,17},{17,1},{2,18},{18,2},{3,19},{19,3},{4,20},{20... | collective-permute-start | bytes 230408 | tf_op jit(solution)/shard_map/ppermute | solution.py:511
  22.2 33.3 %collective-permute-start.20 = (s32[1024]{0:T(1024)S(1)}, s32[1024]{0:T(1024)S(1)}, u32[]{:S(2)}, u32[]{:S(2)}) collective-permute-start(s32[1024]{0:T(1024)S(1)} %bitcast.122), channel_id=1, source_target_pairs={{0,0},{1,4},{2,8},{3,12},{4,1},{5,5},{6,9},{7,13},{8,2},{9,6},{10,... | collective-permute-start | bytes 12296 | tf_op jit(solution)/shard_map/ppermute | solution.py:901
  27.1 143.8 %all-gather.12.cloned.1.call-start = ((), (), s32[]{:S(2)}) async-start(), calls=%async_computation.7 | async-start | bytes 1863680 | tf_op jit(solution)/shard_map/all_gather | solution.py:776
  55.6 105.6 %collective-permute-start.29 = (bf16[416,1664]{1,0:T(8,128)(2,1)}, bf16[416,1664]{1,0:T(8,128)(2,1)}, u32[]{:S(2)}, u32[]{:S(2)}) collective-permute-start(bf16[416,1664]{1,0:T(8,128)(2,1)} %broadcast_select_fusion.26), channel_id=1, source_target_pairs={{0,16},{16,0},{1,17},{17,1},{2,18},{18,2},{3,19},{19,3},{4,20},{20... | collective-permute-start | bytes 4153352 | tf_op jit(solution)/shard_map/ppermute | solution.py:511
  64.7 20.6 %collective-permute-start.10 = (bf16[64,1664]{1,0:T(8,128)(2,1)}, bf16[64,1664]{1,0:T(8,128)(2,1)S(1)}, u32[]{:S(2)}, u32[]{:S(2)}) collective-permute-start(bf16[64,1664]{1,0:T(8,128)(2,1)} %get-tuple-element.75), channel_id=1, source_target_pairs={{0,1},{1,0},{2,3},{3,2},{4,5},{5,4},{6,7},{7,6},{8,9},{9,8},{10,11... | collective-permute-start | bytes 638984 | tf_op jit(solution)/shard_map/ppermute | solution.py:584
  64.8 22.7 %collective-permute-start.11 = (bf16[64,1664]{1,0:T(8,128)(2,1)}, bf16[64,1664]{1,0:T(8,128)(2,1)S(1)}, u32[]{:S(2)}, u32[]{:S(2)}) collective-permute-start(bf16[64,1664]{1,0:T(8,128)(2,1)} %get-tuple-element.76), channel_id=1, source_target_pairs={{0,2},{2,0},{1,3},{3,1},{4,6},{6,4},{5,7},{7,5},{8,10},{10,8},{9,1... | collective-permute-start | bytes 638984 | tf_op jit(solution)/shard_map/ppermute | solution.py:584
  66.1 28.5 %collective-permute-start.12 = (bf16[64,1664]{1,0:T(8,128)(2,1)}, bf16[64,1664]{1,0:T(8,128)(2,1)S(1)}, u32[]{:S(2)}, u32[]{:S(2)}) collective-permute-start(bf16[64,1664]{1,0:T(8,128)(2,1)} %get-tuple-element.77), channel_id=1, source_target_pairs={{0,3},{3,0},{1,2},{2,1},{4,7},{7,4},{5,6},{6,5},{8,11},{11,8},{9,1... | collective-permute-start | bytes 638984 | tf_op jit(solution)/shard_map/ppermute | solution.py:584
  70.9 31.3 %collective-permute-start.1 = (bf16[64,1664]{1,0:T(8,128)(2,1)}, bf16[64,1664]{1,0:T(8,128)(2,1)S(1)}, u32[]{:S(2)}, u32[]{:S(2)}) collective-permute-start(bf16[64,1664]{1,0:T(8,128)(2,1)} %get-tuple-element.63), channel_id=1, source_target_pairs={{0,4},{4,0},{8,12},{12,8},{1,5},{5,1},{9,13},{13,9},{2,6},{6,2},{1... | collective-permute-start | bytes 638984 | tf_op jit(solution)/shard_map/ppermute | solution.py:584
  97.5 170.5 %all-gather.14.cloned.1.call-start = ((), (), s32[]{:S(2)}) async-start(), calls=%async_computation.8 | async-start | bytes 6922240 | tf_op jit(solution)/shard_map/all_gather | solution.py:776
  99.0 29.0 %collective-permute-start.17 = (bf16[128,1664]{1,0:T(8,128)(2,1)}, bf16[128,1664]{1,0:T(8,128)(2,1)S(1)}, u32[]{:S(2)}, u32[]{:S(2)}) collective-permute-start(bf16[128,1664]{1,0:T(8,128)(2,1)} %get-tuple-element.217), channel_id=1, source_target_pairs={{0,4},{4,0},{8,12},{12,8},{1,5},{5,1},{9,13},{13,9},{2,6},{6,2},{1... | collective-permute-start | bytes 1277960 | tf_op jit(solution)/shard_map/ppermute | solution.py:514
  100.9 73.6 %collective-permute-start.14 = (bf16[1664,768]{1,0:T(8,128)(2,1)}, bf16[1664,768]{1,0:T(8,128)(2,1)}, u32[]{:S(2)}, u32[]{:S(2)}) collective-permute-start(bf16[1664,768]{1,0:T(8,128)(2,1)} %shard_map.159), channel_id=1, source_target_pairs={{0,16},{16,0},{1,17},{17,1},{2,18},{18,2},{3,19},{19,3},{4,20},{20... | collective-permute-start | bytes 7667720 | tf_op jit(solution)/shard_map/ppermute | solution.py:511
  105.2 24.8 %collective-permute-start.16 = (bf16[128,1664]{1,0:T(8,128)(2,1)}, bf16[128,1664]{1,0:T(8,128)(2,1)S(1)}, u32[]{:S(2)}, u32[]{:S(2)}) collective-permute-start(bf16[128,1664]{1,0:T(8,128)(2,1)} %get-tuple-element.218), channel_id=1, source_target_pairs={{0,8},{8,0},{4,12},{12,4},{1,9},{9,1},{5,13},{13,5},{2,10},{10,2},... | collective-permute-start | bytes 1277960 | tf_op jit(solution)/shard_map/ppermute | solution.py:517
  117.3 29.7 %collective-permute-start.4 = (bf16[64,1664]{1,0:T(8,128)(2,1)S(1)}, bf16[64,1664]{1,0:T(8,128)(2,1)S(1)}, u32[]{:S(2)}, u32[]{:S(2)}) collective-permute-start(bf16[64,1664]{1,0:T(8,128)(2,1)S(1)} %get-tuple-element.67), channel_id=1, source_target_pairs={{0,1},{1,0},{2,3},{3,2},{4,5},{5,4},{6,7},{7,6},{8,9},{9,8},{10,11... | collective-permute-start | bytes 638984 | tf_op jit(solution)/shard_map/ppermute | solution.py:584
  127.9 22.7 %collective-permute-start.5 = (bf16[64,1664]{1,0:T(8,128)(2,1)S(1)}, bf16[64,1664]{1,0:T(8,128)(2,1)S(1)}, u32[]{:S(2)}, u32[]{:S(2)}) collective-permute-start(bf16[64,1664]{1,0:T(8,128)(2,1)S(1)} %get-tuple-element.68), channel_id=1, source_target_pairs={{0,2},{2,0},{1,3},{3,1},{4,6},{6,4},{5,7},{7,5},{8,10},{10,8},{9,1... | collective-permute-start | bytes 638984 | tf_op jit(solution)/shard_map/ppermute | solution.py:584
  130.1 34.9 %collective-permute-start.19 = (bf16[256,1664]{1,0:T(8,128)(2,1)}, bf16[256,1664]{1,0:T(8,128)(2,1)}, u32[]{:S(2)}, u32[]{:S(2)}) collective-permute-start(bf16[256,1664]{1,0:T(8,128)(2,1)} %pad_maximum_fusion.15), channel_id=1, source_target_pairs={{0,8},{8,0},{4,12},{12,4},{1,9},{9,1},{5,13},{13,5},{2,10},{10,2},... | collective-permute-start | bytes 2555912 | tf_op jit(solution)/shard_map/ppermute | solution.py:517
  147.1 20.4 %collective-permute-start.18 = (bf16[256,1664]{1,0:T(8,128)(2,1)}, bf16[256,1664]{1,0:T(8,128)(2,1)}, u32[]{:S(2)}, u32[]{:S(2)}) collective-permute-start(bf16[256,1664]{1,0:T(8,128)(2,1)} %pad_maximum_fusion.14), channel_id=1, source_target_pairs={{0,4},{4,0},{8,12},{12,8},{1,5},{5,1},{9,13},{13,9},{2,6},{6,2},{1... | collective-permute-start | bytes 2555912 | tf_op jit(solution)/shard_map/ppermute | solution.py:514
  164.7 199.3 %all-gather.16.cloned.1.call-start = ((), (), s32[]{:S(2)}) async-start(), calls=%async_computation.9 | async-start | bytes 3194880 | tf_op jit(solution)/shard_map/all_gather | solution.py:776
  173.3 31.1 %collective-permute-start.25 = (bf16[224,1664]{1,0:T(8,128)(2,1)S(1)}, bf16[224,1664]{1,0:T(8,128)(2,1)S(1)}, u32[]{:S(2)}, u32[]{:S(2)}) collective-permute-start(bf16[224,1664]{1,0:T(8,128)(2,1)S(1)} %get-tuple-element.206), channel_id=1, source_target_pairs={{0,4},{4,0},{8,12},{12,8},{1,5},{5,1},{9,13},{13,9},{2,6},{6,2},{1... | collective-permute-start | bytes 2236424 | tf_op jit(solution)/shard_map/ppermute | solution.py:514
  173.9 34.5 %collective-permute-start.24 = (bf16[224,1664]{1,0:T(8,128)(2,1)}, bf16[224,1664]{1,0:T(8,128)(2,1)}, u32[]{:S(2)}, u32[]{:S(2)}) collective-permute-start(bf16[224,1664]{1,0:T(8,128)(2,1)} %get-tuple-element.207), channel_id=1, source_target_pairs={{0,8},{8,0},{4,12},{12,4},{1,9},{9,1},{5,13},{13,5},{2,10},{10,2},... | collective-permute-start | bytes 2236424 | tf_op jit(solution)/shard_map/ppermute | solution.py:517
  207.7 32.4 %collective-permute-start.27 = (bf16[448,1664]{1,0:T(8,128)(2,1)}, bf16[448,1664]{1,0:T(8,128)(2,1)}, u32[]{:S(2)}, u32[]{:S(2)}) collective-permute-start(bf16[448,1664]{1,0:T(8,128)(2,1)} %pad_maximum_fusion.13), channel_id=1, source_target_pairs={{0,8},{8,0},{4,12},{12,4},{1,9},{9,1},{5,13},{13,5},{2,10},{10,2},... | collective-permute-start | bytes 4472840 | tf_op jit(solution)/shard_map/ppermute | solution.py:517
  209.9 31.9 %collective-permute-start.26 = (bf16[448,1664]{1,0:T(8,128)(2,1)S(1)}, bf16[448,1664]{1,0:T(8,128)(2,1)S(1)}, u32[]{:S(2)}, u32[]{:S(2)}) collective-permute-start(bf16[448,1664]{1,0:T(8,128)(2,1)S(1)} %pad_maximum_fusion.12), channel_id=1, source_target_pairs={{0,4},{4,0},{8,12},{12,8},{1,5},{5,1},{9,13},{13,9},{2,6},{6,2},{1... | collective-permute-start | bytes 4472840 | tf_op jit(solution)/shard_map/ppermute | solution.py:514
  247.5 20.5 %collective-permute-start.28 = (bf16[1792,1664]{1,0:T(8,128)(2,1)}, bf16[1792,1664]{1,0:T(8,128)(2,1)}, u32[]{:S(2)}, u32[]{:S(2)}) collective-permute-start(bf16[1792,1664]{1,0:T(8,128)(2,1)} %shard_map.169), channel_id=1, source_target_pairs={{0,16},{16,0},{1,17},{17,1},{2,18},{18,2},{3,19},{19,3},{4,20},{20... | collective-permute-start | bytes 17891336 | tf_op jit(solution)/shard_map/ppermute | solution.py:511
  275.2 37.8 %collective-permute-start.34 = (bf16[1664,1664]{1,0:T(8,128)(2,1)}, bf16[1664,1664]{1,0:T(8,128)(2,1)}, u32[]{:S(2)}, u32[]{:S(2)}) collective-permute-start(bf16[1664,1664]{1,0:T(8,128)(2,1)} %shard_map.173), channel_id=1, source_target_pairs={{0,16},{16,0},{1,17},{17,1},{2,18},{18,2},{3,19},{19,3},{4,20},{20... | collective-permute-start | bytes 16613384 | tf_op jit(solution)/shard_map/ppermute | solution.py:511
  293.6 174.9 %all-gather.20.cloned.1.call-start = ((), (), s32[]{:S(2)}) async-start(), calls=%async_computation.11 | async-start | bytes 6922240 | tf_op jit(solution)/shard_map/all_gather | solution.py:776
  363.7 166.6 %all-gather.18.cloned.1.call-start = ((), (), s32[]{:S(2)}) async-start(), calls=%async_computation.10 | async-start | bytes 4259840 | tf_op jit(solution)/shard_map/all_gather | solution.py:666
  468.5 64.3 %collective-permute-start.47 = (bf16[1664,1664]{1,0:T(8,128)(2,1)}, bf16[1664,1664]{1,0:T(8,128)(2,1)}, u32[]{:S(2)}, u32[]{:S(2)}) collective-permute-start(bf16[1664,1664]{1,0:T(8,128)(2,1)} %shard_map.182), channel_id=1, source_target_pairs={{0,16},{16,0},{1,17},{17,1},{2,18},{18,2},{3,19},{19,3},{4,20},{20... | collective-permute-start | bytes 16613384 | tf_op jit(solution)/shard_map/ppermute | solution.py:511
  471.2 195.3 %reduce-scatter.11.cloned.1.call-start = ((), (), s32[]{:S(2)}) async-start(), calls=%async_computation.16 | async-start | bytes 4259840 | tf_op jit(solution)/shard_map/reduce_scatter | solution.py:673
  486.8 31.5 %collective-permute-start.51 = (bf16[256,1664]{1,0:T(8,128)(2,1)}, bf16[256,1664]{1,0:T(8,128)(2,1)}, u32[]{:S(2)}, u32[]{:S(2)}) collective-permute-start(bf16[256,1664]{1,0:T(8,128)(2,1)} %pad_maximum_fusion.21), channel_id=1, source_target_pairs={{0,8},{8,0},{4,12},{12,4},{1,9},{9,1},{5,13},{13,5},{2,10},{10,2},... | collective-permute-start | bytes 2555912 | tf_op jit(solution)/shard_map/ppermute | solution.py:517
  489.0 29.4 %collective-permute-start.50 = (bf16[256,1664]{1,0:T(8,128)(2,1)}, bf16[256,1664]{1,0:T(8,128)(2,1)}, u32[]{:S(2)}, u32[]{:S(2)}) collective-permute-start(bf16[256,1664]{1,0:T(8,128)(2,1)} %pad_maximum_fusion.20), channel_id=1, source_target_pairs={{0,4},{4,0},{8,12},{12,8},{1,5},{5,1},{9,13},{13,9},{2,6},{6,2},{1... | collective-permute-start | bytes 2555912 | tf_op jit(solution)/shard_map/ppermute | solution.py:514
  567.9 62.4 %collective-permute-start.71 = (bf16[1664,1664]{1,0:T(8,128)(2,1)}, bf16[1664,1664]{1,0:T(8,128)(2,1)}, u32[]{:S(2)}, u32[]{:S(2)}) collective-permute-start(bf16[1664,1664]{1,0:T(8,128)(2,1)} %convolution_convert_fusion.1), channel_id=1, source_target_pairs={{0,16},{16,0},{1,17},{17,1},{2,18},{18,2},{3,19},{19,3},{4,20},{20... | collective-permute-start | bytes 16613384 | tf_op jit(solution)/shard_map/ppermute | solution.py:511
  585.0 171.6 %reduce-scatter.7.cloned.1.call-start = ((), (), s32[]{:S(2)}) async-start(), calls=%async_computation.12 | async-start | bytes 6922240 | tf_op jit(solution)/shard_map/reduce_scatter | solution.py:1039
  596.4 31.9 %collective-permute-start.52 = (bf16[256,1664]{1,0:T(8,128)(2,1)S(1)}, bf16[256,1664]{1,0:T(8,128)(2,1)S(1)}, u32[]{:S(2)}, u32[]{:S(2)}) collective-permute-start(bf16[256,1664]{1,0:T(8,128)(2,1)S(1)} %get-tuple-element.193), channel_id=1, source_target_pairs={{0,4},{4,0},{8,12},{12,8},{1,5},{5,1},{9,13},{13,9},{2,6},{6,2},{1... | collective-permute-start | bytes 2555912 | tf_op jit(solution)/shard_map/ppermute | solution.py:514
  596.9 46.7 %collective-permute-start.54 = (bf16[256,1664]{1,0:T(8,128)(2,1)}, bf16[256,1664]{1,0:T(8,128)(2,1)}, u32[]{:S(2)}, u32[]{:S(2)}) collective-permute-start(bf16[256,1664]{1,0:T(8,128)(2,1)} %get-tuple-element.194), channel_id=1, source_target_pairs={{0,8},{8,0},{4,12},{12,4},{1,9},{9,1},{5,13},{13,5},{2,10},{10,2},... | collective-permute-start | bytes 2555912 | tf_op jit(solution)/shard_map/ppermute | solution.py:517
  643.1 261.4 %all-gather.22.cloned.1.call-start = ((), (), s32[]{:S(2)}) async-start(), calls=%async_computation.13 | async-start | bytes 6922240 | tf_op jit(solution)/shard_map/all_gather | solution.py:1131
  756.7 170.5 %reduce-scatter.9.cloned.1.call-start = ((), (), s32[]{:S(2)}) async-start(), calls=%async_computation.14 | async-start | bytes 3194880 | tf_op jit(solution)/shard_map/reduce_scatter | solution.py:1039
  764.1 36.7 %collective-permute-start.66 = (bf16[256,1664]{1,0:T(8,128)(2,1)S(1)}, bf16[256,1664]{1,0:T(8,128)(2,1)S(1)}, u32[]{:S(2)}, u32[]{:S(2)}) collective-permute-start(bf16[256,1664]{1,0:T(8,128)(2,1)S(1)} %pad_maximum_fusion.23), channel_id=1, source_target_pairs={{0,8},{8,0},{4,12},{12,4},{1,9},{9,1},{5,13},{13,5},{2,10},{10,2},... | collective-permute-start | bytes 2555912 | tf_op jit(solution)/shard_map/ppermute | solution.py:517
  767.7 33.1 %collective-permute-start.65 = (bf16[256,1664]{1,0:T(8,128)(2,1)S(1)}, bf16[256,1664]{1,0:T(8,128)(2,1)S(1)}, u32[]{:S(2)}, u32[]{:S(2)}) collective-permute-start(bf16[256,1664]{1,0:T(8,128)(2,1)S(1)} %pad_maximum_fusion.22), channel_id=1, source_target_pairs={{0,4},{4,0},{8,12},{12,8},{1,5},{5,1},{9,13},{13,9},{2,6},{6,2},{1... | collective-permute-start | bytes 2555912 | tf_op jit(solution)/shard_map/ppermute | solution.py:514
  774.7 55.2 %collective-permute-start.83 = (bf16[1664,768]{1,0:T(8,128)(2,1)}, bf16[1664,768]{1,0:T(8,128)(2,1)}, u32[]{:S(2)}, u32[]{:S(2)}) collective-permute-start(bf16[1664,768]{1,0:T(8,128)(2,1)} %convolution_convert_fusion.11), channel_id=1, source_target_pairs={{0,16},{16,0},{1,17},{17,1},{2,18},{18,2},{3,19},{19,3},{4,20},{20... | collective-permute-start | bytes 7667720 | tf_op jit(solution)/shard_map/ppermute | solution.py:511
  836.0 197.8 %reduce-scatter.17.cloned.1.call-start = ((), (), s32[]{:S(2)}) async-start(), calls=%async_computation.19 | async-start | bytes 6922240 | tf_op jit(solution)/shard_map/reduce_scatter | solution.py:1039
  852.4 227.0 %all-gather.24.cloned.1.call-start = ((), (), s32[]{:S(2)}) async-start(), calls=%async_computation.15 | async-start | bytes 3194880 | tf_op jit(solution)/shard_map/all_gather | solution.py:1133
  924.5 36.6 %collective-permute-start.74 = (bf16[448,1792]{1,0:T(8,128)(2,1)}, bf16[448,1792]{1,0:T(8,128)(2,1)S(1)}, u32[]{:S(2)}, u32[]{:S(2)}) collective-permute-start(bf16[448,1792]{1,0:T(8,128)(2,1)} %get-tuple-element.173), channel_id=1, source_target_pairs={{0,4},{4,0},{8,12},{12,8},{1,5},{5,1},{9,13},{13,9},{2,6},{6,2},{1... | collective-permute-start | bytes 4816904 | tf_op jit(solution)/shard_map/ppermute | solution.py:514
  925.9 47.2 %collective-permute-start.75 = (bf16[448,1792]{1,0:T(8,128)(2,1)}, bf16[448,1792]{1,0:T(8,128)(2,1)}, u32[]{:S(2)}, u32[]{:S(2)}) collective-permute-start(bf16[448,1792]{1,0:T(8,128)(2,1)} %get-tuple-element.172), channel_id=1, source_target_pairs={{0,8},{8,0},{4,12},{12,4},{1,9},{9,1},{5,13},{13,5},{2,10},{10,2},... | collective-permute-start | bytes 4816904 | tf_op jit(solution)/shard_map/ppermute | solution.py:517
  927.2 241.4 %reduce-scatter.15.cloned.1.call-start = ((), (), s32[]{:S(2)}) async-start(), calls=%async_computation.18 | async-start | bytes 2007040 | tf_op jit(solution)/shard_map/reduce_scatter | solution.py:1039
  963.9 23.5 %collective-permute-start.97 = (bf16[224,1792]{1,0:T(8,128)(2,1)}, bf16[224,1792]{1,0:T(8,128)(2,1)}, u32[]{:S(2)}, u32[]{:S(2)}) collective-permute-start(bf16[224,1792]{1,0:T(8,128)(2,1)} %add_convert_fusion.16), channel_id=1, source_target_pairs={{0,8},{8,0},{4,12},{12,4},{1,9},{9,1},{5,13},{13,5},{2,10},{10,2},... | collective-permute-start | bytes 2408456 | tf_op jit(solution)/shard_map/ppermute | solution.py:517
  970.4 21.1 %collective-permute-start.76 = (bf16[448,256]{1,0:T(8,128)(2,1)S(1)}, bf16[448,256]{1,0:T(8,128)(2,1)S(1)}, u32[]{:S(2)}, u32[]{:S(2)}) collective-permute-start(bf16[448,256]{1,0:T(8,128)(2,1)S(1)} %get-tuple-element.99), channel_id=1, source_target_pairs={{0,4},{4,0},{8,12},{12,8},{1,5},{5,1},{9,13},{13,9},{2,6},{6,2},{1... | collective-permute-start | bytes 688136 | tf_op jit(solution)/shard_map/ppermute | solution.py:514
  971.7 20.5 %collective-permute-start.77 = (bf16[448,256]{1,0:T(8,128)(2,1)S(1)}, bf16[448,256]{1,0:T(8,128)(2,1)S(1)}, u32[]{:S(2)}, u32[]{:S(2)}) collective-permute-start(bf16[448,256]{1,0:T(8,128)(2,1)S(1)} %get-tuple-element.100), channel_id=1, source_target_pairs={{0,8},{8,0},{4,12},{12,4},{1,9},{9,1},{5,13},{13,5},{2,10},{10,2},... | collective-permute-start | bytes 688136 | tf_op jit(solution)/shard_map/ppermute | solution.py:517
  990.0 29.5 %collective-permute-start.98 = (bf16[224,1792]{1,0:T(8,128)(2,1)S(1)}, bf16[224,1792]{1,0:T(8,128)(2,1)S(1)}, u32[]{:S(2)}, u32[]{:S(2)}) collective-permute-start(bf16[224,1792]{1,0:T(8,128)(2,1)S(1)} %get-tuple-element.171), channel_id=1, source_target_pairs={{0,4},{4,0},{8,12},{12,8},{1,5},{5,1},{9,13},{13,9},{2,6},{6,2},{1... | collective-permute-start | bytes 2408456 | tf_op jit(solution)/shard_map/ppermute | solution.py:514
  1022.6 164.7 %all-gather.26.cloned.1.call-start = ((), (), s32[]{:S(2)}) async-start(), calls=%async_computation.20 | async-start | bytes 6922240 | tf_op jit(solution)/shard_map/all_gather | solution.py:1163
  1033.8 181.7 %reduce-scatter.13.cloned.1.call-start = ((), (), s32[]{:S(2)}) async-start(), calls=%async_computation.17 | async-start | bytes 3194880 | tf_op jit(solution)/shard_map/reduce_scatter | solution.py:1039
  1042.9 21.6 %collective-permute-start.81 = (bf16[256,1664]{1,0:T(8,128)(2,1)S(1)}, bf16[256,1664]{1,0:T(8,128)(2,1)S(1)}, u32[]{:S(2)}, u32[]{:S(2)}) collective-permute-start(bf16[256,1664]{1,0:T(8,128)(2,1)S(1)} %get-tuple-element.185), channel_id=1, source_target_pairs={{0,8},{8,0},{4,12},{12,4},{1,9},{9,1},{5,13},{13,5},{2,10},{10,2},... | collective-permute-start | bytes 2555912 | tf_op jit(solution)/shard_map/ppermute | solution.py:517
  1089.9 25.4 %collective-permute-start.86 = (bf16[64,3328]{1,0:T(8,128)(2,1)S(1)}, bf16[64,3328]{1,0:T(8,128)(2,1)S(1)}, u32[]{:S(2)}, u32[]{:S(2)}) collective-permute-start(bf16[64,3328]{1,0:T(8,128)(2,1)S(1)} %get-tuple-element.105), channel_id=1, source_target_pairs={{0,3},{3,0},{1,2},{2,1},{4,7},{7,4},{5,6},{6,5},{8,11},{11,8},{9,1... | collective-permute-start | bytes 1277960 | tf_op jit(solution)/shard_map/ppermute | solution.py:584
  1093.4 181.5 %collective-permute-start.105 = (bf16[1664,1664]{1,0:T(8,128)(2,1)}, bf16[1664,1664]{1,0:T(8,128)(2,1)}, u32[]{:S(2)}, u32[]{:S(2)}) collective-permute-start(bf16[1664,1664]{1,0:T(8,128)(2,1)} %all-gather.22.cloned.1.call-done.refs_1_), channel_id=1, source_target_pairs={{0,16},{1,17},{2,18},{3,19},{4,20},{5,21},{6,22},{7,23},{8,24},{9,... | collective-permute-start | bytes 16613384 | tf_op jit(solution)/shard_map/ppermute | solution.py:511
  1117.0 34.5 %collective-permute-start.89 = (bf16[64,3328]{1,0:T(8,128)(2,1)S(1)}, bf16[64,3328]{1,0:T(8,128)(2,1)S(1)}, u32[]{:S(2)}, u32[]{:S(2)}) collective-permute-start(bf16[64,3328]{1,0:T(8,128)(2,1)S(1)} %get-tuple-element.109), channel_id=1, source_target_pairs={{0,12},{12,0},{4,8},{8,4},{1,13},{13,1},{5,9},{9,5},{2,14},{14,2},... | collective-permute-start | bytes 1277960 | tf_op jit(solution)/shard_map/ppermute | solution.py:584
  1151.6 45.3 %collective-permute-start.90 = (bf16[256,3328]{1,0:T(8,128)(2,1)S(1)}, bf16[256,3328]{1,0:T(8,128)(2,1)}, u32[]{:S(2)}, u32[]{:S(2)}) collective-permute-start(bf16[256,3328]{1,0:T(8,128)(2,1)S(1)} %shard_map.195.mine_ref), channel_id=1, source_target_pairs={{0,16},{16,0},{1,17},{17,1},{2,18},{18,2},{3,19},{19,3},{4,20},{20... | collective-permute-start | bytes 5111816 | tf_op jit(solution)/shard_map/ppermute | solution.py:511
  1168.6 29.8 %collective-permute-start.100 = (bf16[112,1792]{1,0:T(8,128)(2,1)}, bf16[112,1792]{1,0:T(8,128)(2,1)S(1)}, u32[]{:S(2)}, u32[]{:S(2)}) collective-permute-start(bf16[112,1792]{1,0:T(8,128)(2,1)} %reduce-scatter.15.cloned.1.call-done.refs_0_), channel_id=1, source_target_pairs={{0,8},{8,0},{4,12},{12,4},{1,9},{9,1},{5,13},{13,5},{2,10},{10,2},... | collective-permute-start | bytes 1204232 | tf_op jit(solution)/shard_map/ppermute | solution.py:517
  1176.5 23.1 %collective-permute-start.101 = (bf16[112,1792]{1,0:T(8,128)(2,1)}, bf16[112,1792]{1,0:T(8,128)(2,1)S(1)}, u32[]{:S(2)}, u32[]{:S(2)}) collective-permute-start(bf16[112,1792]{1,0:T(8,128)(2,1)} %reduce-scatter.15.cloned.1.call-done.refs_0_), channel_id=1, source_target_pairs={{0,12},{12,0},{4,8},{8,4},{1,13},{13,1},{5,9},{9,5},{2,14},{14,2},... | collective-permute-start | bytes 1204232 | tf_op jit(solution)/shard_map/ppermute | solution.py:520
  1187.3 102.5 %collective-permute-start.106 = (bf16[1664,1664]{1,0:T(8,128)(2,1)}, bf16[1664,1664]{1,0:T(8,128)(2,1)}, u32[]{:S(2)}, u32[]{:S(2)}) collective-permute-start(bf16[1664,1664]{1,0:T(8,128)(2,1)} %all-gather.26.cloned.1.call-done), channel_id=1, source_target_pairs={{16,0},{17,1},{18,2},{19,3},{20,4},{21,5},{22,6},{23,7},{24,8},{25... | collective-permute-start | bytes 16613384 | tf_op jit(solution)/shard_map/ppermute | solution.py:511
  1196.9 76.1 %collective-permute-start.95 = (bf16[1664,768]{1,0:T(8,128)(2,1)}, bf16[1664,768]{1,0:T(8,128)(2,1)}, u32[]{:S(2)}, u32[]{:S(2)}) collective-permute-start(bf16[1664,768]{1,0:T(8,128)(2,1)} %all-gather.24.cloned.1.call-done.refs_1_), channel_id=1, source_target_pairs={{0,16},{1,17},{2,18},{3,19},{4,20},{5,21},{6,22},{7,23},{8,24},{9,... | collective-permute-start | bytes 7667720 | tf_op jit(solution)/shard_map/ppermute | solution.py:511
  1217.5 20.5 %collective-permute-start.93 = (bf16[416,768]{1,0:T(8,128)(2,1)}, bf16[416,768]{1,0:T(8,128)(2,1)S(1)}, u32[]{:S(2)}, u32[]{:S(2)}) collective-permute-start(bf16[416,768]{1,0:T(8,128)(2,1)} %reduce-scatter.13.cloned.1.call-done.refs_0_), channel_id=1, source_target_pairs={{0,8},{8,0},{4,12},{12,4},{1,9},{9,1},{5,13},{13,5},{2,10},{10,2},... | collective-permute-start | bytes 1916936 | tf_op jit(solution)/shard_map/ppermute | solution.py:517
  1238.9 22.8 %collective-permute-start.103 = (bf16[448,896]{1,0:T(8,128)(2,1)}, bf16[448,896]{1,0:T(8,128)(2,1)}, u32[]{:S(2)}, u32[]{:S(2)}) collective-permute-start(bf16[448,896]{1,0:T(8,128)(2,1)} %get-tuple-element.110), channel_id=1, source_target_pairs={{16,0},{17,1},{18,2},{19,3},{20,4},{21,5},{22,6},{23,7},{24,8},{25... | collective-permute-start | bytes 2408456 | tf_op jit(solution)/shard_map/ppermute | solution.py:511
  1247.7 22.1 %collective-permute-start.102 = (bf16[448,896]{1,0:T(8,128)(2,1)}, bf16[448,896]{1,0:T(8,128)(2,1)}, u32[]{:S(2)}, u32[]{:S(2)}) collective-permute-start(bf16[448,896]{1,0:T(8,128)(2,1)} %get-tuple-element.111), channel_id=1, source_target_pairs={{0,16},{1,17},{2,18},{3,19},{4,20},{5,21},{6,22},{7,23},{8,24},{9,... | collective-permute-start | bytes 2408456 | tf_op jit(solution)/shard_map/ppermute | solution.py:511
  1261.7 22.1 %collective-permute-start.96 = (bf16[1664,768]{1,0:T(8,128)(2,1)S(1)}, bf16[1664,768]{1,0:T(8,128)(2,1)}, u32[]{:S(2)}, u32[]{:S(2)}) collective-permute-start(bf16[1664,768]{1,0:T(8,128)(2,1)S(1)} %shard_map.197), channel_id=1, source_target_pairs={{16,0},{17,1},{18,2},{19,3},{20,4},{21,5},{22,6},{23,7},{24,8},{25... | collective-permute-start | bytes 7667720 | tf_op jit(solution)/shard_map/ppermute | solution.py:511
  (231 other events, 2569.8 us)
Sparse Core Ops, SparseCore 0:
  27.2 73.6 all-gather.9
  102.5 43.5 all-gather.11
  164.8 103.1 all-gather.13
  293.7 51.2 all-gather.15
  363.8 104.5 all-gather.19
  471.3 58.9 all-gather.17
  585.1 66.3 reduce-scatter.10
  654.4 98.3 reduce-scatter.6
  756.8 79.0 all-gather.21
  838.7 50.8 reduce-scatter.8
  892.6 98.3 reduce-scatter.16
  992.8 42.7 all-gather.23
  1038.6 35.6 reduce-scatter.14
  1076.1 79.6 all-gather.25
  1158.7 56.8 reduce-scatter.12

commit v4 on v3

--- a/solution.py
+++ b/solution.py
@@ -203,6 +203,41 @@
         compiler_params=pltpu.CompilerParams(vmem_limit_bytes=48 * 2**20),
         cost_estimate=pl.CostEstimate(flops=0, bytes_accessed=size, transcendentals=0),
     )(member.reshape(1), *inputs)
+
+
+def chosen_kernel(kernel, count, section_ref, *refs):
+    inputs, out_ref = refs[: 2 * count], refs[2 * count]
+    held, sem = refs[2 * count + 1 : -1], refs[-1]
+    for side in range(2):
+
+        @pl.when(section_ref[0] == side)
+        def _(side=side):
+            copies = [
+                pltpu.make_async_copy(inputs[2 * i + side], held[i], sem.at[i])
+                for i in range(count)
+            ]
+            for copy in copies:
+                copy.start()
+            for copy in copies:
+                copy.wait()
+
+    kernel(section_ref, *held, out_ref)
+
+
+def chosen_call(kernel, section, pairs, out):
+    count = len(pairs)
+    size = sum(a.size * a.dtype.itemsize for a, _ in pairs) + out.size * out.dtype.itemsize
+    return pl.pallas_call(
+        partial(chosen_kernel, kernel, count),
+        in_specs=[pl.BlockSpec(memory_space=pltpu.SMEM)]
+        + [pl.BlockSpec(memory_space=pl.ANY)] * (2 * count),
+        out_specs=pl.BlockSpec(memory_space=pltpu.VMEM),
+        out_shape=out,
+        scratch_shapes=[pltpu.VMEM(a.shape, a.dtype) for a, _ in pairs]
+        + [pltpu.SemaphoreType.DMA((count,))],
+        compiler_params=pltpu.CompilerParams(vmem_limit_bytes=48 * 2**20),
+        cost_estimate=pl.CostEstimate(flops=0, bytes_accessed=size, transcendentals=0),
+    )(section.reshape(1), *[x for pair in pairs for x in pair])
 
 
 def slab_places(member, rows, step, slab):
@@ -1043,25 +1078,23 @@
 
         def finish(kernel, pairs, shape):
             (mine_0, other_0), (mine_1, other_1) = pairs
-            left, right = pick(mine_0, other_1), pick(other_0, mine_1)
-            out = jax.ShapeDtypeStruct(shape, F32)
-            return kernel_call(kernel, member, [left, right], [out])[0]
+            choices = [(mine_0, other_1), (other_0, mine_1)]
+            return chosen_call(kernel, section, choices, jax.ShapeDtypeStruct(shape, F32))
 
         def finish_fc(pairs):
             (mine_0, other_0), (mine_1, other_1) = pairs
-            left, right = pick(mine_0, other_1), pick(other_0, mine_1)
-            w_in = kernel_call(
+            w_in = chosen_call(
                 partial(finish_in_kernel, cut, padded),
-                member,
-                [left],
-                [jax.ShapeDtypeStruct((rows, hidden), F32)],
-            )[0]
-            w_out = kernel_call(
+                section,
+                [(mine_0, other_1)],
+                jax.ShapeDtypeStruct((rows, hidden), F32),
+            )
+            w_out = chosen_call(
                 partial(finish_out_kernel, cut, padded),
-                member,
-                [right],
-                [jax.ShapeDtypeStruct((hid, width), F32)],
-            )[0]
+                section,
+                [(other_0, mine_1)],
+                jax.ShapeDtypeStruct((hid, width), F32),
+            )
             return w_in, w_out
 
         def reduce_small(small):

time: 1310 us -> 1410 us (1.076)
  waiting for transfers between devices: 560 us -> 639 us
  local copies, waits for them, and re-layouts: 82.8 us -> 100 us
    ppermute x30, waiting for transfers between devices: 165 us -> 209 us  [across(): return lax.ppermute(value, 'replica', ACROSS)]
    ppermute x30, waiting for transfers between devices: 207 us -> 238 us  [side(): return lax.ppermute(value, 'replica', SIDE)]
    ppermute x24, starting transfers between devices: 44 us -> 71.2 us  [turned(): lax.ppermute(x, axis, pairs)]
    pallas_call x0 -> x4, Pallas kernels: none -> 24.8 us  [chosen_call(): pl.pallas_call(partial(chosen_kernel, kernel, count), in_specs=[pl.BlockS...]
    unnamed x340 -> x346, local copies, waits for them, and re-layouts: 38.2 us -> 55.3 us
    pallas_call x32 -> x28, Pallas kernels: 52.5 us -> 35.7 us  [kernel_call(): pl.pallas_call(kernel, in_specs=[pl.BlockSpec(memory_space=pltpu.SMEM)] +...]
    reduce_scatter x5, waiting for transfers between devices: 15.2 us -> 0.01 us  [over_planes(): return lax.psum_scatter(total, 'seq', scatter_dimension=0, tiled=True)]
    select_n x18 -> x12, other arithmetic: 33.3 us -> 22.5 us  [pick(): return jnp.where(first, a, b)]
  transfers between devices with their start and end apart: 129 -> 129, of which waited for: 69 -> 67; matrix products, arithmetic and copies ran while one was open for 25% -> 22% of each run, Pallas kernels for 9% -> 9%
where the time goes in v4:
time: 1410 us; the launch traced here: 1400 us
  waiting for transfers between devices  639 us (45%)
  matrix products  212 us (15%)
  starting transfers between devices  205 us (15%)
  Pallas kernels  134 us (10%)
  local copies, waits for them, and re-layouts  100 us (7%)
  other arithmetic  95.4 us (7%)
  between operations  16.7 us (1%)
    ppermute x30, waiting for transfers between devices, side(): return lax.ppermute(value, 'replica', SIDE)  238 us
    dot_general x30, matrix products, dot(): lax.dot_general(left, right, ((contract[:1], contract[1:]), ((), ())), pr...  212 us
    ppermute x30, waiting for transfers between devices, across(): return lax.ppermute(value, 'replica', ACROSS)  209 us
    ppermute x24, waiting for transfers between devices, turned(): lax.ppermute(x, axis, pairs)  120 us
    ppermute x24, starting transfers between devices, turned(): lax.ppermute(x, axis, pairs)  71.2 us
    ppermute x23, starting transfers between devices, cross(): return lax.ppermute(value, 'section', pairs)  62.1 us
    unnamed x346, local copies, waits for them, and re-layouts  55.3 us
    pallas_call x2, Pallas kernels, attend_back(): pl.pallas_call(partial(attend_back_kernel, grouped), grid=(slots,), in_sp...  39.3 us
  transfers between devices with their start and end apart: 129, of which 67 were waited for; matrix products, arithmetic and copies ran while one was open for 22% of the time, Pallas kernels for 9%

profile of v4, /device:TPU:1, one launch (start us, length us, event | category | flops | bytes accessed | tf_op | source)
XLA Modules:
  0.0 1403.2 jit_solution(2668725309394161398)
XLA Ops:
  56.3 7.3 collective-permute-done.8.refs_2_
  73.5 13.2 collective-permute-done.10.refs_1_
  110.5 10.7 collective-permute-done.3.refs_3_
  124.7 6.4 collective-permute-start.4
  134.6 16.0 %collective-permute-done.4.refs_1_ = bf16[64,1664]{1,0:T(8,128)(2,1)S(1)} collective-permute-done((bf16[64,1664]{1,0:T(8,128)(2,1)S(1)}, bf16[64,1664]{1,0:T(8,128)(2,1)S(1)}, u32[]{:S(2)}, u32[]{:S(2)}) %collective-permute-start.4) | collective-permute-done | bytes 213024 | tf_op jit(solution)/shard_map/ppermute | solution.py:619
  189.9 17.6 %shard_map.162 = (bf16[448,256]{1,0:T(8,128)(2,1)S(1)}, bf16[448,256]{1,0:T(8,128)(2,1)}, bf16[448,256]{1,0:T(8,128)(2,1)S(1)}, bf16[448,256]{1,0:T(8,128)(2,1)S(1)}, f32[7,1,1024]{2,1,0:T(1,128)S(1)}) custom-call(bf16[1408,1024]{1,0:T(8,128)(2,1)S(1)} %add_convert_fusion.7.q_ref.k_ref.v_ref.refs_1_, ...), custom_call_target="tpu_custom_call" | custom-call | flops 19730006016 | bytes 7864320 | tf_op jit(solution)/shard_map/pallas_call | solution.py:142
  214.1 29.8 %collective-permute-done.27.far_b = bf16[448,1664]{1,0:T(8,128)(2,1)} collective-permute-done((bf16[448,1664]{1,0:T(8,128)(2,1)}, bf16[448,1664]{1,0:T(8,128)(2,1)}, u32[]{:S(2)}, u32[]{:S(2)}) %collective-permute-start.27) | collective-permute-done | bytes 1490976 | tf_op jit(solution)/shard_map/ppermute | solution.py:552
  282.5 8.5 collective-permute-done.31.near_b
  296.5 14.9 %collective-permute-done.33.far_b = bf16[256,1664]{1,0:T(8,128)(2,1)S(1)} collective-permute-done((bf16[256,1664]{1,0:T(8,128)(2,1)}, bf16[256,1664]{1,0:T(8,128)(2,1)S(1)}, u32[]{:S(2)}, u32[]{:S(2)}) %collective-permute-start.33) | collective-permute-done | bytes 852000 | tf_op jit(solution)/shard_map/ppermute | solution.py:552
  316.6 14.0 %add_convert_fusion.3 = (bf16[1024,1664]{1,0:T(8,128)(2,1)}, bf16[1024,1664]{1,0:T(8,128)(2,1)S(1)}) fusion(f32[1664]{0:T(1024)S(1)} %add.689, bf16[1024,1664]{1,0:T(8,128)(2,1)} %shard_map.172, bf16[1664,1664]{1,0:T(8,128)(2,1)} %shard_map.173, bf16[1664,1664]{1,0:T(8,128)(2,1)} %collective-permute-done.34, pred[]{:T(512)S(6)} %eq.18), kind=kOutput, calls=%fused_computation.19 | convolution fusion | flops 5707546624 | bytes 21305856 | tf_op jit(solution)/shard_map/dot_general | solution.py:23
  330.7 7.5 convolution_convert_fusion.7.refs_1_
  339.9 12.7 collective-permute-done.35
  353.5 11.2 collective-permute-done.36
  388.9 12.5 collective-permute-done.43.far_b
  403.4 7.8 add_convert_fusion.6.q_ref.k_ref.v_ref
  411.1 17.1 %shard_map.177 = (bf16[448,256]{1,0:T(8,128)(2,1)S(1)}, bf16[448,256]{1,0:T(8,128)(2,1)S(1)}, bf16[448,256]{1,0:T(8,128)(2,1)S(1)}, bf16[448,256]{1,0:T(8,128)(2,1)S(1)}, f32[7,1,1024]{2,1,0:T(1,128)S(1)}) custom-call(bf16[1408,1024]{1,0:T(8,128)(2,1)S(1)} %add_convert_fusion.6.q_ref.k_ref.v_ref, bf16[1408,1024]{1,0:T(8,128)(2,1)S(1)} %add_convert_fusion.6.q_ref.k_ref.v_ref, ...), custom_call_target="tpu_custom_call" | custom-call | flops 19730006016 | bytes 7864320 | tf_op jit(solution)/shard_map/pallas_call | solution.py:142
  447.1 24.9 %all-gather.20.cloned.1.call-done.refs_0_ = bf16[1664,1664]{1,0:T(8,128)(2,1)} async-done(((bf16[416,1664]{1,0:T(8,128)(2,1)}), bf16[1664,1664]{1,0:T(8,128)(2,1)}) %all-gather.20.cloned.1.call-update) | async-done | bytes 5537808 | tf_op jit(solution)/shard_map/all_gather | solution.py:811
  477.3 12.1 collective-permute-done.49.near_b
  494.7 27.1 %collective-permute-done.51.far_b = bf16[256,1664]{1,0:T(8,128)(2,1)} collective-permute-done((bf16[256,1664]{1,0:T(8,128)(2,1)}, bf16[256,1664]{1,0:T(8,128)(2,1)}, u32[]{:S(2)}, u32[]{:S(2)}) %collective-permute-start.51) | collective-permute-done | bytes 852000 | tf_op jit(solution)/shard_map/ppermute | solution.py:552
  525.2 8.6 all-gather.18.cloned.1.call-done.value_ref
  536.3 15.4 %add_convert_fusion.2 = (bf16[1024,1664]{1,0:T(8,128)(2,1)S(1)}, bf16[1024,1664]{1,0:T(8,128)(2,1)}) fusion(f32[1664]{0:T(1024)S(1)} %add.720, bf16[1024,1664]{1,0:T(8,128)(2,1)} %shard_map.183, bf16[1664,1664]{1,0:T(8,128)(2,1)} %shard_map.182, bf16[1664,1664]{1,0:T(8,128)(2,1)} %collective-permute-done.47, pred[]{:T(512)S(6)} %eq.18), kind=kOutput, calls=%fused_computation.16 | convolution fusion | flops 5707546624 | bytes 21305856 | tf_op jit(solution)/shard_map/dot_general | solution.py:23
  551.7 7.4 multiply_convert_fusion.1
  559.1 12.3 convolution_convert_fusion.1
  574.4 10.1 convolution_convert_fusion.2.value_ref
  588.6 10.3 convolution_convert_fusion.6
  601.4 30.4 %collective-permute-done.52 = bf16[256,1664]{1,0:T(8,128)(2,1)S(1)} collective-permute-done((bf16[256,1664]{1,0:T(8,128)(2,1)S(1)}, bf16[256,1664]{1,0:T(8,128)(2,1)S(1)}, u32[]{:S(2)}, u32[]{:S(2)}) %collective-permute-start.52) | collective-permute-done | bytes 852000 | tf_op jit(solution)/shard_map/ppermute | solution.py:549
  633.9 12.7 add_convert_fusion.1
  655.2 9.1 collective-permute-done.55
  693.3 19.6 %shard_map.185 = bf16[1408,1024]{1,0:T(8,128)(2,1)S(1)} custom-call(bf16[1408,1024]{1,0:T(8,128)(2,1)S(1)} %copy-done.74, bf16[1408,1024]{1,0:T(8,128)(2,1)S(1)} %copy-done.74, bf16[1408,1024]{1,0:T(8,128)(2,1)S(1)} %copy-done.74, f32[1024,1024]{1,0:T(8,128)S(1)} %copy-done.25, f32[7,1,1024]{2,1,0:T(1,128)S(1)} %get-tuple-element.91.lse_ref, ...), custom_call_target="tpu_custom_call" | custom-call | flops 22548578304 | bytes 10616832 | tf_op jit(solution)/shard_map/pallas_call | solution.py:165
  713.0 6.3 convolution_convert_fusion.5
  721.8 15.6 %collective-permute-done.59 = bf16[256,1664]{1,0:T(8,128)(2,1)S(1)} collective-permute-done((bf16[256,1664]{1,0:T(8,128)(2,1)S(1)}, bf16[256,1664]{1,0:T(8,128)(2,1)S(1)}, u32[]{:S(2)}, u32[]{:S(2)}) %collective-permute-start.59) | collective-permute-done | bytes 852000 | tf_op jit(solution)/shard_map/ppermute | solution.py:549
  738.9 8.6 collective-permute-done.60
  749.1 7.3 collective-permute-done.62
  771.2 6.9 convolution_convert_fusion.11
  778.1 10.0 collective-permute-start.83
  788.2 16.1 %collective-permute-done.66.far_b = bf16[256,1664]{1,0:T(8,128)(2,1)S(1)} collective-permute-done((bf16[256,1664]{1,0:T(8,128)(2,1)S(1)}, bf16[256,1664]{1,0:T(8,128)(2,1)S(1)}, u32[]{:S(2)}, u32[]{:S(2)}) %collective-permute-start.66) | collective-permute-done | bytes 852000 | tf_op jit(solution)/shard_map/ppermute | solution.py:552
  806.2 9.8 multiply_convert_fusion
  816.1 9.1 convolution_convert_fusion
  825.2 8.1 collective-permute-start.104
  833.3 6.2 add_convert_fusion.9
  842.4 13.5 add_convert_fusion
  856.3 10.2 convolution_convert_fusion.4
  869.5 17.6 %collective-permute-done.67 = bf16[256,1664]{1,0:T(8,128)(2,1)S(1)} collective-permute-done((bf16[256,1664]{1,0:T(8,128)(2,1)S(1)}, bf16[256,1664]{1,0:T(8,128)(2,1)S(1)}, u32[]{:S(2)}, u32[]{:S(2)}) %collective-permute-start.67) | collective-permute-done | bytes 852000 | tf_op jit(solution)/shard_map/ppermute | solution.py:549
  888.7 8.8 collective-permute-done.68
  939.1 25.9 %collective-permute-done.74.refs_1_ = bf16[448,1792]{1,0:T(8,128)(2,1)} collective-permute-done((bf16[448,1792]{1,0:T(8,128)(2,1)}, bf16[448,1792]{1,0:T(8,128)(2,1)}, u32[]{:S(2)}, u32[]{:S(2)}) %collective-permute-start.74) | collective-permute-done | bytes 1605664 | tf_op jit(solution)/shard_map/ppermute | solution.py:549
  980.8 19.6 %shard_map.190 = bf16[1408,1024]{1,0:T(8,128)(2,1)S(1)} custom-call(bf16[1408,1024]{1,0:T(8,128)(2,1)S(1)} %copy-done.17, bf16[1408,1024]{1,0:T(8,128)(2,1)S(1)} %copy-done.17, bf16[1408,1024]{1,0:T(8,128)(2,1)S(1)} %copy-done.17, f32[1024,1024]{1,0:T(8,128)S(1)} %copy-done.26, f32[7,1,1024]{2,1,0:T(1,128)S(1)} %copy-done.52, ...), custom_call_target="tpu_custom_call" | custom-call | flops 22548578304 | bytes 10616832 | tf_op jit(solution)/shard_map/pallas_call | solution.py:165
  1018.5 31.5 %collective-permute-done.97 = bf16[224,1792]{1,0:T(8,128)(2,1)S(1)} collective-permute-done((bf16[224,1792]{1,0:T(8,128)(2,1)S(1)}, bf16[224,1792]{1,0:T(8,128)(2,1)S(1)}, u32[]{:S(2)}, u32[]{:S(2)}) %collective-permute-start.97) | collective-permute-done | bytes 802848 | tf_op jit(solution)/shard_map/ppermute | solution.py:552
  1054.2 24.3 %collective-permute-done.98 = bf16[224,1792]{1,0:T(8,128)(2,1)S(1)} collective-permute-done((bf16[224,1792]{1,0:T(8,128)(2,1)S(1)}, bf16[224,1792]{1,0:T(8,128)(2,1)S(1)}, u32[]{:S(2)}, u32[]{:S(2)}) %collective-permute-start.98) | collective-permute-done | bytes 802848 | tf_op jit(solution)/shard_map/ppermute | solution.py:549
  1082.4 8.4 convolution_convert_fusion.3
  1099.4 32.1 %collective-permute-done.79 = bf16[256,1664]{1,0:T(8,128)(2,1)S(1)} collective-permute-done((bf16[256,1664]{1,0:T(8,128)(2,1)S(1)}, bf16[256,1664]{1,0:T(8,128)(2,1)S(1)}, u32[]{:S(2)}, u32[]{:S(2)}) %collective-permute-start.79) | collective-permute-done | bytes 852000 | tf_op jit(solution)/shard_map/ppermute | solution.py:549
  1149.0 6.1 collective-permute-done.82
  1157.7 6.3 collective-permute-start.107
  1175.6 25.7 %collective-permute-done.84.refs_1_ = bf16[64,3328]{1,0:T(8,128)(2,1)S(1)} collective-permute-done((bf16[64,3328]{1,0:T(8,128)(2,1)S(1)}, bf16[64,3328]{1,0:T(8,128)(2,1)S(1)}, u32[]{:S(2)}, u32[]{:S(2)}) %collective-permute-start.84) | collective-permute-done | bytes 426016 | tf_op jit(solution)/shard_map/ppermute | solution.py:619
  1202.5 11.3 collective-permute-done.86.refs_3_
  1220.9 6.5 collective-permute-done.110.refs_3_
  1227.7 31.3 %collective-permute-start.111 = (f32[150,128]{1,0:T(8,128)S(1)}, f32[150,128]{1,0:T(8,128)S(1)}, u32[]{:S(2)}, u32[]{:S(2)}) collective-permute-start(f32[150,128]{1,0:T(8,128)S(1)} %shard_map.204.refs_0_), channel_id=1, source_target_pairs={{0,1},{1,0},{2,3},{3,2},{4,5},{5,4},{6,7},{7,6},{8,9},{9,8},{10,11... | collective-permute-start | bytes 230408 | tf_op jit(solution)/shard_map/ppermute | solution.py:619
  1276.5 8.7 collective-permute-done.89.refs_3_
  1286.2 8.9 collective-permute-done.100.refs_2_
  1301.2 21.3 %collective-permute-done.93.refs_2_ = bf16[416,768]{1,0:T(8,128)(2,1)S(1)} collective-permute-done((bf16[416,768]{1,0:T(8,128)(2,1)}, bf16[416,768]{1,0:T(8,128)(2,1)S(1)}, u32[]{:S(2)}, u32[]{:S(2)}) %collective-permute-start.93) | collective-permute-done | bytes 639008 | tf_op jit(solution)/shard_map/ppermute | solution.py:552
  1326.1 7.6 collective-permute-done.101.refs_3_
  1335.0 6.9 collective-permute-done.99.refs_1_
  1373.4 8.1 shard_map.202
  1381.5 6.3 shard_map.198
  1387.9 8.2 shard_map.203
  (856 shorter events, 519.9 us)
Async XLA Ops:
  7.2 98.4 %all-gather.10.cloned.1.call-start = ((), (), s32[]{:S(2)}) async-start(), calls=%async_computation.6 | async-start | bytes 3194880 | tf_op jit(solution)/shard_map/all_gather | solution.py:811
  14.3 29.9 %collective-permute-start = (bf16[256,1664]{1,0:T(8,128)(2,1)}, bf16[256,1664]{1,0:T(8,128)(2,1)}, u32[]{:S(2)}, u32[]{:S(2)}) collective-permute-start(bf16[256,1664]{1,0:T(8,128)(2,1)} %broadcast_select_fusion.27), channel_id=1, source_target_pairs={{0,16},{16,0},{1,17},{17,1},{2,18},{18,2},{3,19},{19,3},{4,20},{20... | collective-permute-start | bytes 2555912 | tf_op jit(solution)/shard_map/ppermute | solution.py:546
  22.2 46.6 %collective-permute-start.15 = (f32[19200]{0:T(1024)}, f32[19200]{0:T(1024)}, u32[]{:S(2)}, u32[]{:S(2)}) collective-permute-start(f32[19200]{0:T(1024)} %pad_maximum_fusion.25), channel_id=1, source_target_pairs={{0,16},{16,0},{1,17},{17,1},{2,18},{18,2},{3,19},{19,3},{4,20},{20... | collective-permute-start | bytes 230408 | tf_op jit(solution)/shard_map/ppermute | solution.py:546
  22.9 32.0 %collective-permute-start.20 = (s32[1024]{0:T(1024)}, s32[1024]{0:T(1024)}, u32[]{:S(2)}, u32[]{:S(2)}) collective-permute-start(s32[1024]{0:T(1024)} %bitcast.9), channel_id=1, source_target_pairs={{0,0},{1,4},{2,8},{3,12},{4,1},{5,5},{6,9},{7,13},{8,2},{9,6},{10,... | collective-permute-start | bytes 12296 | tf_op jit(solution)/shard_map/ppermute | solution.py:936
  27.7 146.5 %all-gather.12.cloned.1.call-start = ((), (), s32[]{:S(2)}) async-start(), calls=%async_computation.7 | async-start | bytes 1863680 | tf_op jit(solution)/shard_map/all_gather | solution.py:811
  54.9 110.2 %collective-permute-start.29 = (bf16[416,1664]{1,0:T(8,128)(2,1)}, bf16[416,1664]{1,0:T(8,128)(2,1)}, u32[]{:S(2)}, u32[]{:S(2)}) collective-permute-start(bf16[416,1664]{1,0:T(8,128)(2,1)} %broadcast_select_fusion.22), channel_id=1, source_target_pairs={{0,16},{16,0},{1,17},{17,1},{2,18},{18,2},{3,19},{19,3},{4,20},{20... | collective-permute-start | bytes 4153352 | tf_op jit(solution)/shard_map/ppermute | solution.py:546
  65.2 24.2 %collective-permute-start.11 = (bf16[64,1664]{1,0:T(8,128)(2,1)}, bf16[64,1664]{1,0:T(8,128)(2,1)S(1)}, u32[]{:S(2)}, u32[]{:S(2)}) collective-permute-start(bf16[64,1664]{1,0:T(8,128)(2,1)} %get-tuple-element.76), channel_id=1, source_target_pairs={{0,2},{2,0},{1,3},{3,1},{4,6},{6,4},{5,7},{7,5},{8,10},{10,8},{9,1... | collective-permute-start | bytes 638984 | tf_op jit(solution)/shard_map/ppermute | solution.py:619
  67.2 28.7 %collective-permute-start.12 = (bf16[64,1664]{1,0:T(8,128)(2,1)}, bf16[64,1664]{1,0:T(8,128)(2,1)S(1)}, u32[]{:S(2)}, u32[]{:S(2)}) collective-permute-start(bf16[64,1664]{1,0:T(8,128)(2,1)} %get-tuple-element.77), channel_id=1, source_target_pairs={{0,3},{3,0},{1,2},{2,1},{4,7},{7,4},{5,6},{6,5},{8,11},{11,8},{9,1... | collective-permute-start | bytes 638984 | tf_op jit(solution)/shard_map/ppermute | solution.py:619
  72.5 33.9 %collective-permute-start.1 = (bf16[64,1664]{1,0:T(8,128)(2,1)}, bf16[64,1664]{1,0:T(8,128)(2,1)}, u32[]{:S(2)}, u32[]{:S(2)}) collective-permute-start(bf16[64,1664]{1,0:T(8,128)(2,1)} %get-tuple-element.63), channel_id=1, source_target_pairs={{0,4},{4,0},{8,12},{12,8},{1,5},{5,1},{9,13},{13,9},{2,6},{6,2},{1... | collective-permute-start | bytes 638984 | tf_op jit(solution)/shard_map/ppermute | solution.py:619
  103.1 168.5 %all-gather.14.cloned.1.call-start = ((), (), s32[]{:S(2)}) async-start(), calls=%async_computation.8 | async-start | bytes 6922240 | tf_op jit(solution)/shard_map/all_gather | solution.py:811
  104.6 26.5 %collective-permute-start.17 = (bf16[128,1664]{1,0:T(8,128)(2,1)}, bf16[128,1664]{1,0:T(8,128)(2,1)S(1)}, u32[]{:S(2)}, u32[]{:S(2)}) collective-permute-start(bf16[128,1664]{1,0:T(8,128)(2,1)} %get-tuple-element.217), channel_id=1, source_target_pairs={{0,4},{4,0},{8,12},{12,8},{1,5},{5,1},{9,13},{13,9},{2,6},{6,2},{1... | collective-permute-start | bytes 1277960 | tf_op jit(solution)/shard_map/ppermute | solution.py:549
  105.6 72.3 %collective-permute-start.14 = (bf16[1664,768]{1,0:T(8,128)(2,1)}, bf16[1664,768]{1,0:T(8,128)(2,1)}, u32[]{:S(2)}, u32[]{:S(2)}) collective-permute-start(bf16[1664,768]{1,0:T(8,128)(2,1)} %shard_map.159), channel_id=1, source_target_pairs={{0,16},{16,0},{1,17},{17,1},{2,18},{18,2},{3,19},{19,3},{4,20},{20... | collective-permute-start | bytes 7667720 | tf_op jit(solution)/shard_map/ppermute | solution.py:546
  108.4 24.9 %collective-permute-start.16 = (bf16[128,1664]{1,0:T(8,128)(2,1)}, bf16[128,1664]{1,0:T(8,128)(2,1)S(1)}, u32[]{:S(2)}, u32[]{:S(2)}) collective-permute-start(bf16[128,1664]{1,0:T(8,128)(2,1)} %get-tuple-element.218), channel_id=1, source_target_pairs={{0,8},{8,0},{4,12},{12,4},{1,9},{9,1},{5,13},{13,5},{2,10},{10,2},... | collective-permute-start | bytes 1277960 | tf_op jit(solution)/shard_map/ppermute | solution.py:552
  124.7 26.0 %collective-permute-start.4 = (bf16[64,1664]{1,0:T(8,128)(2,1)S(1)}, bf16[64,1664]{1,0:T(8,128)(2,1)S(1)}, u32[]{:S(2)}, u32[]{:S(2)}) collective-permute-start(bf16[64,1664]{1,0:T(8,128)(2,1)S(1)} %get-tuple-element.67), channel_id=1, source_target_pairs={{0,1},{1,0},{2,3},{3,2},{4,5},{5,4},{6,7},{7,6},{8,9},{9,8},{10,11... | collective-permute-start | bytes 638984 | tf_op jit(solution)/shard_map/ppermute | solution.py:619
  131.1 23.3 %collective-permute-start.5 = (bf16[64,1664]{1,0:T(8,128)(2,1)S(1)}, bf16[64,1664]{1,0:T(8,128)(2,1)S(1)}, u32[]{:S(2)}, u32[]{:S(2)}) collective-permute-start(bf16[64,1664]{1,0:T(8,128)(2,1)S(1)} %get-tuple-element.68), channel_id=1, source_target_pairs={{0,2},{2,0},{1,3},{3,1},{4,6},{6,4},{5,7},{7,5},{8,10},{10,8},{9,1... | collective-permute-start | bytes 638984 | tf_op jit(solution)/shard_map/ppermute | solution.py:619
  133.3 35.6 %collective-permute-start.19 = (bf16[256,1664]{1,0:T(8,128)(2,1)}, bf16[256,1664]{1,0:T(8,128)(2,1)}, u32[]{:S(2)}, u32[]{:S(2)}) collective-permute-start(bf16[256,1664]{1,0:T(8,128)(2,1)} %pad_maximum_fusion.15), channel_id=1, source_target_pairs={{0,8},{8,0},{4,12},{12,4},{1,9},{9,1},{5,13},{13,5},{2,10},{10,2},... | collective-permute-start | bytes 2555912 | tf_op jit(solution)/shard_map/ppermute | solution.py:552
  168.7 198.9 %all-gather.16.cloned.1.call-start = ((), (), s32[]{:S(2)}) async-start(), calls=%async_computation.9 | async-start | bytes 3194880 | tf_op jit(solution)/shard_map/all_gather | solution.py:811
  176.7 31.5 %collective-permute-start.25 = (bf16[224,1664]{1,0:T(8,128)(2,1)S(1)}, bf16[224,1664]{1,0:T(8,128)(2,1)S(1)}, u32[]{:S(2)}, u32[]{:S(2)}) collective-permute-start(bf16[224,1664]{1,0:T(8,128)(2,1)S(1)} %get-tuple-element.206), channel_id=1, source_target_pairs={{0,4},{4,0},{8,12},{12,8},{1,5},{5,1},{9,13},{13,9},{2,6},{6,2},{1... | collective-permute-start | bytes 2236424 | tf_op jit(solution)/shard_map/ppermute | solution.py:549
  177.8 34.3 %collective-permute-start.24 = (bf16[224,1664]{1,0:T(8,128)(2,1)}, bf16[224,1664]{1,0:T(8,128)(2,1)}, u32[]{:S(2)}, u32[]{:S(2)}) collective-permute-start(bf16[224,1664]{1,0:T(8,128)(2,1)} %get-tuple-element.207), channel_id=1, source_target_pairs={{0,8},{8,0},{4,12},{12,4},{1,9},{9,1},{5,13},{13,5},{2,10},{10,2},... | collective-permute-start | bytes 2236424 | tf_op jit(solution)/shard_map/ppermute | solution.py:552
  211.4 32.5 %collective-permute-start.27 = (bf16[448,1664]{1,0:T(8,128)(2,1)}, bf16[448,1664]{1,0:T(8,128)(2,1)}, u32[]{:S(2)}, u32[]{:S(2)}) collective-permute-start(bf16[448,1664]{1,0:T(8,128)(2,1)} %pad_maximum_fusion.13), channel_id=1, source_target_pairs={{0,8},{8,0},{4,12},{12,4},{1,9},{9,1},{5,13},{13,5},{2,10},{10,2},... | collective-permute-start | bytes 4472840 | tf_op jit(solution)/shard_map/ppermute | solution.py:552
  213.6 31.9 %collective-permute-start.26 = (bf16[448,1664]{1,0:T(8,128)(2,1)S(1)}, bf16[448,1664]{1,0:T(8,128)(2,1)S(1)}, u32[]{:S(2)}, u32[]{:S(2)}) collective-permute-start(bf16[448,1664]{1,0:T(8,128)(2,1)S(1)} %pad_maximum_fusion.12), channel_id=1, source_target_pairs={{0,4},{4,0},{8,12},{12,8},{1,5},{5,1},{9,13},{13,9},{2,6},{6,2},{1... | collective-permute-start | bytes 4472840 | tf_op jit(solution)/shard_map/ppermute | solution.py:549
  278.8 37.8 %collective-permute-start.34 = (bf16[1664,1664]{1,0:T(8,128)(2,1)}, bf16[1664,1664]{1,0:T(8,128)(2,1)}, u32[]{:S(2)}, u32[]{:S(2)}) collective-permute-start(bf16[1664,1664]{1,0:T(8,128)(2,1)} %shard_map.173), channel_id=1, source_target_pairs={{0,16},{16,0},{1,17},{17,1},{2,18},{18,2},{3,19},{19,3},{4,20},{20... | collective-permute-start | bytes 16613384 | tf_op jit(solution)/shard_map/ppermute | solution.py:546
  296.5 175.5 %all-gather.20.cloned.1.call-start = ((), (), s32[]{:S(2)}) async-start(), calls=%async_computation.11 | async-start | bytes 6922240 | tf_op jit(solution)/shard_map/all_gather | solution.py:811
  367.3 166.6 %all-gather.18.cloned.1.call-start = ((), (), s32[]{:S(2)}) async-start(), calls=%async_computation.10 | async-start | bytes 4259840 | tf_op jit(solution)/shard_map/all_gather | solution.py:701
  472.0 64.3 %collective-permute-start.47 = (bf16[1664,1664]{1,0:T(8,128)(2,1)}, bf16[1664,1664]{1,0:T(8,128)(2,1)}, u32[]{:S(2)}, u32[]{:S(2)}) collective-permute-start(bf16[1664,1664]{1,0:T(8,128)(2,1)} %shard_map.182), channel_id=1, source_target_pairs={{0,16},{16,0},{1,17},{17,1},{2,18},{18,2},{3,19},{19,3},{4,20},{20... | collective-permute-start | bytes 16613384 | tf_op jit(solution)/shard_map/ppermute | solution.py:546
  474.7 195.3 %reduce-scatter.11.cloned.1.call-start = ((), (), s32[]{:S(2)}) async-start(), calls=%async_computation.16 | async-start | bytes 4259840 | tf_op jit(solution)/shard_map/reduce_scatter | solution.py:708
  490.4 31.4 %collective-permute-start.51 = (bf16[256,1664]{1,0:T(8,128)(2,1)}, bf16[256,1664]{1,0:T(8,128)(2,1)}, u32[]{:S(2)}, u32[]{:S(2)}) collective-permute-start(bf16[256,1664]{1,0:T(8,128)(2,1)} %pad_maximum_fusion.21), channel_id=1, source_target_pairs={{0,8},{8,0},{4,12},{12,4},{1,9},{9,1},{5,13},{13,5},{2,10},{10,2},... | collective-permute-start | bytes 2555912 | tf_op jit(solution)/shard_map/ppermute | solution.py:552
  492.5 29.3 %collective-permute-start.50 = (bf16[256,1664]{1,0:T(8,128)(2,1)}, bf16[256,1664]{1,0:T(8,128)(2,1)}, u32[]{:S(2)}, u32[]{:S(2)}) collective-permute-start(bf16[256,1664]{1,0:T(8,128)(2,1)} %pad_maximum_fusion.20), channel_id=1, source_target_pairs={{0,4},{4,0},{8,12},{12,8},{1,5},{5,1},{9,13},{13,9},{2,6},{6,2},{1... | collective-permute-start | bytes 2555912 | tf_op jit(solution)/shard_map/ppermute | solution.py:549
  571.4 62.4 %collective-permute-start.71 = (bf16[1664,1664]{1,0:T(8,128)(2,1)}, bf16[1664,1664]{1,0:T(8,128)(2,1)}, u32[]{:S(2)}, u32[]{:S(2)}) collective-permute-start(bf16[1664,1664]{1,0:T(8,128)(2,1)} %convolution_convert_fusion.1), channel_id=1, source_target_pairs={{0,16},{16,0},{1,17},{17,1},{2,18},{18,2},{3,19},{19,3},{4,20},{20... | collective-permute-start | bytes 16613384 | tf_op jit(solution)/shard_map/ppermute | solution.py:546
  588.5 171.6 %reduce-scatter.7.cloned.1.call-start = ((), (), s32[]{:S(2)}) async-start(), calls=%async_computation.12 | async-start | bytes 6922240 | tf_op jit(solution)/shard_map/reduce_scatter | solution.py:1074
  599.9 31.9 %collective-permute-start.52 = (bf16[256,1664]{1,0:T(8,128)(2,1)S(1)}, bf16[256,1664]{1,0:T(8,128)(2,1)S(1)}, u32[]{:S(2)}, u32[]{:S(2)}) collective-permute-start(bf16[256,1664]{1,0:T(8,128)(2,1)S(1)} %get-tuple-element.193), channel_id=1, source_target_pairs={{0,4},{4,0},{8,12},{12,8},{1,5},{5,1},{9,13},{13,9},{2,6},{6,2},{1... | collective-permute-start | bytes 2555912 | tf_op jit(solution)/shard_map/ppermute | solution.py:549
  600.3 46.7 %collective-permute-start.54 = (bf16[256,1664]{1,0:T(8,128)(2,1)}, bf16[256,1664]{1,0:T(8,128)(2,1)}, u32[]{:S(2)}, u32[]{:S(2)}) collective-permute-start(bf16[256,1664]{1,0:T(8,128)(2,1)} %get-tuple-element.194), channel_id=1, source_target_pairs={{0,8},{8,0},{4,12},{12,4},{1,9},{9,1},{5,13},{13,5},{2,10},{10,2},... | collective-permute-start | bytes 2555912 | tf_op jit(solution)/shard_map/ppermute | solution.py:552
  646.6 261.9 %all-gather.22.cloned.1.call-start = ((), (), s32[]{:S(2)}) async-start(), calls=%async_computation.13 | async-start | bytes 6922240 | tf_op jit(solution)/shard_map/all_gather | solution.py:1164
  760.1 178.8 %reduce-scatter.9.cloned.1.call-start = ((), (), s32[]{:S(2)}) async-start(), calls=%async_computation.14 | async-start | bytes 3194880 | tf_op jit(solution)/shard_map/reduce_scatter | solution.py:1074
  767.5 36.7 %collective-permute-start.66 = (bf16[256,1664]{1,0:T(8,128)(2,1)S(1)}, bf16[256,1664]{1,0:T(8,128)(2,1)S(1)}, u32[]{:S(2)}, u32[]{:S(2)}) collective-permute-start(bf16[256,1664]{1,0:T(8,128)(2,1)S(1)} %pad_maximum_fusion.23), channel_id=1, source_target_pairs={{0,8},{8,0},{4,12},{12,4},{1,9},{9,1},{5,13},{13,5},{2,10},{10,2},... | collective-permute-start | bytes 2555912 | tf_op jit(solution)/shard_map/ppermute | solution.py:552
  771.1 33.1 %collective-permute-start.65 = (bf16[256,1664]{1,0:T(8,128)(2,1)S(1)}, bf16[256,1664]{1,0:T(8,128)(2,1)S(1)}, u32[]{:S(2)}, u32[]{:S(2)}) collective-permute-start(bf16[256,1664]{1,0:T(8,128)(2,1)S(1)} %pad_maximum_fusion.22), channel_id=1, source_target_pairs={{0,4},{4,0},{8,12},{12,8},{1,5},{5,1},{9,13},{13,9},{2,6},{6,2},{1... | collective-permute-start | bytes 2555912 | tf_op jit(solution)/shard_map/ppermute | solution.py:549
  778.1 55.2 %collective-permute-start.83 = (bf16[1664,768]{1,0:T(8,128)(2,1)}, bf16[1664,768]{1,0:T(8,128)(2,1)}, u32[]{:S(2)}, u32[]{:S(2)}) collective-permute-start(bf16[1664,768]{1,0:T(8,128)(2,1)} %convolution_convert_fusion.11), channel_id=1, source_target_pairs={{0,16},{16,0},{1,17},{17,1},{2,18},{18,2},{3,19},{19,3},{4,20},{20... | collective-permute-start | bytes 7667720 | tf_op jit(solution)/shard_map/ppermute | solution.py:546
  839.5 175.6 %reduce-scatter.17.cloned.1.call-start = ((), (), s32[]{:S(2)}) async-start(), calls=%async_computation.19 | async-start | bytes 6922240 | tf_op jit(solution)/shard_map/reduce_scatter | solution.py:1074
  855.9 281.3 %all-gather.24.cloned.1.call-start = ((), (), s32[]{:S(2)}) async-start(), calls=%async_computation.15 | async-start | bytes 3194880 | tf_op jit(solution)/shard_map/all_gather | solution.py:1166
  928.4 36.6 %collective-permute-start.74 = (bf16[448,1792]{1,0:T(8,128)(2,1)}, bf16[448,1792]{1,0:T(8,128)(2,1)}, u32[]{:S(2)}, u32[]{:S(2)}) collective-permute-start(bf16[448,1792]{1,0:T(8,128)(2,1)} %get-tuple-element.173), channel_id=1, source_target_pairs={{0,4},{4,0},{8,12},{12,8},{1,5},{5,1},{9,13},{13,9},{2,6},{6,2},{1... | collective-permute-start | bytes 4816904 | tf_op jit(solution)/shard_map/ppermute | solution.py:549
  929.8 36.3 %collective-permute-start.75 = (bf16[448,1792]{1,0:T(8,128)(2,1)}, bf16[448,1792]{1,0:T(8,128)(2,1)}, u32[]{:S(2)}, u32[]{:S(2)}) collective-permute-start(bf16[448,1792]{1,0:T(8,128)(2,1)} %get-tuple-element.172), channel_id=1, source_target_pairs={{0,8},{8,0},{4,12},{12,4},{1,9},{9,1},{5,13},{13,5},{2,10},{10,2},... | collective-permute-start | bytes 4816904 | tf_op jit(solution)/shard_map/ppermute | solution.py:552
  936.3 33.6 %collective-permute-start.76 = (bf16[448,256]{1,0:T(8,128)(2,1)S(1)}, bf16[448,256]{1,0:T(8,128)(2,1)S(1)}, u32[]{:S(2)}, u32[]{:S(2)}) collective-permute-start(bf16[448,256]{1,0:T(8,128)(2,1)S(1)} %get-tuple-element.99), channel_id=1, source_target_pairs={{0,4},{4,0},{8,12},{12,8},{1,5},{5,1},{9,13},{13,9},{2,6},{6,2},{1... | collective-permute-start | bytes 688136 | tf_op jit(solution)/shard_map/ppermute | solution.py:549
  936.5 34.5 %collective-permute-start.77 = (bf16[448,256]{1,0:T(8,128)(2,1)S(1)}, bf16[448,256]{1,0:T(8,128)(2,1)S(1)}, u32[]{:S(2)}, u32[]{:S(2)}) collective-permute-start(bf16[448,256]{1,0:T(8,128)(2,1)S(1)} %get-tuple-element.100), channel_id=1, source_target_pairs={{0,8},{8,0},{4,12},{12,4},{1,9},{9,1},{5,13},{13,5},{2,10},{10,2},... | collective-permute-start | bytes 688136 | tf_op jit(solution)/shard_map/ppermute | solution.py:552
  936.8 39.2 %collective-permute-start.78 = (bf16[448,256]{1,0:T(8,128)(2,1)S(1)}, bf16[448,256]{1,0:T(8,128)(2,1)S(1)}, u32[]{:S(2)}, u32[]{:S(2)}) collective-permute-start(bf16[448,256]{1,0:T(8,128)(2,1)S(1)} %get-tuple-element.101), channel_id=1, source_target_pairs={{0,12},{12,0},{4,8},{8,4},{1,13},{13,1},{5,9},{9,5},{2,14},{14,2},... | collective-permute-start | bytes 688136 | tf_op jit(solution)/shard_map/ppermute | solution.py:555
  939.0 225.0 %all-gather.26.cloned.1.call-start = ((), (), s32[]{:S(2)}) async-start(), calls=%async_computation.20 | async-start | bytes 6922240 | tf_op jit(solution)/shard_map/all_gather | solution.py:1196
  1015.1 260.8 %reduce-scatter.15.cloned.1.call-start = ((), (), s32[]{:S(2)}) async-start(), calls=%async_computation.18 | async-start | bytes 2007040 | tf_op jit(solution)/shard_map/reduce_scatter | solution.py:1074
  1017.1 32.9 %collective-permute-start.97 = (bf16[224,1792]{1,0:T(8,128)(2,1)S(1)}, bf16[224,1792]{1,0:T(8,128)(2,1)S(1)}, u32[]{:S(2)}, u32[]{:S(2)}) collective-permute-start(bf16[224,1792]{1,0:T(8,128)(2,1)S(1)} %add_convert_fusion.16), channel_id=1, source_target_pairs={{0,8},{8,0},{4,12},{12,4},{1,9},{9,1},{5,13},{13,5},{2,10},{10,2},... | collective-permute-start | bytes 2408456 | tf_op jit(solution)/shard_map/ppermute | solution.py:552
  1051.9 26.6 %collective-permute-start.98 = (bf16[224,1792]{1,0:T(8,128)(2,1)S(1)}, bf16[224,1792]{1,0:T(8,128)(2,1)S(1)}, u32[]{:S(2)}, u32[]{:S(2)}) collective-permute-start(bf16[224,1792]{1,0:T(8,128)(2,1)S(1)} %get-tuple-element.171), channel_id=1, source_target_pairs={{0,4},{4,0},{8,12},{12,8},{1,5},{5,1},{9,13},{13,9},{2,6},{6,2},{1... | collective-permute-start | bytes 2408456 | tf_op jit(solution)/shard_map/ppermute | solution.py:549
  1081.6 194.7 %reduce-scatter.13.cloned.1.call-start = ((), (), s32[]{:S(2)}) async-start(), calls=%async_computation.17 | async-start | bytes 3194880 | tf_op jit(solution)/shard_map/reduce_scatter | solution.py:1074
  1093.6 37.9 %collective-permute-start.79 = (bf16[256,1664]{1,0:T(8,128)(2,1)S(1)}, bf16[256,1664]{1,0:T(8,128)(2,1)S(1)}, u32[]{:S(2)}, u32[]{:S(2)}) collective-permute-start(bf16[256,1664]{1,0:T(8,128)(2,1)S(1)} %get-tuple-element.184), channel_id=1, source_target_pairs={{0,4},{4,0},{8,12},{12,8},{1,5},{5,1},{9,13},{13,9},{2,6},{6,2},{1... | collective-permute-start | bytes 2555912 | tf_op jit(solution)/shard_map/ppermute | solution.py:549
  1099.3 42.3 %collective-permute-start.81 = (bf16[256,1664]{1,0:T(8,128)(2,1)}, bf16[256,1664]{1,0:T(8,128)(2,1)S(1)}, u32[]{:S(2)}, u32[]{:S(2)}) collective-permute-start(bf16[256,1664]{1,0:T(8,128)(2,1)} %get-tuple-element.185), channel_id=1, source_target_pairs={{0,8},{8,0},{4,12},{12,4},{1,9},{9,1},{5,13},{13,5},{2,10},{10,2},... | collective-permute-start | bytes 2555912 | tf_op jit(solution)/shard_map/ppermute | solution.py:552
  1138.0 232.8 %collective-permute-start.105 = (bf16[1664,1664]{1,0:T(8,128)(2,1)}, bf16[1664,1664]{1,0:T(8,128)(2,1)}, u32[]{:S(2)}, u32[]{:S(2)}) collective-permute-start(bf16[1664,1664]{1,0:T(8,128)(2,1)} %all-gather.22.cloned.1.call-done.refs_1_), channel_id=1, source_target_pairs={{0,16},{1,17},{2,18},{3,19},{4,20},{5,21},{6,22},{7,23},{8,24},{9,... | collective-permute-start | bytes 16613384 | tf_op jit(solution)/shard_map/ppermute | solution.py:546
  1164.0 223.9 %collective-permute-start.106 = (bf16[1664,1664]{1,0:T(8,128)(2,1)}, bf16[1664,1664]{1,0:T(8,128)(2,1)}, u32[]{:S(2)}, u32[]{:S(2)}) collective-permute-start(bf16[1664,1664]{1,0:T(8,128)(2,1)} %all-gather.26.cloned.1.call-done.refs_0_), channel_id=1, source_target_pairs={{16,0},{17,1},{18,2},{19,3},{20,4},{21,5},{22,6},{23,7},{24,8},{25... | collective-permute-start | bytes 16613384 | tf_op jit(solution)/shard_map/ppermute | solution.py:546
  1172.0 29.3 %collective-permute-start.84 = (bf16[64,3328]{1,0:T(8,128)(2,1)S(1)}, bf16[64,3328]{1,0:T(8,128)(2,1)S(1)}, u32[]{:S(2)}, u32[]{:S(2)}) collective-permute-start(bf16[64,3328]{1,0:T(8,128)(2,1)S(1)} %get-tuple-element.103), channel_id=1, source_target_pairs={{0,1},{1,0},{2,3},{3,2},{4,5},{5,4},{6,7},{7,6},{8,9},{9,8},{10,11... | collective-permute-start | bytes 1277960 | tf_op jit(solution)/shard_map/ppermute | solution.py:619
  1172.1 30.4 %collective-permute-start.85 = (bf16[64,3328]{1,0:T(8,128)(2,1)S(1)}, bf16[64,3328]{1,0:T(8,128)(2,1)S(1)}, u32[]{:S(2)}, u32[]{:S(2)}) collective-permute-start(bf16[64,3328]{1,0:T(8,128)(2,1)S(1)} %get-tuple-element.104), channel_id=1, source_target_pairs={{0,2},{2,0},{1,3},{3,1},{4,6},{6,4},{5,7},{7,5},{8,10},{10,8},{9,1... | collective-permute-start | bytes 1277960 | tf_op jit(solution)/shard_map/ppermute | solution.py:619
  1172.4 41.4 %collective-permute-start.86 = (bf16[64,3328]{1,0:T(8,128)(2,1)S(1)}, bf16[64,3328]{1,0:T(8,128)(2,1)S(1)}, u32[]{:S(2)}, u32[]{:S(2)}) collective-permute-start(bf16[64,3328]{1,0:T(8,128)(2,1)S(1)} %get-tuple-element.105), channel_id=1, source_target_pairs={{0,3},{3,0},{1,2},{2,1},{4,7},{7,4},{5,6},{6,5},{8,11},{11,8},{9,1... | collective-permute-start | bytes 1277960 | tf_op jit(solution)/shard_map/ppermute | solution.py:619
  1214.0 61.9 %collective-permute-start.87 = (bf16[64,3328]{1,0:T(8,128)(2,1)S(1)}, bf16[64,3328]{1,0:T(8,128)(2,1)S(1)}, u32[]{:S(2)}, u32[]{:S(2)}) collective-permute-start(bf16[64,3328]{1,0:T(8,128)(2,1)S(1)} %get-tuple-element.107), channel_id=1, source_target_pairs={{0,4},{4,0},{8,12},{12,8},{1,5},{5,1},{9,13},{13,9},{2,6},{6,2},{1... | collective-permute-start | bytes 1277960 | tf_op jit(solution)/shard_map/ppermute | solution.py:619
  1216.4 59.8 %collective-permute-start.88 = (bf16[64,3328]{1,0:T(8,128)(2,1)S(1)}, bf16[64,3328]{1,0:T(8,128)(2,1)S(1)}, u32[]{:S(2)}, u32[]{:S(2)}) collective-permute-start(bf16[64,3328]{1,0:T(8,128)(2,1)S(1)} %get-tuple-element.108), channel_id=1, source_target_pairs={{0,8},{8,0},{4,12},{12,4},{1,9},{9,1},{5,13},{13,5},{2,10},{10,2},... | collective-permute-start | bytes 1277960 | tf_op jit(solution)/shard_map/ppermute | solution.py:619
  1227.7 33.1 %collective-permute-start.111 = (f32[150,128]{1,0:T(8,128)S(1)}, f32[150,128]{1,0:T(8,128)S(1)}, u32[]{:S(2)}, u32[]{:S(2)}) collective-permute-start(f32[150,128]{1,0:T(8,128)S(1)} %shard_map.204.refs_0_), channel_id=1, source_target_pairs={{0,1},{1,0},{2,3},{3,2},{4,5},{5,4},{6,7},{7,6},{8,9},{9,8},{10,11... | collective-permute-start | bytes 230408 | tf_op jit(solution)/shard_map/ppermute | solution.py:619
  1285.9 36.6 %collective-permute-start.93 = (bf16[416,768]{1,0:T(8,128)(2,1)}, bf16[416,768]{1,0:T(8,128)(2,1)S(1)}, u32[]{:S(2)}, u32[]{:S(2)}) collective-permute-start(bf16[416,768]{1,0:T(8,128)(2,1)} %reduce-scatter.13.cloned.1.call-done.refs_0_), channel_id=1, source_target_pairs={{0,8},{8,0},{4,12},{12,4},{1,9},{9,1},{5,13},{13,5},{2,10},{10,2},... | collective-permute-start | bytes 1916936 | tf_op jit(solution)/shard_map/ppermute | solution.py:552
  1295.8 27.9 %collective-permute-start.94 = (bf16[416,768]{1,0:T(8,128)(2,1)}, bf16[416,768]{1,0:T(8,128)(2,1)S(1)}, u32[]{:S(2)}, u32[]{:S(2)}) collective-permute-start(bf16[416,768]{1,0:T(8,128)(2,1)} %reduce-scatter.13.cloned.1.call-done.refs_0_), channel_id=1, source_target_pairs={{0,12},{12,0},{4,8},{8,4},{1,13},{13,1},{5,9},{9,5},{2,14},{14,2},... | collective-permute-start | bytes 1916936 | tf_op jit(solution)/shard_map/ppermute | solution.py:555
  1298.3 49.4 %collective-permute-start.90 = (bf16[256,3328]{1,0:T(8,128)(2,1)S(1)}, bf16[256,3328]{1,0:T(8,128)(2,1)S(1)}, u32[]{:S(2)}, u32[]{:S(2)}) collective-permute-start(bf16[256,3328]{1,0:T(8,128)(2,1)S(1)} %shard_map.195.mine_ref), channel_id=1, source_target_pairs={{0,16},{16,0},{1,17},{17,1},{2,18},{18,2},{3,19},{19,3},{4,20},{20... | collective-permute-start | bytes 5111816 | tf_op jit(solution)/shard_map/ppermute | solution.py:546
  1333.7 47.8 %collective-permute-start.95 = (bf16[1664,768]{1,0:T(8,128)(2,1)}, bf16[1664,768]{1,0:T(8,128)(2,1)}, u32[]{:S(2)}, u32[]{:S(2)}) collective-permute-start(bf16[1664,768]{1,0:T(8,128)(2,1)} %all-gather.24.cloned.1.call-done.refs_1_.refs_3_), channel_id=1, source_target_pairs={{0,16},{1,17},{2,18},{3,19},{4,20},{5,21},{6,22},{7,23},{8,24},{9,... | collective-permute-start | bytes 7667720 | tf_op jit(solution)/shard_map/ppermute | solution.py:546
  1342.0 39.6 %collective-permute-start.96 = (bf16[1664,768]{1,0:T(8,128)(2,1)}, bf16[1664,768]{1,0:T(8,128)(2,1)}, u32[]{:S(2)}, u32[]{:S(2)}) collective-permute-start(bf16[1664,768]{1,0:T(8,128)(2,1)} %shard_map.197.refs_0_), channel_id=1, source_target_pairs={{16,0},{17,1},{18,2},{19,3},{20,4},{21,5},{22,6},{23,7},{24,8},{25... | collective-permute-start | bytes 7667720 | tf_op jit(solution)/shard_map/ppermute | solution.py:546
  (234 other events, 2655.3 us)
Sparse Core Ops, SparseCore 0:
  27.8 72.6 all-gather.9
  103.3 47.1 all-gather.11
  168.8 102.7 all-gather.13
  296.6 51.2 all-gather.15
  367.4 104.5 all-gather.19
  474.8 58.9 all-gather.17
  588.6 66.3 reduce-scatter.10
  657.9 98.3 reduce-scatter.6
  760.3 79.0 all-gather.21
  842.1 50.8 reduce-scatter.8
  896.0 98.3 reduce-scatter.16
  996.3 53.5 all-gather.23
  1051.9 87.7 all-gather.25
  1142.6 54.5 reduce-scatter.14
  1200.0 59.0 reduce-scatter.12
